TPU v7x, 128 devices: a whole 4x4x4 slice. The times are simulated.
128 devices in a mesh: dp: 16 (over z, x_lo, core), tensor: 8 (over x_hi, y).
Axes of the slice: x: 4 (x_hi: 2, x_lo: 2; x = x_hi * 2 + x_lo), y: 4, z: 4, core: 2. Of those that a mesh axis runs over, the one named last changes fastest.
Arguments:
- layer_input: bfloat16 [5120, 2048], P('dp'), may hold values from -4.5 to 4.5
- doc_lengths: int32 [4], replicated, may hold values from 1 to 4800, as said below
- expert_ids: int32 [5120, 4], P('dp'), may hold values from 0 to 15, all different within a row; in each aligned block of 320 rows (0 to 319, 320 to 639, ...) at most 110 rows name the same one
- attn_gain: float32 [2048], replicated, may hold values from 0.1 to 1.9
- qkv_weight: bfloat16 [2048, 3, 16, 128], P(None, None, 'tensor'), may hold values from -0.125 to 0.125
- qkv_bias: bfloat16 [3, 16, 128], P(None, 'tensor'), may hold values from -3 to 3
- out_weight: bfloat16 [16, 128, 2048], P('tensor'), may hold values from -0.5 to 0.5
- ffn_gain: float32 [2048], replicated, may hold values from 0.1 to 1.9
- router_weight: bfloat16 [2048, 16], replicated, may hold values from -0.0625 to 0.0625
- shared_gate: bfloat16 [2048], replicated, may hold values from -0.125 to 0.125
- shared_in: bfloat16 [2048, 2, 5632], P(None, None, 'tensor'), may hold values from -0.125 to 0.125
- shared_out: bfloat16 [5632, 2048], P('tensor'), may hold values from -0.3125 to 0.3125
- expert_in: bfloat16 [16, 2048, 2, 1408], P('dp', None, None, 'tensor'), may hold values from -0.125 to 0.125
- expert_out: bfloat16 [16, 1408, 2048], P('dp', 'tensor'), may hold values from -1.25 to 1.25
- cotangent: bfloat16 [5120, 2048], P('dp'), may hold values from -6 to 6
Outputs:
- layer_output: bfloat16 [5120, 2048], P('dp')
- input_grad: float32 [5120, 2048], P('dp')
- qkv_grad: float32 [2048, 3, 16, 128], P('dp', None, 'tensor')
- bias_grad: float32 [3, 16, 128], P(None, 'tensor', 'dp')
- outproj_grad: float32 [16, 128, 2048], P('tensor', None, 'dp')
- attn_gain_grad: float32 [2048], P('dp')
- ffn_gain_grad: float32 [2048], P('dp')
- router_grad: float32 [2048, 16], P('dp')
- shared_gate_grad: float32 [2048], P('dp')
- shared_in_grad: float32 [2048, 2, 5632], P('dp', None, 'tensor')
- shared_out_grad: float32 [5632, 2048], P('tensor', 'dp')
- expert_in_grad: float32 [16, 2048, 2, 1408], P('dp', None, None, 'tensor')
- expert_out_grad: float32 [16, 1408, 2048], P('dp', 'tensor')
- rms_stats: float32 [5], replicated
Inputs may be any that keep to these rules, and one draw needn't show every extreme that they name: `doc_lengths`: positive lengths that add up to 5120; one of the two middle documents has exactly 4800 tokens, beginning within the first 320 tokens and ending within the last 320. `expert_ids`: the tokens of one group name each expert at most 110 times; some group names some expert exactly 110 times.
All inputs are finite; a program needn't handle non-finite values.
Results may differ from a plain program's by a relative error of at most 0.02.
Values may be sent and summed in bfloat16 or wider, within the bound.
A program may use at most 256 MiB of HBM per device.

v0:
```python
import math

import jax
import jax.numpy as jnp
from jax import lax
from jax.sharding import PartitionSpec as P

DBLOCK = 256


EPSILON = 1e-06
THETA = 1000000.0
NEG_FILL = -1e30
PRECISE = lax.Precision.HIGHEST


def doc_layout(lengths, token_index):
    doc_ends = jnp.cumsum(lengths)
    starts = doc_ends - lengths
    seq_ids = jnp.sum((token_index[:, None] >= doc_ends[None, :]).astype(jnp.int32), axis=1)
    member = seq_ids[:, None] == jnp.arange(lengths.shape[0], dtype=jnp.int32)[None, :]
    begins = jnp.sum(jnp.where(member, starts[None, :], 0), axis=1)
    offsets = token_index - begins
    return (seq_ids, offsets, offsets // DBLOCK)


def rope_tables(offsets, head_dim):
    half_dim = head_dim // 2
    frequencies = jnp.exp(
        jnp.arange(half_dim, dtype=jnp.float32) * (-2.0 * math.log(THETA) / head_dim)
    )
    angles = offsets.astype(jnp.float32)[:, None] * frequencies[None, :]
    return (jnp.cos(angles)[:, None, :], jnp.sin(angles)[:, None, :])


def rotate(vectors, cosine, sine_table):
    half_dim = vectors.shape[-1] // 2
    front_half = vectors[..., :half_dim]
    back_half = vectors[..., half_dim:]
    return jnp.concatenate(
        [
            front_half * cosine - back_half * sine_table,
            back_half * cosine + front_half * sine_table,
        ],
        axis=-1,
    )


def rotate_back(gradient, cosine, sine_table):
    half_dim = gradient.shape[-1] // 2
    front_half = gradient[..., :half_dim]
    back_half = gradient[..., half_dim:]
    return jnp.concatenate(
        [
            front_half * cosine + back_half * sine_table,
            back_half * cosine - front_half * sine_table,
        ],
        axis=-1,
    )


def softmax_rows(logits):
    row_peak = jnp.max(logits, axis=-1, keepdims=True)
    exp_terms = jnp.exp(logits - row_peak)
    return exp_terms / jnp.sum(exp_terms, axis=-1, keepdims=True)


def silu_back(gate_up, d_hidden):
    gate_part = gate_up[:, 0]
    up_part = gate_up[:, 1]
    sigmoid_gate = jax.nn.sigmoid(gate_part)
    d_gate = d_hidden * up_part * sigmoid_gate * (1.0 + gate_part * (1.0 - sigmoid_gate))
    d_up = d_hidden * gate_part * sigmoid_gate
    return jnp.stack([d_gate, d_up], axis=1)


def on_device(
    layer_input,
    doc_lengths,
    expert_ids,
    attn_gain,
    qkv_weight,
    qkv_bias,
    out_weight,
    ffn_gain,
    router_weight,
    shared_gate,
    shared_in,
    shared_out,
    expert_in,
    expert_out,
    cotangent,
):
    tok_dev, model_width = layer_input.shape
    data_size = lax.axis_size("dp")
    tensor_size = lax.axis_size("tensor")
    experts = router_weight.shape[1]
    top_k = expert_ids.shape[1]
    capacity = tok_dev * top_k * 11 // (8 * experts)
    head_dim = qkv_weight.shape[3]
    stream = tok_dev * data_size
    score_scale = head_dim ** (-0.5)
    bf16 = jnp.bfloat16
    f32 = jnp.float32
    local_index = lax.axis_index("dp") * tok_dev + jnp.arange(tok_dev, dtype=jnp.int32)
    every_index = jnp.arange(stream, dtype=jnp.int32)
    seq_local, pos_local, blk_local = doc_layout(doc_lengths, local_index)
    seq_all, pos_all, blk_all = doc_layout(doc_lengths, every_index)
    allowed = (seq_local[:, None] == seq_all[None, :]) & (blk_all[None, :] <= blk_local[:, None])
    cosine, sine_table = rope_tables(pos_local, head_dim)
    residual = layer_input.astype(f32)
    inv_first = lax.rsqrt(jnp.mean(residual * residual, axis=1, keepdims=True) + EPSILON)
    normed_one = (residual * inv_first * attn_gain).astype(bf16)
    projected = (
        jnp.einsum("td,dshe->tshe", normed_one, qkv_weight, preferred_element_type=f32)
        + qkv_bias.astype(f32)[None]
    )
    queries = rotate(projected[:, 0], cosine, sine_table).astype(bf16)
    keys_own = rotate(projected[:, 1], cosine, sine_table).astype(bf16)
    values_own = projected[:, 2].astype(bf16)
    keys_all, values_all = (
        lax.all_gather(keys_own, "dp", axis=0, tiled=True),
        lax.all_gather(values_own, "dp", axis=0, tiled=True),
    )
    raw_scores = (
        jnp.einsum("qhe,khe->hqk", queries, keys_all, preferred_element_type=f32) * score_scale
    )
    masked = jnp.where(allowed[None], raw_scores, NEG_FILL)
    row_peak = jnp.max(masked, axis=2, keepdims=True)
    exp_terms = jnp.where(allowed[None], jnp.exp(masked - row_peak), 0.0)
    attn_probs = exp_terms / jnp.sum(exp_terms, axis=2, keepdims=True)
    probs_low = attn_probs.astype(bf16)
    heads_out = jnp.einsum(
        "hqk,khe->qhe", probs_low, values_all, preferred_element_type=f32
    ).astype(bf16)
    attn_part = jnp.einsum("qhe,hed->qd", heads_out, out_weight, preferred_element_type=f32)
    attn_out = lax.psum(attn_part, "tensor")
    middle = residual + attn_out
    inv_second = lax.rsqrt(jnp.mean(middle * middle, axis=1, keepdims=True) + EPSILON)
    normed_two = (middle * inv_second * ffn_gain).astype(bf16)
    router_probs = softmax_rows(jnp.dot(normed_two, router_weight, preferred_element_type=f32))
    route_hot = (
        expert_ids[:, :, None] == jnp.arange(experts, dtype=jnp.int32)[None, None, :]
    ).astype(f32)
    route_gates = jnp.sum(route_hot * router_probs[:, None, :], axis=2)
    gate_value = jax.nn.sigmoid(jnp.dot(normed_two, shared_gate, preferred_element_type=f32))
    shared_gu = jnp.einsum("td,dsf->tsf", normed_two, shared_in, preferred_element_type=f32)
    shared_hidden = (jax.nn.silu(shared_gu[:, 0]) * shared_gu[:, 1]).astype(bf16)
    shared_part = jnp.dot(shared_hidden, shared_out, preferred_element_type=f32)
    flat_ids = expert_ids.reshape(-1)
    onehot = (flat_ids[:, None] == jnp.arange(experts, dtype=jnp.int32)[None, :]).astype(jnp.int32)
    rank_in = jnp.cumsum(onehot, axis=0) - onehot
    slot_in = jnp.sum(rank_in * onehot, axis=1)
    targets = flat_ids * capacity + slot_in
    send_rows = (
        jnp.zeros((experts * capacity, model_width), bf16)
        .at[targets]
        .set(jnp.repeat(normed_two, top_k, axis=0))
    )
    received = lax.all_to_all(
        send_rows.reshape(experts, capacity, model_width),
        "dp",
        split_axis=0,
        concat_axis=0,
        tiled=True,
    )
    exp_rows = received.reshape(-1, model_width)
    expert_gu = jnp.einsum("rd,dsf->rsf", exp_rows, expert_in[0], preferred_element_type=f32)
    expert_hidden = (jax.nn.silu(expert_gu[:, 0]) * expert_gu[:, 1]).astype(bf16)
    expert_part = jnp.dot(expert_hidden, expert_out[0], preferred_element_type=f32)
    expert_send = lax.psum(expert_part, "tensor")
    returned = lax.all_to_all(
        expert_send.reshape(data_size, capacity, model_width),
        "dp",
        split_axis=0,
        concat_axis=0,
        tiled=True,
    )
    route_out = returned.reshape(-1, model_width)[targets].reshape(tok_dev, top_k, model_width)
    routed = jnp.sum(route_gates[:, :, None] * route_out, axis=1)
    mixed_term = gate_value[:, None] * shared_part
    moe_out = lax.psum(mixed_term.astype(jnp.bfloat16), "tensor").astype(jnp.float32)
    moe_out = moe_out + routed
    output = middle + moe_out
    squares = jnp.stack(
        [
            jnp.sum(residual * residual),
            jnp.sum(attn_out * attn_out),
            jnp.sum(middle * middle),
            jnp.sum(moe_out * moe_out),
            jnp.sum(output * output),
        ]
    )
    totals = lax.psum(squares, "dp")
    rms_stats = jnp.sqrt(totals / (stream * model_width))
    upstream = cotangent.astype(f32)
    d_shared = (gate_value[:, None] * upstream).astype(bf16)
    gate_partial = jnp.sum(upstream * shared_part, axis=1) * gate_value * (1.0 - gate_value)
    shared_out_part = jnp.einsum("tf,td->fd", shared_hidden, d_shared, preferred_element_type=f32)
    d_shared_hidden = jnp.einsum("td,fd->tf", d_shared, shared_out, preferred_element_type=f32)
    d_shared_gu = silu_back(shared_gu, d_shared_hidden).astype(bf16)
    shared_in_part = jnp.einsum("td,tsf->dsf", normed_two, d_shared_gu, preferred_element_type=f32)
    d_route = (route_gates[:, :, None] * upstream[:, None, :]).astype(bf16)
    send_grads = (
        jnp.zeros((experts * capacity, model_width), bf16)
        .at[targets]
        .set(d_route.reshape(-1, model_width))
    )
    got_grads = lax.all_to_all(
        send_grads.reshape(experts, capacity, model_width),
        "dp",
        split_axis=0,
        concat_axis=0,
        tiled=True,
    ).reshape(-1, model_width)
    d_expert_hidden = jnp.einsum("rd,fd->rf", got_grads, expert_out[0], preferred_element_type=f32)
    expert_out_grad = jnp.einsum("rf,rd->fd", expert_hidden, got_grads, preferred_element_type=f32)[
        None
    ]
    d_expert_gu = silu_back(expert_gu, d_expert_hidden).astype(bf16)
    expert_in_grad = jnp.einsum("rd,rsf->dsf", exp_rows, d_expert_gu, preferred_element_type=f32)[
        None
    ]
    d_rows = jnp.einsum("rsf,dsf->rd", d_expert_gu, expert_in[0], preferred_element_type=f32)
    d_rows = lax.psum(d_rows, "tensor")
    got_back = lax.all_to_all(
        d_rows.reshape(data_size, capacity, model_width),
        "dp",
        split_axis=0,
        concat_axis=0,
        tiled=True,
    )
    d_routed = jnp.sum(
        got_back.reshape(-1, model_width)[targets].reshape(tok_dev, top_k, model_width), axis=1
    )
    d_gates = jnp.sum(upstream[:, None, :] * route_out, axis=2)
    d_gates = d_gates / tensor_size
    d_rprobs = jnp.sum(route_hot * d_gates[:, :, None], axis=1)
    d_logits = router_probs * (d_rprobs - jnp.sum(router_probs * d_rprobs, axis=1, keepdims=True))
    normed_wide = normed_two.astype(f32)
    router_part = jnp.dot(normed_wide.T, d_logits, precision=PRECISE)
    gate_vec_part = jnp.dot(gate_partial, normed_wide, precision=PRECISE)
    d_normed_two = jnp.einsum("tsf,dsf->td", d_shared_gu, shared_in, preferred_element_type=f32)
    d_normed_two = d_normed_two + jnp.dot(d_logits, router_weight.astype(f32).T, precision=PRECISE)
    d_normed_two = d_normed_two + gate_partial[:, None] * shared_gate.astype(f32)[None, :]
    d_normed_two, router_full, gate_vec_full = lax.psum(
        (d_normed_two, router_part, gate_vec_part), "tensor"
    )
    d_normed_two = d_normed_two + d_routed
    scaled_two = d_normed_two * ffn_gain
    ffn_gain_part = jnp.sum(d_normed_two * middle * inv_second, axis=0)
    cube_two = inv_second * inv_second * inv_second
    d_middle = (
        upstream
        + inv_second * scaled_two
        - middle * cube_two * jnp.mean(scaled_two * middle, axis=1, keepdims=True)
    )
    d_attn = d_middle.astype(bf16)
    outproj_part = jnp.einsum("qhe,qd->hed", heads_out, d_attn, preferred_element_type=f32)
    d_heads = jnp.einsum("qd,hed->qhe", d_attn, out_weight, preferred_element_type=f32).astype(bf16)
    d_values_all = jnp.einsum("hqk,qhe->khe", probs_low, d_heads, preferred_element_type=f32)
    d_probs = jnp.einsum("qhe,khe->hqk", d_heads, values_all, preferred_element_type=f32)
    d_scores = (
        attn_probs * (d_probs - jnp.sum(attn_probs * d_probs, axis=2, keepdims=True))
    ).astype(bf16)
    d_queries = (
        jnp.einsum("hqk,khe->qhe", d_scores, keys_all, preferred_element_type=f32) * score_scale
    )
    d_keys_all = (
        jnp.einsum("hqk,qhe->khe", d_scores, queries, preferred_element_type=f32) * score_scale
    )
    d_keys, d_values = (
        lax.psum_scatter(d_keys_all, "dp", scatter_dimension=0, tiled=True),
        lax.psum_scatter(d_values_all, "dp", scatter_dimension=0, tiled=True),
    )
    d_proj = jnp.stack(
        [
            rotate_back(d_queries, cosine, sine_table),
            rotate_back(d_keys, cosine, sine_table),
            d_values,
        ],
        axis=1,
    ).astype(bf16)
    qkv_part = jnp.einsum("td,tshe->dshe", normed_one, d_proj, preferred_element_type=f32)
    bias_part = jnp.sum(d_proj.astype(f32), axis=0)
    d_normed_one = jnp.einsum("tshe,dshe->td", d_proj, qkv_weight, preferred_element_type=f32)
    d_normed_one = lax.psum(d_normed_one.astype(jnp.bfloat16), "tensor").astype(jnp.float32)
    scaled_one = d_normed_one * attn_gain
    attn_gain_part = jnp.sum(d_normed_one * residual * inv_first, axis=0)
    cube_one = inv_first * inv_first * inv_first
    input_grad = (
        d_middle
        + inv_first * scaled_one
        - residual * cube_one * jnp.mean(scaled_one * residual, axis=1, keepdims=True)
    )
    (
        qkv_grad,
        bias_grad,
        outproj_grad,
        attn_gain_grad,
        ffn_gain_grad,
        router_grad,
        shared_gate_grad,
        shared_in_grad,
        shared_out_grad,
    ) = (
        lax.psum_scatter(qkv_part, "dp", scatter_dimension=0, tiled=True),
        lax.psum_scatter(bias_part, "dp", scatter_dimension=2, tiled=True),
        lax.psum_scatter(outproj_part, "dp", scatter_dimension=2, tiled=True),
        lax.psum_scatter(attn_gain_part, "dp", scatter_dimension=0, tiled=True),
        lax.psum_scatter(ffn_gain_part, "dp", scatter_dimension=0, tiled=True),
        lax.psum_scatter(router_full, "dp", scatter_dimension=0, tiled=True),
        lax.psum_scatter(gate_vec_full, "dp", scatter_dimension=0, tiled=True),
        lax.psum_scatter(shared_in_part, "dp", scatter_dimension=0, tiled=True),
        lax.psum_scatter(shared_out_part, "dp", scatter_dimension=1, tiled=True),
    )
    return (
        output.astype(bf16),
        input_grad,
        qkv_grad,
        bias_grad,
        outproj_grad,
        attn_gain_grad,
        ffn_gain_grad,
        router_grad,
        shared_gate_grad,
        shared_in_grad,
        shared_out_grad,
        expert_in_grad,
        expert_out_grad,
        rms_stats,
    )


def solution(mesh):
    in_specs = (
        P("dp", None),
        P(),
        P("dp", None),
        P(),
        P(None, None, "tensor", None),
        P(None, "tensor", None),
        P("tensor", None, None),
        P(),
        P(),
        P(),
        P(None, None, "tensor"),
        P("tensor", None),
        P("dp", None, None, "tensor"),
        P("dp", "tensor", None),
        P("dp", None),
    )
    out_specs = (
        P("dp", None),
        P("dp", None),
        P("dp", None, "tensor", None),
        P(None, "tensor", "dp"),
        P("tensor", None, "dp"),
        P("dp"),
        P("dp"),
        P("dp", None),
        P("dp"),
        P("dp", None, "tensor"),
        P("tensor", "dp"),
        P("dp", None, None, "tensor"),
        P("dp", "tensor", None),
        P(),
    )
    return jax.shard_map(
        on_device, mesh=mesh, in_specs=in_specs, out_specs=out_specs, check_vma=False
    )
```

profile of v0, /device:TPU:1, one launch (start us, length us, event | category | flops | bytes accessed | tf_op | source)
XLA Modules:
  0.0 2253.4 jit_solution(15173759019745294520)
XLA Ops:
  21.6 34.2 %all-gather.4.cloned.1.call-done = bf16[5120,2,128]{2,0,1:T(8,128)(2,1)} async-done(((bf16[320,2,128]{2,0,1:T(8,128)(2,1)}), bf16[5120,2,128]{2,0,1:T(8,128)(2,1)}) %all-gather.4.cloned.1.call-update) | async-done | bytes 2621456 | tf_op jit(solution)/shard_map/all_gather | solution.py:122
  55.8 8.3 fusion.99
  64.1 26.1 %fusion.114 = (f32[2,320]{1,0:T(2,128)S(1)}, f32[2,320,5120]{2,1,0:T(8,128)}) fusion(f32[2,320,5120]{2,1,0:T(8,128)} %fusion.99, pred[320,5120]{1,0:T(8,128)(4,1)} %compare_and_fusion), kind=kOutput, calls=%fused_computation.218 | output fusion | flops 16389119 | bytes 27855360 | tf_op jit(solution)/shard_map/sub | solution.py:130
  93.1 7.5 fusion.71
  104.2 4.5 reduce-window.19
  109.9 85.2 %all-reduce.13.cloned.1.call-done = f32[320,2048]{1,0:T(8,128)} async-done(((f32[320,2048]{1,0:T(8,128)}), f32[320,2048]{1,0:T(8,128)}) %all-reduce.13.cloned.1.call-update) | async-done | bytes 2621456 | tf_op jit(solution)/shard_map/psum | solution.py:137
  195.1 3.7 multiply_reduce_fusion.10
  201.6 6.3 broadcast_in_dim.55
  208.0 8.3 reshape.397
  216.3 15.1 scatter_custom_fusion
  231.4 7.1 reshape.367
  238.5 93.0 %all_to_all.20 = bf16[16,110,2048]{2,1,0:T(8,128)(2,1)} all-to-all(bf16[16,110,2048]{2,1,0:T(8,128)(2,1)} %reshape.367), channel_id=1, replica_groups=mesh['dp'=16,'tensor'=8] {'dp'}, dimensions={0} | all-to-all | bytes 14417920 | tf_op jit(solution)/shard_map/all_to_all | solution.py:160
  331.5 7.1 reshape.368
  338.6 6.2 fusion.118
  347.4 7.2 fusion.78
  354.6 10.5 reshape.369
  365.2 6.6 mul.540
  371.8 12.7 mul.554
  387.2 21.0 scatter_custom_fusion.1
  408.2 7.2 reshape.372
  415.3 168.2 %all_to_all.21 = bf16[16,110,2048]{2,1,0:T(8,128)(2,1)} all-to-all(bf16[16,110,2048]{2,1,0:T(8,128)(2,1)} %reshape.372), channel_id=1, replica_groups=mesh['dp'=16,'tensor'=8] {'dp'}, dimensions={0} | all-to-all | bytes 14417920 | tf_op jit(solution)/shard_map/all_to_all | solution.py:209
  583.5 161.5 %all-reduce.17.cloned.1.call-done = f32[16,110,2048]{2,1,0:T(8,128)} async-done(((f32[16,110,2048]{2,1,0:T(8,128)}), f32[16,110,2048]{2,1,0:T(8,128)}) %all-reduce.17.cloned.1.call-update) | async-done | bytes 14417936 | tf_op jit(solution)/shard_map/psum | solution.py:171
  745.0 5.5 all-to-all-start.1
  755.2 5.0 fusion.48
  764.8 3.8 convolution_bitcast_fusion.2
  768.6 7.5 reshape.373
  776.2 6.7 fusion.88
  784.0 7.1 convolution_bitcast_fusion
  791.0 10.6 reshape.374
  801.6 111.0 %all-to-all-done.1 = f32[16,110,2048]{2,1,0:T(8,128)} async-done(((f32[16,110,2048]{2,1,0:T(8,128)}), f32[16,110,2048]{2,1,0:T(8,128)}, u32[]{:S(2)}, u32[]{:S(2)}) %all-to-all-start.1) | async-done | bytes 14417952 | tf_op jit(solution)/shard_map/all_to_all | solution.py:172
  912.6 10.6 reshape.370
  923.2 15.9 gather_fusion
  939.1 12.1 reshape.371
  951.2 13.5 multiply_reduce_fusion.1
  965.5 4.6 fusion.24
  970.2 350.1 %all-reduce.21.cloned.1.call-done = (f32[320,2048]{1,0:T(8,128)}, f32[16,110,2048]{2,1,0:T(8,128)}) async-done(((f32[320,2048]{1,0:T(8,128)}, f32[16,110,2048]{2,1,0:T(8,128)}), (f32[320,2048]{1,0:T(8,128)}, f32[16,110,2048]{2,1,0:T(8,128)})) %all-reduce.21.cloned.1.call-update) | async-done | bytes 17039376 | tf_op jit(solution)/shard_map/psum | solution.py:246
  1320.3 5.4 all-to-all-start.3
  1326.4 186.8 %all-to-all-done.3 = f32[16,110,2048]{2,1,0:T(8,128)} async-done(((f32[16,110,2048]{2,1,0:T(8,128)}), f32[16,110,2048]{2,1,0:T(8,128)}, u32[]{:S(2)}, u32[]{:S(2)}) %all-to-all-start.3) | async-done | bytes 14417952 | tf_op jit(solution)/shard_map/all_to_all | solution.py:226
  1513.2 10.8 reshape.375
  1524.0 15.8 gather_fusion.1
  1539.8 12.1 reshape.376
  1551.9 12.3 reduce_sum.261
  1564.3 7.2 multiply_reduce_fusion.3
  1574.8 11.3 multiply_reduce_fusion
  1586.4 6.6 multiply_convert_fusion
  1595.8 5.0 fusion.2
  1600.8 10.1 convolution_bitcast_fusion.1
  1611.1 6.4 fusion.62
  1617.4 50.4 %reduce-scatter.9.cloned.1.call-done = f32[320,2,128]{2,0,1:T(8,128)} async-done(((f32[5120,2,128]{2,0,1:T(8,128)}), f32[320,2,128]{2,0,1:T(8,128)}) %reduce-scatter.9.cloned.1.call-update) | async-done | bytes 327696 | tf_op jit(solution)/shard_map/reduce_scatter | solution.py:273
  1669.7 72.2 %reduce-scatter.11.cloned.1.call-done = f32[320,2,128]{2,0,1:T(8,128)} async-done(((f32[5120,2,128]{2,0,1:T(8,128)}), f32[320,2,128]{2,0,1:T(8,128)}) %reduce-scatter.11.cloned.1.call-update) | async-done | bytes 327696 | tf_op jit(solution)/shard_map/reduce_scatter | solution.py:274
  1749.3 6.0 fusion.80
  1756.0 5.7 fusion.89
  1761.8 9.1 fusion.46
  1771.9 3.9 fusion.42
  1781.1 5.8 convolution_bitcast_fusion.4
  1786.9 7.5 fusion.120
  1794.4 36.7 %all-reduce.19.cloned.1.call-done = bf16[320,2048]{1,0:T(8,128)(2,1)} async-done(((bf16[320,2048]{1,0:T(8,128)(2,1)}), bf16[320,2048]{1,0:T(8,128)(2,1)}) %all-reduce.19.cloned.1.call-update) | async-done | bytes 1310736 | tf_op jit(solution)/shard_map/psum | solution.py:287
  1838.1 54.2 %all-reduce.4 = (f32[3,2,128]{2,1,0:T(2,128)S(1)}, f32[2048]{0:T(1024)S(1)}, f32[2048]{0:T(1024)S(1)}, f32[2048]{0:T(1024)S(1)}, f32[5]{0:T(128)S(1)}) all-reduce(f32[3,2,128]{2,1,0:T(2,128)S(1)} %get-tuple-element.119, f32[2048]{0:T(1024)S(1)} %get-tuple-element.107, ...), channel_id=6, replica_groups=mesh['dp'=16,'tensor'=8] {'dp'}, use_global_device_ids=true, to_apply=%region_36.37.clone | all-reduce | flops 6917 | bytes 55336
  1893.6 21.0 all-reduce.5
  1915.7 4.8 fusion.29
  1920.5 53.0 %reduce-scatter.13.cloned.1.call-done = f32[128,3,2,128]{3,0,2,1:T(8,128)} async-done(((f32[2048,3,2,128]{3,0,2,1:T(8,128)}), f32[128,3,2,128]{3,0,2,1:T(8,128)}) %reduce-scatter.13.cloned.1.call-update) | async-done | bytes 393232 | tf_op jit(solution)/shard_map/reduce_scatter | solution.py:307
  1975.5 74.8 %reduce-scatter.19.cloned.1.call-done = f32[704,128]{1,0:T(8,128)} async-done(((f32[704,2048]{1,0:T(8,128)}), f32[704,128]{1,0:T(8,128)}) %reduce-scatter.19.cloned.1.call-update) | async-done | bytes 360464 | tf_op jit(solution)/shard_map/reduce_scatter | solution.py:315
  2050.3 131.7 %reduce-scatter.17.cloned.1.call-done = f32[128,2,704]{0,2,1:T(8,128)} async-done(((f32[2048,2,704]{0,2,1:T(8,128)}), f32[128,2,704]{0,2,1:T(8,128)}) %reduce-scatter.17.cloned.1.call-update) | async-done | bytes 720912 | tf_op jit(solution)/shard_map/reduce_scatter | solution.py:314
  2182.0 64.7 %reduce-scatter.15.cloned.1.call-done = f32[2,128,128]{2,1,0:T(8,128)} async-done(((f32[2,128,2048]{2,1,0:T(8,128)}), f32[2,128,128]{2,1,0:T(8,128)}) %reduce-scatter.15.cloned.1.call-update) | async-done | bytes 131088 | tf_op jit(solution)/shard_map/reduce_scatter | solution.py:309
  (238 shorter events, 74.4 us)
Async XLA Ops:
  7.2 4.9 copy-start
  7.2 48.6 %all-gather.4.cloned.1.call-start = ((), (), s32[]{:S(2)}) async-start(), calls=%async_computation.11 | async-start | bytes 2785280 | tf_op jit(solution)/shard_map/all_gather | solution.py:122
  11.4 3.3 copy-start.45
  16.1 48.0 %copy-start.15 = (bf16[320,2,64]{2,0,1:T(8,128)(2,1)}, bf16[320,2,64]{2,0,1:T(8,128)(2,1)S(1)}, u32[]{:S(2)}) copy-start(bf16[320,2,64]{2,0,1:T(8,128)(2,1)S(1)} %get-tuple-element.138) | copy-start | bytes 245764
  16.1 48.0 %copy-start.17 = (bf16[320,2,64]{2,0,1:T(8,128)(2,1)}, bf16[320,2,64]{2,0,1:T(8,128)(2,1)S(1)}, u32[]{:S(2)}) copy-start(bf16[320,2,64]{2,0,1:T(8,128)(2,1)S(1)} %get-tuple-element.139) | copy-start | bytes 245764
  17.0 76.1 %all-gather.6.cloned.1.call-start = ((), (), s32[]{:S(2)}) async-start(), calls=%async_computation.22 | async-start | bytes 2785280 | tf_op jit(solution)/shard_map/all_gather | solution.py:123
  18.7 176.4 %all-reduce.13.cloned.1.call-start = ((), (), s32[]{:S(2)}) async-start(), calls=%async_computation.12 | async-start | bytes 5242880 | tf_op jit(solution)/shard_map/psum | solution.py:137
  90.2 10.3 copy-start.52
  93.1 8.1 copy-start.12
  101.2 2.5 copy-start.34
  103.3 641.7 %all-reduce.17.cloned.1.call-start = ((), (), s32[]{:S(2)}) async-start(), calls=%async_computation.14 | async-start | bytes 29360128 | tf_op jit(solution)/shard_map/psum | solution.py:171
  109.9 90.4 %copy-start.37 = (f32[2048]{0:T(1024)S(1)}, f32[2048]{0:T(1024)}, u32[]{:S(2)}) copy-start(f32[2048]{0:T(1024)} %param.22) | copy-start | bytes 24580
  199.4 8.5 copy-start.41
  344.8 2.6 copy-start.25
  371.8 12.7 copy-start.33
  745.0 167.6 %all-to-all-start.1 = ((f32[16,110,2048]{2,1,0:T(8,128)}), f32[16,110,2048]{2,1,0:T(8,128)}, u32[]{:S(2)}, u32[]{:S(2)}) async-start(f32[16,110,2048]{2,1,0:T(8,128)} %all-reduce.17.cloned.1.call-done), calls=%async_computation.1 | async-start | bytes 29360128 | tf_op jit(solution)/shard_map/all_to_all | solution.py:172
  750.5 3.5 copy-start.47
  750.5 569.9 %all-reduce.21.cloned.1.call-start = ((), (), s32[]{:S(2)}) async-start(), calls=%async_computation.24 | async-start | bytes 34603008 | tf_op jit(solution)/shard_map/psum | solution.py:246
  750.8 3.9 copy-start.1
  754.6 168.6 %copy-start.35 = (s32[2048]{0:T(1024)}, s32[2048]{0:T(1024)S(1)}, u32[]{:S(2)}) copy-start(s32[2048]{0:T(1024)S(1)} %pad_clamp_fusion) | copy-start | bytes 24580
  755.1 6.7 copy-start.49
  755.1 5.1 copy-start.7
  755.1 5.1 copy-start.54
  755.2 9.7 slice-start.4
  760.2 4.6 slice-start.5
  761.8 2.5 copy-start.32
  761.8 3.1 copy-start.30
  761.8 3.0 copy-start.31
  776.2 7.8 copy-start.56
  1320.3 192.9 %all-to-all-start.3 = ((f32[16,110,2048]{2,1,0:T(8,128)}), f32[16,110,2048]{2,1,0:T(8,128)}, u32[]{:S(2)}, u32[]{:S(2)}) async-start(f32[16,110,2048]{2,1,0:T(8,128)} %get-tuple-element.118), calls=%async_computation.3 | async-start | bytes 29360128 | tf_op jit(solution)/shard_map/all_to_all | solution.py:226
  1325.8 238.4 %all-reduce.15.cloned.1.call-start = ((), (), s32[]{:S(2)}) async-start(), calls=%async_computation.13 | async-start | bytes 2621440 | tf_op jit(solution)/shard_map/psum | solution.py:182
  1326.3 197.6 %copy-start.36 = (s32[2048]{0:T(1024)S(1)}, s32[2048]{0:T(1024)}, u32[]{:S(2)}) copy-start(s32[2048]{0:T(1024)} %copy-done.35) | copy-start | bytes 24580
  1326.4 341.5 %reduce-scatter.9.cloned.1.call-start = ((), (), s32[]{:S(2)}) async-start(), calls=%async_computation.15 | async-start | bytes 5570560 | tf_op jit(solution)/shard_map/reduce_scatter | solution.py:273
  1551.9 12.3 copy-start.38
  1551.9 12.3 copy-start.42
  1564.2 7.3 copy-start.4
  1564.2 7.3 copy-start.6
  1564.2 7.3 copy-start.8
  1564.2 7.6 copy-start.9
  1564.2 7.6 copy-start.51
  1571.8 2.9 copy-start.53
  1571.8 2.9 copy-start.55
  1574.2 12.0 slice-start
  1574.7 11.4 slice-start.1
  1574.7 11.4 slice-start.2
  1574.7 11.7 slice-start.3
  1586.4 9.4 copy-start.16
  1586.4 9.4 copy-start.18
  1593.1 2.7 copy-start.5
  1600.8 141.1 %reduce-scatter.11.cloned.1.call-start = ((), (), s32[]{:S(2)}) async-start(), calls=%async_computation.16 | async-start | bytes 5570560 | tf_op jit(solution)/shard_map/reduce_scatter | solution.py:274
  1611.0 56.9 %copy-start.20 = (f32[320,64]{1,0:T(8,128)S(1)}, f32[320,64]{1,0:T(8,128)}, u32[]{:S(2)}) copy-start(f32[320,64]{1,0:T(8,128)} %copy-done.19) | copy-start | bytes 245764
  1611.0 56.9 %copy-start.22 = (f32[320,64]{1,0:T(8,128)S(1)}, f32[320,64]{1,0:T(8,128)}, u32[]{:S(2)}) copy-start(f32[320,64]{1,0:T(8,128)} %copy-done.21) | copy-start | bytes 245764
  1611.0 220.1 %all-reduce.19.cloned.1.call-start = ((), (), s32[]{:S(2)}) async-start(), calls=%async_computation.17 | async-start | bytes 2621440 | tf_op jit(solution)/shard_map/psum | solution.py:287
  1746.1 3.2 copy-start.39
  1746.1 3.2 copy-start.46
  1746.1 147.4 %reduce-scatter.21.cloned.1.call-start = ((), (), s32[]{:S(2)}) async-start(), calls=%async_computation.23 | async-start | bytes 139264 | tf_op jit(solution)/shard_map/reduce_scatter | solution.py:312
  1748.8 224.7 %reduce-scatter.13.cloned.1.call-start = ((), (), s32[]{:S(2)}) async-start(), calls=%async_computation.18 | async-start | bytes 6684672 | tf_op jit(solution)/shard_map/reduce_scatter | solution.py:307
  1755.4 295.0 %reduce-scatter.19.cloned.1.call-start = ((), (), s32[]{:S(2)}) async-start(), calls=%async_computation.21 | async-start | bytes 6127616 | tf_op jit(solution)/shard_map/reduce_scatter | solution.py:315
  1761.7 420.3 %reduce-scatter.17.cloned.1.call-start = ((), (), s32[]{:S(2)}) async-start(), calls=%async_computation.20 | async-start | bytes 12255232 | tf_op jit(solution)/shard_map/reduce_scatter | solution.py:314
  1771.0 4.8 copy-start.57
  1771.0 6.7 copy-start.43
  1771.0 475.7 %reduce-scatter.15.cloned.1.call-start = ((), (), s32[]{:S(2)}) async-start(), calls=%async_computation.19 | async-start | bytes 2228224 | tf_op jit(solution)/shard_map/reduce_scatter | solution.py:309
  1777.7 3.4 copy-start.11
  1794.4 121.3 %copy-start.48 = (f32[320]{0:T(512)S(1)}, f32[320]{0:T(512)}, u32[]{:S(2)}) copy-start(f32[320]{0:T(512)} %get-tuple-element.148) | copy-start | bytes 3844
  (16 other events, 16.6 us)
Sparse Core Ops, SparseCore 0:
  17.1 38.6 all-gather.3
  58.0 35.0 all-gather.5
  103.4 91.6 all-reduce.12
  365.3 379.6 all-reduce.16
  970.3 349.9 all-reduce.20
  1329.4 93.0 all-reduce.14
  1600.9 66.8 reduce-scatter.8
  1670.3 71.5 reduce-scatter.10
  1746.2 84.8 all-reduce.18
  1833.3 59.4 reduce-scatter.20
  1895.3 78.1 reduce-scatter.12
  1976.5 73.7 reduce-scatter.18
  2053.5 128.5 reduce-scatter.16
  2184.9 61.7 reduce-scatter.14
where the time goes:
time: 2270 us; the launch traced here: 2250 us
  waiting for transfers between devices  1420 us (63%)
  blocking collectives  336 us (15%)
  local copies, waits for them, and re-layouts  200 us (9%)
  matrix products  146 us (6%)
  other arithmetic  127 us (6%)
    psum x1, waiting for transfers between devices, on_device(): lax.psum((d_normed_two, router_part, gate_vec_part), 'tensor')  350 us
    all_to_all x1, waiting for transfers between devices, on_device(): lax.all_to_all(d_rows.reshape(data_size, capacity, model_width), 'dp', sp...  187 us
    all_to_all x1, blocking collectives, on_device(): lax.all_to_all(send_grads.reshape(experts, capacity, model_width), 'dp',...  168 us
    psum x1, waiting for transfers between devices, on_device(): expert_send = lax.psum(expert_part, 'tensor')  161 us
    reduce_scatter x1, waiting for transfers between devices, on_device(): lax.psum_scatter(shared_in_part, 'dp', scatter_dimension=0, tiled=True)  132 us
    all_to_all x1, waiting for transfers between devices, on_device(): lax.all_to_all(expert_send.reshape(data_size, capacity, model_width), 'dp...  111 us
    all_to_all x1, blocking collectives, on_device(): lax.all_to_all(send_rows.reshape(experts, capacity, model_width), 'dp', s...  93 us
    psum x1, waiting for transfers between devices, on_device(): attn_out = lax.psum(attn_part, 'tensor')  85.2 us
  transfers between devices with their start and end apart: 16, of which 14 were waited for; matrix products, arithmetic and copies ran while one was open for 12% of the time, Pallas kernels for 0%

commit v1 on v0

v1 whole, which is shorter than its diff:
```python
import math

import jax
import jax.numpy as jnp
from jax import lax
from jax.experimental import pallas as pl
from jax.experimental.pallas import tpu as pltpu
from jax.sharding import PartitionSpec as P

DBLOCK = 256
EPSILON = 1e-06
THETA = 1000000.0
NEG_FILL = -1e30
MESH = pl.DeviceIdType.MESH
f32 = jnp.float32
bf16 = jnp.bfloat16
N_DP = 16
N_T = 8
SLOTS = 112

HBM = pl.BlockSpec(memory_space=pl.ANY)
VMEM = pl.BlockSpec(memory_space=pltpu.VMEM)


def greet(peers):
    barrier = pltpu.get_barrier_semaphore()
    for peer in peers:
        pl.semaphore_signal(barrier, inc=1, device_id=peer, device_id_type=MESH)
    pl.semaphore_wait(barrier, len(peers))


def remote(src, dst, send, recv, device):
    return pltpu.make_async_remote_copy(
        src_ref=src,
        dst_ref=dst,
        send_sem=send,
        recv_sem=recv,
        device_id=device,
        device_id_type=MESH,
    )


def dma(*shape):
    return pltpu.SemaphoreType.DMA(shape)


def comm_params(number, limit=None):
    return pltpu.CompilerParams(
        collective_id=number, has_side_effects=True, vmem_limit_bytes=limit
    )


def gather_keys(kv, q):
    def kernel(kv_ref, q_ref, all_ref, pair_ref, send, recv, qsend, qrecv, local):
        me = lax.axis_index("dp")
        core = lax.rem(me, 2)
        greet([{"dp": me ^ k} for k in range(1, N_DP)])
        swap = remote(
            q_ref.at[1 - core], pair_ref.at[core], qsend, qrecv, {"dp": me ^ 1}
        )
        swap.start()
        copies = []
        for k in (2, 4, 12, 6, 14, 8, 10, 3, 5, 13, 7, 15, 9, 11, 1):
            peer = me ^ k
            head = core if k % 2 == 0 else 1 - core
            copies.append(
                remote(kv_ref.at[head], all_ref.at[me], send.at[k], recv.at[k], {"dp": peer})
            )
            copies[-1].start()
        own = pltpu.make_async_copy(kv_ref.at[core], all_ref.at[me], local.at[0])
        own.start()
        own_q = pltpu.make_async_copy(q_ref.at[core], pair_ref.at[core], local.at[1])
        own_q.start()
        swap.wait()
        for copy in copies:
            copy.wait()
        own.wait()
        own_q.wait()

    return pl.pallas_call(
        kernel,
        out_shape=(
            jax.ShapeDtypeStruct((N_DP,) + kv.shape[1:], kv.dtype),
            jax.ShapeDtypeStruct(q.shape, q.dtype),
        ),
        in_specs=[HBM, HBM],
        out_specs=(HBM, HBM),
        scratch_shapes=[dma(N_DP), dma(N_DP), pltpu.SemaphoreType.DMA, pltpu.SemaphoreType.DMA, dma(2)],
        compiler_params=comm_params(1),
        name="gather_keys",
    )(kv, q)


def swap_cores(x, number):
    def kernel(x_ref, out_ref, send, recv, local):
        me = lax.axis_index("dp")
        core = lax.rem(me, 2)
        greet([{"dp": me ^ 1}])
        swap = remote(x_ref.at[1 - core], out_ref.at[core], send, recv, {"dp": me ^ 1})
        swap.start()
        own = pltpu.make_async_copy(x_ref.at[core], out_ref.at[core], local)
        own.start()
        swap.wait()
        own.wait()

    return pl.pallas_call(
        kernel,
        out_shape=jax.ShapeDtypeStruct(x.shape, x.dtype),
        in_specs=[HBM],
        out_specs=HBM,
        scratch_shapes=[pltpu.SemaphoreType.DMA, pltpu.SemaphoreType.DMA, pltpu.SemaphoreType.DMA],
        compiler_params=comm_params(number),
        name="swap_cores",
    )(x)


ORDER = (2, 4, 12, 6, 14, 8, 10, 3, 5, 13, 7, 15, 9, 11, 1)


def rows_out(x, number):
    def kernel(x_ref, out_ref, send, recv, local):
        me = lax.axis_index("dp")
        parity = lax.rem(lax.axis_index("tensor"), 2)
        core = lax.rem(me, 2)
        greet([{"dp": me ^ k} for k in range(1, N_DP)])

        def copy(k):
            return remote(
                x_ref.at[me ^ k], out_ref.at[me // 2], send.at[k], recv.at[k], {"dp": me ^ k}
            )

        @pl.when(core == parity)
        def _():
            for k in ORDER:
                copy(k).start()
            own = pltpu.make_async_copy(x_ref.at[me], out_ref.at[me // 2], local)
            own.start()
            own.wait()
            for k in ORDER:
                copy(k).wait_send()
                if k % 2 == 0:
                    copy(k).wait_recv()

        @pl.when(core != parity)
        def _():
            for k in ORDER:
                if k % 2 == 1:
                    copy(k).wait_recv()

    return pl.pallas_call(
        kernel,
        out_shape=jax.ShapeDtypeStruct((8,) + x.shape[1:], x.dtype),
        in_specs=[HBM],
        out_specs=HBM,
        scratch_shapes=[dma(N_DP), dma(N_DP), pltpu.SemaphoreType.DMA],
        compiler_params=comm_params(number),
        name="rows_out",
    )(x)


def rows_back(xs, number):
    count = len(xs)

    def kernel(*refs):
        x_refs, out_refs = refs[:count], refs[count : 2 * count]
        send, recv, local = refs[2 * count :]
        me = lax.axis_index("dp")
        parity = lax.rem(lax.axis_index("tensor"), 2)
        core = lax.rem(me, 2)
        greet([{"dp": me ^ k} for k in range(1, N_DP)])

        def copy(i, k):
            peer = me ^ k
            return remote(
                x_refs[i].at[peer // 2],
                out_refs[i].at[me],
                send.at[i, k],
                recv.at[i, k],
                {"dp": peer},
            )

        def own(i):
            return pltpu.make_async_copy(x_refs[i].at[me // 2], out_refs[i].at[me], local.at[i])

        @pl.when(core == parity)
        def _():
            for i in range(count):
                for k in ORDER:
                    if k % 2 == 0:
                        copy(i, k).start()
                own(i).start()
            for i in range(count):
                own(i).wait()
                for k in ORDER:
                    if k % 2 == 0:
                        copy(i, k).wait_send()
                    copy(i, k).wait_recv()

        @pl.when(core != parity)
        def _():
            for i in range(count):
                for k in ORDER:
                    if k % 2 == 1:
                        copy(i, k).start()
            for i in range(count):
                for k in ORDER:
                    if k % 2 == 1:
                        copy(i, k).wait_send()

    return pl.pallas_call(
        kernel,
        out_shape=tuple(jax.ShapeDtypeStruct((N_DP,) + x.shape[1:], x.dtype) for x in xs),
        in_specs=[HBM] * count,
        out_specs=(HBM,) * count,
        scratch_shapes=[dma(count, N_DP), dma(count, N_DP), dma(count)],
        compiler_params=comm_params(number),
        name="rows_back",
    )(*xs)


def scatter_keys(dkv, dq, number):
    def kernel(x_ref, q_ref, out_ref, pair_ref, send, recv, qsend, qrecv, local):
        me = lax.axis_index("dp")
        core = lax.rem(me, 2)
        greet([{"dp": me ^ k} for k in range(1, N_DP)])
        copies = []
        for k in ORDER:
            peer = me ^ k
            copies.append(
                remote(x_ref.at[peer], out_ref.at[me], send.at[k], recv.at[k], {"dp": peer})
            )
            copies[-1].start()
        swap = remote(
            q_ref.at[1 - core], pair_ref.at[core], qsend, qrecv, {"dp": me ^ 1}
        )
        swap.start()
        own = pltpu.make_async_copy(x_ref.at[me], out_ref.at[me], local.at[0])
        own.start()
        own_q = pltpu.make_async_copy(q_ref.at[core], pair_ref.at[core], local.at[1])
        own_q.start()
        swap.wait()
        for copy in copies:
            copy.wait()
        own.wait()
        own_q.wait()

    return pl.pallas_call(
        kernel,
        out_shape=(
            jax.ShapeDtypeStruct(dkv.shape, dkv.dtype),
            jax.ShapeDtypeStruct(dq.shape, dq.dtype),
        ),
        in_specs=[HBM, HBM],
        out_specs=(HBM, HBM),
        scratch_shapes=[dma(N_DP), dma(N_DP), pltpu.SemaphoreType.DMA, pltpu.SemaphoreType.DMA, dma(2)],
        compiler_params=comm_params(number),
        name="scatter_keys",
    )(dkv, dq)


def join(finish, partials, slices, gains, n_gather, plain_shapes, number, name):
    n_part, n_slice, n_gain = len(partials), len(slices), len(gains)
    rows, width = partials[0].shape[1:]
    n_in = n_part + n_slice + n_gain
    n_plain = len(plain_shapes)

    def kernel(*refs):
        part_refs = refs[:n_part]
        slice_refs = refs[n_part : n_part + n_slice]
        gain_refs = refs[n_part + n_slice : n_in]
        full_refs = refs[n_in : n_in + n_gather]
        plain_refs = refs[n_in + n_gather : n_in + n_gather + n_plain]
        got, mine, send, recv, asend, arecv, local = refs[n_in + n_gather + n_plain :]
        me = lax.axis_index("tensor")
        greet([{"tensor": me ^ k} for k in range(1, N_T)])
        steps = (1, 3, 2, 4, 5, 7, 6)
        arriving = []
        for i in range(n_part):
            arriving.append([])
            for k in steps:
                copy = remote(
                    part_refs[i].at[me ^ k],
                    got.at[i, k],
                    send.at[i, k],
                    recv.at[i, k],
                    {"tensor": me ^ k},
                )
                copy.start()
                arriving[i].append(copy)
        leaving = []

        def total(i):
            value = part_refs[i][me].astype(f32)
            for k, copy in zip(steps, arriving[i]):
                copy.wait_recv()
                value = value + got[i, k].astype(f32)
            return value

        def gather(i, value):
            mine[i] = value.astype(bf16)
            for k in steps:
                copy = remote(
                    mine.at[i],
                    full_refs[i].at[me],
                    asend.at[i, k],
                    arecv.at[i, k],
                    {"tensor": me ^ k},
                )
                copy.start()
                leaving.append(copy)
            own = pltpu.make_async_copy(mine.at[i], full_refs[i].at[me], local.at[i])
            own.start()
            leaving.append(own)

        own_slices = [ref[me] if ref.ndim == 3 else ref[...] for ref in slice_refs]
        finish(total, gather, own_slices, [ref[...] for ref in gain_refs], plain_refs)
        for copies in arriving:
            for copy in copies:
                copy.wait_send()
        for copy in leaving:
            copy.wait()

    return pl.pallas_call(
        kernel,
        out_shape=tuple(jax.ShapeDtypeStruct((N_T, rows, width), bf16) for _ in range(n_gather))
        + tuple(jax.ShapeDtypeStruct(s, f32) for s in plain_shapes),
        in_specs=[VMEM] * n_in,
        out_specs=(HBM,) * n_gather + (VMEM,) * n_plain,
        scratch_shapes=[
            pltpu.VMEM((n_part, N_T, rows, width), bf16),
            pltpu.VMEM((n_gather, rows, width), bf16),
            dma(n_part, N_T),
            dma(n_part, N_T),
            dma(n_gather, N_T),
            dma(n_gather, N_T),
            dma(n_gather),
        ],
        compiler_params=comm_params(number, 48 * 1024 * 1024),
        name=name,
    )(*partials, *slices, *gains)


def sum_small(pack, number):
    rows = pack.shape[1]

    def kernel(x_ref, one_ref, both_ref, got, mine, more, send, recv, tsend, trecv):
        me = lax.axis_index("dp")
        t = lax.axis_index("tensor")
        greet([{"dp": me ^ k} for k in range(1, N_DP)] + [{"tensor": t ^ k} for k in range(1, N_T)])
        copies = []
        for k in range(1, N_DP):
            copies.append(
                remote(x_ref.at[me ^ k], got.at[k], send.at[k], recv.at[k], {"dp": me ^ k})
            )
            copies[-1].start()
        value = x_ref[me]
        for k in range(1, N_DP):
            copies[k - 1].wait_recv()
            value = value + got[k]
        one_ref[...] = value
        mine[...] = value
        others = []
        for k in range(1, N_T):
            others.append(remote(mine, more.at[k], tsend.at[k], trecv.at[k], {"tensor": t ^ k}))
            others[-1].start()
        for k in range(1, N_T):
            others[k - 1].wait_recv()
            value = value + more[k]
        both_ref[...] = value
        for copy in copies + others:
            copy.wait_send()

    return pl.pallas_call(
        kernel,
        out_shape=(jax.ShapeDtypeStruct((rows, 128), f32),) * 2,
        in_specs=[VMEM],
        out_specs=(VMEM, VMEM),
        scratch_shapes=[
            pltpu.VMEM((N_DP, rows, 128), f32),
            pltpu.VMEM((rows, 128), f32),
            pltpu.VMEM((N_T, rows, 128), f32),
            dma(N_DP),
            dma(N_DP),
            dma(N_T),
            dma(N_T),
        ],
        compiler_params=comm_params(number),
        name="sum_small",
    )(pack)


def doc_layout(lengths, token_index):
    doc_ends = jnp.cumsum(lengths)
    starts = doc_ends - lengths
    seq_ids = jnp.sum((token_index[:, None] >= doc_ends[None, :]).astype(jnp.int32), axis=1)
    member = seq_ids[:, None] == jnp.arange(lengths.shape[0], dtype=jnp.int32)[None, :]
    begins = jnp.sum(jnp.where(member, starts[None, :], 0), axis=1)
    offsets = token_index - begins
    return (seq_ids, offsets, offsets // DBLOCK)


def rope_tables(offsets, head_dim):
    half_dim = head_dim // 2
    frequencies = jnp.exp(
        jnp.arange(half_dim, dtype=f32) * (-2.0 * math.log(THETA) / head_dim)
    )
    angles = offsets.astype(f32)[:, None] * frequencies[None, :]
    return (jnp.cos(angles)[:, None, :], jnp.sin(angles)[:, None, :])


def rotate(vectors, cosine, sine):
    half_dim = vectors.shape[-1] // 2
    front, back = vectors[..., :half_dim], vectors[..., half_dim:]
    return jnp.concatenate([front * cosine - back * sine, back * cosine + front * sine], axis=-1)


def silu_back(gate_part, up_part, d_hidden):
    sigmoid_gate = jax.nn.sigmoid(gate_part)
    d_gate = d_hidden * up_part * sigmoid_gate * (1.0 + gate_part * (1.0 - sigmoid_gate))
    d_up = d_hidden * gate_part * sigmoid_gate
    return d_gate, d_up


def dot(pattern, a, b):
    return jnp.einsum(pattern, a, b, preferred_element_type=f32)


def attn_finish(total, gather, slices, gains, plain):
    resid = slices[0].astype(f32)
    attn_out = total(0)
    middle = resid + attn_out
    inv = lax.rsqrt(jnp.mean(middle * middle, axis=1, keepdims=True) + EPSILON)
    gather(0, middle * inv * gains[0])
    plain[0][...] = middle
    plain[1][0:1] = jnp.sum(resid * resid, axis=0, keepdims=True)
    plain[1][1:2] = jnp.sum(attn_out * attn_out, axis=0, keepdims=True)
    plain[1][2:3] = jnp.sum(middle * middle, axis=0, keepdims=True)


def ffn_finish(total, gather, slices, gains, plain):
    upstream, middle = slices[0].astype(f32), slices[1]
    inv = lax.rsqrt(jnp.mean(middle * middle, axis=1, keepdims=True) + EPSILON)
    d_normed = total(0)
    scaled = d_normed * gains[0]
    d_middle = (
        upstream
        + inv * scaled
        - middle * (inv * inv * inv) * jnp.mean(scaled * middle, axis=1, keepdims=True)
    )
    gather(0, d_middle)
    plain[0][...] = d_middle
    plain[1][0:1] = jnp.sum(d_normed * middle * inv, axis=0, keepdims=True)
    moe_out = total(1)
    output = middle + moe_out
    gather(1, output)
    plain[1][1:2] = jnp.sum(moe_out * moe_out, axis=0, keepdims=True)
    plain[1][2:3] = jnp.sum(output * output, axis=0, keepdims=True)


def input_finish(total, gather, slices, gains, plain):
    resid, d_middle = slices[0].astype(f32), slices[1]
    inv = lax.rsqrt(jnp.mean(resid * resid, axis=1, keepdims=True) + EPSILON)
    d_normed = total(0)
    scaled = d_normed * gains[0]
    gather(
        0,
        d_middle
        + inv * scaled
        - resid * (inv * inv * inv) * jnp.mean(scaled * resid, axis=1, keepdims=True),
    )
    plain[0][0:1] = jnp.sum(d_normed * resid * inv, axis=0, keepdims=True)


def on_device(
    layer_input,
    doc_lengths,
    expert_ids,
    attn_gain,
    qkv_weight,
    qkv_bias,
    out_weight,
    ffn_gain,
    router_weight,
    shared_gate,
    shared_in,
    shared_out,
    expert_in,
    expert_out,
    cotangent,
):
    tok, width = layer_input.shape
    dp, tn = lax.axis_index("dp"), lax.axis_index("tensor")
    core = lax.rem(dp, 2)
    parity = lax.rem(tn, 2)
    experts = router_weight.shape[1]
    head_dim = qkv_weight.shape[3]
    stream = tok * N_DP
    part_rows = tok // N_T
    score_scale = head_dim ** (-0.5)
    eff = expert_out.shape[1]

    pairs = [(i, i ^ 1) for i in range(N_T)]
    other_in = lax.ppermute(expert_in[0], "tensor", pairs)
    other_out = lax.ppermute(expert_out[0], "tensor", pairs)

    hot = jnp.sum(
        (expert_ids[:, :, None] == jnp.arange(experts, dtype=jnp.int32)[None, None, :]).astype(f32),
        axis=1,
    )
    before = (jnp.arange(tok)[:, None] > jnp.arange(tok)[None, :]).astype(bf16)
    rank = dot("ts,se->te", before, hot.astype(bf16))
    place = jnp.where(hot > 0, rank, -1.0).astype(jnp.int32).T
    places = (
        place[:, None, :] == jnp.arange(SLOTS, dtype=jnp.int32)[None, :, None]
    ).astype(bf16)
    places_flat = places.reshape(experts * SLOTS, tok)

    up_send = dot("rt,td->rd", places_flat, cotangent).astype(bf16)
    up_rows = rows_out(up_send.reshape(experts, SLOTS, width), 2).reshape(-1, width)

    local_index = dp * tok + jnp.arange(tok, dtype=jnp.int32)
    pair_index = (dp // 2) * (2 * tok) + jnp.arange(2 * tok, dtype=jnp.int32)
    every_index = jnp.arange(stream, dtype=jnp.int32)
    _, pos_local, _ = doc_layout(doc_lengths, local_index)
    seq_pair, _, blk_pair = doc_layout(doc_lengths, pair_index)
    seq_all, _, blk_all = doc_layout(doc_lengths, every_index)
    allowed = (seq_pair[:, None] == seq_all[None, :]) & (blk_all[None, :] <= blk_pair[:, None])
    cosine, sine = rope_tables(pos_local, head_dim)
    residual = layer_input.astype(f32)
    inv_first = lax.rsqrt(jnp.mean(residual * residual, axis=1, keepdims=True) + EPSILON)
    normed_one = (residual * inv_first * attn_gain).astype(bf16)
    projected = dot("td,dshe->tshe", normed_one, qkv_weight) + qkv_bias.astype(f32)[None]
    q_own = rotate(projected[:, 0], cosine, sine).astype(bf16).transpose(1, 0, 2)
    k_own = rotate(projected[:, 1], cosine, sine).astype(bf16).transpose(1, 0, 2)
    v_own = projected[:, 2].astype(bf16).transpose(1, 0, 2)
    kv_own = jnp.concatenate([k_own, v_own], axis=1)
    kv_all, queries = gather_keys(kv_own, q_own)
    queries = queries.reshape(2 * tok, head_dim)
    keys = kv_all[:, :tok].reshape(stream, head_dim)
    values = kv_all[:, tok:].reshape(stream, head_dim)

    raw_scores = dot("qe,ke->qk", queries, keys) * score_scale
    masked = jnp.where(allowed, raw_scores, NEG_FILL)
    row_peak = jnp.max(masked, axis=1, keepdims=True)
    exp_terms = jnp.where(allowed, jnp.exp(masked - row_peak), 0.0)
    attn_probs = exp_terms / jnp.sum(exp_terms, axis=1, keepdims=True)
    probs_low = attn_probs.astype(bf16)
    pair_out = dot("qk,ke->qe", probs_low, values).astype(bf16)
    heads_out = swap_cores(pair_out.reshape(2, tok, head_dim), 3)
    attn_part = dot("hqe,hed->qd", heads_out, out_weight).astype(bf16)
    normed_two, middle, stats_one = join(
        attn_finish,
        [attn_part.reshape(N_T, part_rows, width)],
        [layer_input.reshape(N_T, part_rows, width)],
        [ffn_gain.reshape(1, width)],
        1,
        [(part_rows, width), (8, width)],
        4,
        "join_attn",
    )
    normed_two = normed_two.reshape(tok, width)

    row_send = dot("rt,td->rd", places_flat, normed_two).astype(bf16)
    exp_rows = rows_out(row_send.reshape(experts, SLOTS, width), 5).reshape(-1, width)

    gate_value = jax.nn.sigmoid(dot("td,d->t", normed_two, shared_gate))
    shared_gu = dot("td,dsf->tsf", normed_two, shared_in)
    shared_hidden = (jax.nn.silu(shared_gu[:, 0]) * shared_gu[:, 1]).astype(bf16)
    shared_part = dot("tf,fd->td", shared_hidden, shared_out)
    upstream = cotangent.astype(f32)
    d_shared = (gate_value[:, None] * upstream).astype(bf16)
    gate_partial = jnp.sum(upstream * shared_part, axis=1) * gate_value * (1.0 - gate_value)
    d_shared_hidden = dot("td,fd->tf", d_shared, shared_out)
    d_gate, d_up = silu_back(shared_gu[:, 0], shared_gu[:, 1], d_shared_hidden)
    d_shared_gu = jnp.stack([d_gate, d_up], axis=1).astype(bf16)
    shared_out_part = dot("tf,td->fd", shared_hidden, d_shared).astype(bf16)
    shared_in_part = dot("td,tsf->dsf", normed_two, d_shared_gu).astype(bf16)
    shared_d_normed = (
        dot("tsf,dsf->td", d_shared_gu, shared_in)
        + gate_partial[:, None] * shared_gate.astype(f32)[None, :]
    )
    gate_vec_part = dot("t,td->d", gate_partial, normed_two.astype(f32))

    w_in = jnp.concatenate([expert_in[0], other_in], axis=2)
    w_out = jnp.concatenate([expert_out[0], other_out], axis=0)
    row_logits = dot("rd,de->re", exp_rows, router_weight)
    row_probs = jax.nn.softmax(row_logits, axis=1)
    own_expert = (jnp.arange(experts, dtype=jnp.int32) == dp).astype(f32)[None, :]
    row_gate = jnp.sum(row_probs * own_expert, axis=1, keepdims=True)
    expert_gu = dot("rd,dsf->rsf", exp_rows, w_in)
    expert_hidden = (jax.nn.silu(expert_gu[:, 0]) * expert_gu[:, 1]).astype(bf16)
    expert_part = (row_gate * dot("rf,fd->rd", expert_hidden, w_out)).astype(bf16)
    raw_hidden = dot("rd,fd->rf", up_rows, w_out)
    d_gate_row = jnp.sum(expert_hidden.astype(f32) * raw_hidden, axis=1, keepdims=True)
    d_row_logits = (d_gate_row * row_gate * (own_expert - row_probs)).astype(bf16)
    d_gate, d_up = silu_back(expert_gu[:, 0], expert_gu[:, 1], row_gate * raw_hidden)
    d_expert_gu = jnp.stack([d_gate, d_up], axis=1).astype(bf16)
    d_rows = (
        dot("rsf,dsf->rd", d_expert_gu, w_in) + dot("re,de->rd", d_row_logits, router_weight)
    ).astype(bf16)
    router_part = dot("re,rd->ed", d_row_logits, exp_rows)
    gated_hidden = (expert_hidden.astype(f32) * row_gate).astype(bf16)
    send_in = dot("rd,rsf->dsf", exp_rows, d_expert_gu[:, :, eff:]).astype(bf16)
    send_out = dot("rf,rd->fd", gated_hidden[:, eff:], up_rows).astype(bf16)
    got_in = lax.ppermute(send_in, "tensor", pairs)
    got_out = lax.ppermute(send_out, "tensor", pairs)
    expert_in_grad = (
        dot("rd,rsf->dsf", exp_rows, d_expert_gu[:, :, :eff]) + got_in.astype(f32)
    )[None]
    expert_out_grad = (
        dot("rf,rd->fd", gated_hidden[:, :eff], up_rows) + got_out.astype(f32)
    )[None]

    back_grads, back_out = rows_back(
        [d_rows.reshape(8, SLOTS, width), expert_part.reshape(8, SLOTS, width)], 6
    )

    def combine(operands):
        flat, one, two = operands
        return (
            dot("rt,rd->td", flat, one.reshape(-1, width)),
            dot("rt,rd->td", flat, two.reshape(-1, width)),
        )

    d_routed, routed = lax.cond(
        core == parity,
        combine,
        lambda operands: (jnp.zeros((tok, width), f32),) * 2,
        (places_flat, back_grads, back_out),
    )
    d_normed_part = (shared_d_normed + d_routed).astype(bf16)
    moe_part = (gate_value[:, None] * shared_part + routed).astype(bf16)
    d_attn, output, d_middle, stats_two = join(
        ffn_finish,
        [d_normed_part.reshape(N_T, part_rows, width), moe_part.reshape(N_T, part_rows, width)],
        [cotangent.reshape(N_T, part_rows, width), middle],
        [ffn_gain.reshape(1, width)],
        2,
        [(part_rows, width), (8, width)],
        7,
        "join_ffn",
    )
    d_attn = d_attn.reshape(tok, width)

    outproj_part = dot("hqe,qd->hed", heads_out, d_attn).astype(bf16)
    d_heads = dot("qd,hed->hqe", d_attn, out_weight).astype(bf16)
    d_heads = swap_cores(d_heads, 8).reshape(2 * tok, head_dim)
    d_values = dot("qk,qe->ke", probs_low, d_heads)
    d_probs = dot("qe,ke->qk", d_heads, values)
    d_scores = (
        attn_probs * (d_probs - jnp.sum(attn_probs * d_probs, axis=1, keepdims=True))
    ).astype(bf16)
    d_queries = dot("qk,ke->qe", d_scores, keys) * score_scale
    d_keys = dot("qk,qe->ke", d_scores, queries) * score_scale
    dkv = jnp.concatenate(
        [d_keys.reshape(N_DP, tok, head_dim), d_values.reshape(N_DP, tok, head_dim)], axis=1
    ).astype(bf16)
    got_kv, d_queries = scatter_keys(
        dkv, d_queries.astype(bf16).reshape(2, tok, head_dim), 9
    )
    d_kv = jnp.sum(got_kv.astype(f32).reshape(8, 2, 2, tok, head_dim), axis=0)
    d_q = rotate(d_queries.astype(f32).transpose(1, 0, 2), cosine, -sine)
    d_k = rotate(d_kv[:, 0].transpose(1, 0, 2), cosine, -sine)
    d_v = d_kv[:, 1].transpose(1, 0, 2)
    d_proj = jnp.stack([d_q, d_k, d_v], axis=1).astype(bf16)
    d_normed_one = dot("tshe,dshe->td", d_proj, qkv_weight).astype(bf16)
    qkv_part = dot("td,tshe->dshe", normed_one, d_proj).astype(bf16)
    bias_part = jnp.sum(d_proj.astype(f32), axis=0)
    input_grad, stats_three = join(
        input_finish,
        [d_normed_one.reshape(N_T, part_rows, width)],
        [layer_input.reshape(N_T, part_rows, width), d_middle],
        [attn_gain.reshape(1, width)],
        1,
        [(8, width)],
        10,
        "join_input",
    )
    input_grad = input_grad.reshape(tok, width).astype(f32)

    def slices(row):
        return row.reshape(-1, N_DP, 128).transpose(1, 0, 2)

    five = jnp.concatenate([jnp.sum(stats_one[:3], axis=1), jnp.sum(stats_two[1:3], axis=1)])
    pack = jnp.concatenate(
        [
            slices(router_part),
            slices(gate_vec_part),
            slices(stats_two[0]),
            slices(stats_three[0]),
            jnp.broadcast_to(jnp.pad(five, (0, 123))[None, None], (N_DP, 1, 128)),
            jnp.pad(
                bias_part.reshape(6, N_DP, 8).transpose(1, 0, 2).reshape(N_DP, 1, 48),
                ((0, 0), (0, 3), (0, 80)),
            ),
        ],
        axis=1,
    )
    over_dp, over_both = sum_small(pack, 11)
    bias_grad = over_dp[20, :48].reshape(3, 2, 8)
    router_grad = over_both[:16].T
    rms_stats = jnp.sqrt(over_both[19, :5] / (stream * width))

    def scattered(part, dim):
        return lax.psum_scatter(part, "dp", scatter_dimension=dim, tiled=True).astype(f32)

    return (
        output.reshape(tok, width),
        input_grad,
        scattered(qkv_part, 0),
        bias_grad,
        scattered(outproj_part, 2),
        over_both[18],
        over_both[17],
        router_grad,
        over_both[16],
        scattered(shared_in_part, 0),
        scattered(shared_out_part, 1),
        expert_in_grad,
        expert_out_grad,
        rms_stats,
    )


def solution(mesh):
    in_specs = (
        P("dp", None),
        P(),
        P("dp", None),
        P(),
        P(None, None, "tensor", None),
        P(None, "tensor", None),
        P("tensor", None, None),
        P(),
        P(),
        P(),
        P(None, None, "tensor"),
        P("tensor", None),
        P("dp", None, None, "tensor"),
        P("dp", "tensor", None),
        P("dp", None),
    )
    out_specs = (
        P("dp", None),
        P("dp", None),
        P("dp", None, "tensor", None),
        P(None, "tensor", "dp"),
        P("tensor", None, "dp"),
        P("dp"),
        P("dp"),
        P("dp", None),
        P("dp"),
        P("dp", None, "tensor"),
        P("tensor", "dp"),
        P("dp", None, None, "tensor"),
        P("dp", "tensor", None),
        P(),
    )
    return jax.shard_map(
        on_device, mesh=mesh, in_specs=in_specs, out_specs=out_specs, check_vma=False
    )
```

time: 2270 us -> 835 us (0.37)
  waiting for transfers between devices: 1420 us -> 35.8 us
  Pallas kernels: 0 us -> 521 us
  blocking collectives: 336 us -> 0 us
  local copies, waits for them, and re-layouts: 200 us -> 61.1 us
  other arithmetic: 127 us -> 63.2 us
    psum x5 -> x0, waiting for transfers between devices: 634 us -> none  [the longest x1 350 us: on_device(): lax.psum((d_normed_two, router_part, gate_vec_part), 'tensor')]
    pallas_call x0 -> x11, Pallas kernels: none -> 521 us  [the longest x3 182 us: join(): pl.pallas_call(kernel, out_shape=tuple((jax.ShapeDtypeStruct((N_T, rows,...]
    reduce_scatter x7 -> x1, waiting for transfers between devices: 447 us -> 0.01 us  [scattered(): lax.psum_scatter(part, 'dp', scatter_dimension=dim, tiled=True).astype(f32)]
    all_to_all x2 -> x0, waiting for transfers between devices: 298 us -> none  [the longest x1 187 us: on_device(): lax.all_to_all(d_rows.reshape(data_size, capacity, model_width), 'dp', sp...]
    all_to_all x2 -> x0, blocking collectives: 261 us -> none  [the longest x1 168 us: on_device(): lax.all_to_all(send_grads.reshape(experts, capacity, model_width), 'dp',...]
    reshape x11 -> x2, local copies, waits for them, and re-layouts: 104 us -> 0.15 us  [on_device(): bias_part.reshape(6, N_DP, 8).transpose(1, 0, 2).reshape(N_DP, 1, 48)]
    unnamed x1 -> x0, blocking collectives: 54.2 us -> none
    all_gather x2 -> x0, waiting for transfers between devices: 37 us -> none  [the longest x1 34.2 us: on_device(): lax.all_gather(keys_own, 'dp', axis=0, tiled=True)]
  transfers between devices with their start and end apart: 16 -> 8, of which waited for: 14 -> 1; matrix products, arithmetic and copies ran while one was open for 12% -> 24% of each run, Pallas kernels for 0% -> 42%
where the time goes in v1:
time: 835 us; the launch traced here: 827 us
  Pallas kernels  521 us (62%)
  matrix products  127 us (15%)
  other arithmetic  63.2 us (8%)
  local copies, waits for them, and re-layouts  61.1 us (7%)
  waiting for transfers between devices  35.8 us (4%)
  between operations  15.3 us (2%)
    pallas_call x3, Pallas kernels, join(): pl.pallas_call(kernel, out_shape=tuple((jax.ShapeDtypeStruct((N_T, rows,...  182 us
    dot_general x32, matrix products, dot(): return jnp.einsum(pattern, a, b, preferred_element_type=f32)  120 us
    pallas_call x2, Pallas kernels, rows_out(): pl.pallas_call(kernel, out_shape=jax.ShapeDtypeStruct((8,) + x.shape[1:],...  110 us
    pallas_call x1, Pallas kernels, rows_back(): pl.pallas_call(kernel, out_shape=tuple((jax.ShapeDtypeStruct((N_DP,) + x....  98 us
    pallas_call x1, Pallas kernels, scatter_keys(): pl.pallas_call(kernel, out_shape=(jax.ShapeDtypeStruct(dkv.shape, dkv.dty...  60.1 us
    pallas_call x1, Pallas kernels, gather_keys(): pl.pallas_call(kernel, out_shape=(jax.ShapeDtypeStruct((N_DP,) + kv.shape...  41.7 us
    ppermute x1, waiting for transfers between devices, on_device(): got_out = lax.ppermute(send_out, 'tensor', pairs)  35.7 us
    unnamed x177, local copies, waits for them, and re-layouts  34.8 us
  transfers between devices with their start and end apart: 8, of which 1 were waited for; matrix products, arithmetic and copies ran while one was open for 24% of the time, Pallas kernels for 42%

profile of v1, /device:TPU:1, one launch (start us, length us, event | category | flops | bytes accessed | tf_op | source)
XLA Modules:
  0.0 826.5 jit_solution(7994659499869259004)
XLA Ops:
  7.2 2.2 collective-permute-start
  9.5 1.7 fusion.26
  11.9 2.6 fusion.36
  17.6 1.9 fusion.87
  24.3 41.7 %gather_keys.1 = (bf16[16,640,128]{2,1,0:T(8,128)(2,1)}, bf16[2,320,128]{2,1,0:T(8,128)(2,1)}) custom-call(bf16[2,640,128]{2,1,0:T(8,128)(2,1)} %pad_maximum_fusion.13.kv_ref, bf16[2,320,128]{2,1,0:T(8,128)(2,1)} %get-tuple-element.163.q_ref), custom_call_target="tpu_custom_call" | custom-call | tf_op jit(solution)/shard_map/gather_keys/pallas_call | solution.py:80
  66.0 3.5 fusion.88
  69.9 4.9 fusion.5
  74.8 4.9 fusion.8
  79.7 4.9 fusion.7
  84.7 3.1 fusion.42
  87.8 1.7 copy-done.16
  89.5 3.8 swap_cores.2
  93.3 2.0 fusion.22
  95.3 40.8 %join_attn.1 = (bf16[8,40,2048]{2,1,0:T(8,128)(2,1)S(1)}, f32[40,2048]{1,0:T(8,128)S(1)}, f32[8,2048]{1,0:T(8,128)S(1)}) custom-call(bf16[8,40,2048]{2,1,0:T(8,128)(2,1)S(1)} %bitcast.285, bf16[8,40,2048]{2,1,0:T(8,128)(2,1)S(1)} %bitcast.277, f32[1,2048]{1,0:T(1,128)S(1)} %bitcast.291), custom_call_target="tpu_custom_call" | custom-call | tf_op jit(solution)/shard_map/join_attn/pallas_call | solution.py:323
  136.1 6.0 convolution_convert_fusion.1
  142.1 55.3 %rows_out.2 = bf16[8,112,2048]{2,1,0:T(8,128)(2,1)} custom-call(bf16[16,112,2048]{2,1,0:T(8,128)(2,1)} %bitcast.312), custom_call_target="tpu_custom_call" | custom-call | tf_op jit(solution)/shard_map/rows_out/pallas_call | solution.py:150
  197.4 1.8 convolution_reduce_fusion
  199.2 8.6 %convolution_convert_fusion = bf16[1792,2048]{1,0:T(8,128)(2,1)} fusion(pred[1792,320]{1,0:T(32,128)(4,1)} %get-tuple-element.149, bf16[320,2048]{1,0:T(8,128)(2,1)} %param.31), kind=kOutput, calls=%fused_computation.12 | convolution fusion | flops 2352480256 | bytes 9224192 | tf_op jit(solution)/shard_map/rt,td->rd/dot_general | solution.py:425
  209.1 6.1 fusion.94
  217.7 54.7 %rows_out.3 = bf16[8,112,2048]{2,1,0:T(8,128)(2,1)} custom-call(bf16[16,112,2048]{2,1,0:T(8,128)(2,1)} %bitcast.311), custom_call_target="tpu_custom_call" | custom-call | tf_op jit(solution)/shard_map/rows_out/pallas_call | solution.py:150
  273.3 5.6 fusion.62
  278.9 3.0 fusion.50
  281.9 4.6 fusion.31
  286.5 1.6 fusion.56
  289.5 5.0 multiply_convert_fusion.1
  294.6 6.7 fusion.6
  301.2 98.0 %rows_back.1 = (bf16[16,112,2048]{2,1,0:T(8,128)(2,1)}, bf16[16,112,2048]{2,1,0:T(8,128)(2,1)}) custom-call(bf16[8,112,2048]{2,1,0:T(8,128)(2,1)} %bitcast.318, bf16[8,112,2048]{2,1,0:T(8,128)(2,1)} %bitcast.317), custom_call_target="tpu_custom_call" | custom-call | tf_op jit(solution)/shard_map/rows_back/pallas_call | solution.py:210
  399.9 3.9 add_convert_fusion
  403.8 5.0 fusion.21
  408.8 80.0 %join_ffn.1 = (bf16[8,40,2048]{2,1,0:T(8,128)(2,1)S(1)}, bf16[8,40,2048]{2,1,0:T(8,128)(2,1)S(1)}, f32[40,2048]{1,0:T(8,128)S(1)}, f32[8,2048]{1,0:T(8,128)S(1)}) custom-call(bf16[8,40,2048]{2,1,0:T(8,128)(2,1)S(1)} %bitcast.289, bf16[8,40,2048]{2,1,0:T(8,128)(2,1)S(1)} %bitcast.279, bf16[8,40,2048]{2,1,0:T(8,128)(2,1)} %bitcast.313, ...), custom_call_target="tpu_custom_call" | custom-call | tf_op jit(solution)/shard_map/join_ffn/pallas_call | solution.py:323
  492.3 1.7 convolution_convert_fusion.5
  494.0 3.7 copy.71
  497.7 2.3 copy.106
  500.3 4.8 convolution_convert_fusion.4
  505.1 4.6 copy.75
  510.5 10.1 %fusion.4 = bf16[5120,640]{0,1:T(8,128)(2,1)} fusion(f32[640,5120]{1,0:T(8,128)} %copy-done.15, f32[640]{0:T(1024)S(1)} %copy-done.60, f32[640]{0:T(1024)S(1)} %copy-done.58, s32[5120]{0:T(1024)S(1)} %copy-done.46, s32[5120]{0:T(1024)S(1)} %copy-done.41, s32[640]{0:T(1024)S(1)} %copy-done.55, s32[640]{0:T(1024)S(1)} %copy-done.53), kind=kLoop, calls=%fused_computation.8 | loop fusion | flops 29491200 | bytes 19712000 | tf_op jit(solution)/shard_map/convert_element_type | solution.py:547
  520.6 9.5 %copy.57 = bf16[5120,640]{1,0:T(8,128)(2,1)} copy(bf16[5120,640]{0,1:T(8,128)(2,1)} %fusion.4) | data formatting | bytes 13107200 | tf_op jit(solution)/shard_map/convert_element_type | solution.py:547
  530.1 2.8 fusion.45.x_ref
  532.9 6.2 swap_cores.3
  539.2 7.3 multiply_reduce_fusion
  546.5 4.9 convolution_convert_fusion.7
  551.5 8.1 multiply_convert_fusion
  559.6 4.9 fusion.11
  564.5 1.7 pad_maximum_fusion.1.x_ref
  566.3 2.5 fusion.41
  568.9 60.1 %scatter_keys.1 = (bf16[16,640,128]{2,1,0:T(8,128)(2,1)}, bf16[2,320,128]{2,1,0:T(8,128)(2,1)}) custom-call(bf16[16,640,128]{2,1,0:T(8,128)(2,1)} %pad_maximum_fusion.1.x_ref, bf16[2,320,128]{2,1,0:T(8,128)(2,1)} %bitcast.335), custom_call_target="tpu_custom_call" | custom-call | tf_op jit(solution)/shard_map/scatter_keys/pallas_call | solution.py:247
  630.0 2.2 convert_reduce_fusion
  634.4 3.7 convolution_convert_fusion.3
  638.1 7.3 convolution_convert_fusion.2
  645.4 8.5 %copy.77 = bf16[2048,1408]{1,0:T(8,128)(2,1)} copy(bf16[2048,1408]{0,1:T(8,128)(2,1)} %bitcast.314) | data formatting | bytes 11534336
  653.9 6.1 copy.70
  660.5 2.4 fusion.23
  663.0 61.5 %join_input.1 = (bf16[8,40,2048]{2,1,0:T(8,128)(2,1)S(1)}, f32[8,2048]{1,0:T(8,128)S(1)}) custom-call(bf16[8,40,2048]{2,1,0:T(8,128)(2,1)S(1)} %bitcast.290, bf16[8,40,2048]{2,1,0:T(8,128)(2,1)S(1)} %bitcast.278, f32[40,2048]{1,0:T(8,128)S(1)} %copy-done.11, f32[1,2048]{1,0:T(1,128)S(1)} %bitcast.293), custom_call_target="tpu_custom_call" | custom-call | tf_op jit(solution)/shard_map/join_input/pallas_call | solution.py:323
  729.2 19.2 %sum_small.1 = (f32[24,128]{1,0:T(8,128)}, f32[24,128]{1,0:T(8,128)}) custom-call(f32[16,24,128]{2,1,0:T(8,128)} %concatenate.44.x_ref), custom_call_target="tpu_custom_call" | custom-call | tf_op jit(solution)/shard_map/sum_small/pallas_call | solution.py:373
  748.4 1.4 fusion.54
  749.9 3.8 fusion.96
  756.4 1.8 convolution_convert_fusion.6
  758.2 3.3 fusion.95
  764.5 3.1 bitcast_convert_fusion
  767.7 35.7 %collective-permute-done.3 = bf16[176,2048]{1,0:T(8,128)(2,1)S(1)} collective-permute-done((bf16[176,2048]{1,0:T(8,128)(2,1)}, bf16[176,2048]{1,0:T(8,128)(2,1)S(1)}, u32[]{:S(2)}, u32[]{:S(2)}) %collective-permute-start.3) | collective-permute-done | bytes 720928 | tf_op jit(solution)/shard_map/ppermute | solution.py:606
  803.4 3.0 add_bitcast_fusion.1
  806.4 3.3 add_bitcast_fusion
  813.3 1.9 copy.65
  817.3 2.5 copy.114
  (259 shorter events, 40.6 us)
Async XLA Ops:
  7.2 4.7 copy-start
  7.2 802.6 %reduce-scatter.13.cloned.1.call-start = ((), (), s32[]{:S(2)}) async-start(), calls=%async_computation.5 | async-start | bytes 1114112
  7.2 271.6 %collective-permute-start = (bf16[176,2048]{1,0:T(8,128)(2,1)}, bf16[176,2048]{1,0:T(8,128)(2,1)}, u32[]{:S(2)}, u32[]{:S(2)}) collective-permute-start(bf16[176,2048]{1,0:T(8,128)(2,1)} %bitcast.343), channel_id=1, source_target_pairs={{0,1},{1,0},{2,3},{3,2},{4,5},{5,4},{6,7},{7,6},{8,9},{9,8},{10,11... | collective-permute-start | bytes 2162696 | tf_op jit(solution)/shard_map/ppermute | solution.py:504
  9.4 272.4 %collective-permute-start.1 = (bf16[2048,2,176]{0,2,1:T(8,128)(2,1)}, bf16[2048,2,176]{0,2,1:T(8,128)(2,1)}, u32[]{:S(2)}, u32[]{:S(2)}) collective-permute-start(bf16[2048,2,176]{0,2,1:T(8,128)(2,1)} %bitcast.340), channel_id=1, source_target_pairs={{0,1},{1,0},{2,3},{3,2},{4,5},{5,4},{6,7},{7,6},{8,9},{9,8},{10,11... | collective-permute-start | bytes 4325384 | tf_op jit(solution)/shard_map/ppermute | solution.py:503
  11.2 3.3 copy-start.72
  11.9 4.2 copy-start.71
  14.5 4.9 copy-start.78
  19.6 3.9 copy-start.44
  19.8 59.9 %copy-start.40 = (s32[5120]{0:T(1024)}, s32[5120]{0:T(1024)S(1)}, u32[]{:S(2)}) copy-start(s32[5120]{0:T(1024)S(1)} %convert_reduce_fusion.3) | copy-start | bytes 61444
  66.0 3.9 copy-start.76
  69.6 10.1 %copy-start.45 = (s32[5120]{0:T(1024)}, s32[5120]{0:T(1024)S(1)}, u32[]{:S(2)}) copy-start(s32[5120]{0:T(1024)S(1)} %add_select_fusion) | copy-start | bytes 61444
  69.7 9.9 %copy-start.52 = (s32[640]{0:T(1024)}, s32[640]{0:T(1024)S(1)}, u32[]{:S(2)}) copy-start(s32[640]{0:T(1024)S(1)} %convert_reduce_fusion.4) | copy-start | bytes 7684
  69.9 9.8 %copy-start.54 = (s32[640]{0:T(1024)}, s32[640]{0:T(1024)S(1)}, u32[]{:S(2)}) copy-start(s32[640]{0:T(1024)S(1)} %add_select_fusion.1) | copy-start | bytes 7684
  74.8 5.0 copy-start.15
  74.8 5.0 copy-start.57
  79.7 5.0 copy-start.59
  79.7 5.0 copy-start.26
  84.7 4.8 copy-start.16
  84.7 10.6 %copy-start.12 = (f32[2048]{0:T(1024)S(1)}, f32[2048]{0:T(1024)}, u32[]{:S(2)}) copy-start(f32[2048]{0:T(1024)} %param.24) | copy-start | bytes 24580
  93.3 42.8 %copy-start.42 = (pred[16,112,320]{2,1,0:T(8,128)(4,1)S(1)}, pred[16,112,320]{2,1,0:T(8,128)(4,1)}, u32[]{:S(2)}) copy-start(pred[16,112,320]{2,1,0:T(8,128)(4,1)} %iota_compare_fusion) | copy-start | bytes 1720324
  136.1 6.0 copy-start.4
  142.1 55.3 %copy-start.63 = (bf16[2048]{0:T(1024)(128)(2,1)S(1)}, bf16[2048]{0:T(1024)(128)(2,1)}, u32[]{:S(2)}) copy-start(bf16[2048]{0:T(1024)(128)(2,1)} %param.26) | copy-start | bytes 12292
  199.2 16.1 %copy-start.61 = (f32[320]{0:T(512)}, f32[320]{0:T(512)S(1)}, u32[]{:S(2)}) copy-start(f32[320]{0:T(512)S(1)} %convolution_reduce_fusion) | copy-start | bytes 3844
  199.2 8.6 %copy-start.17 = (bf16[8,112,2048]{2,1,0:T(8,128)(2,1)S(1)}, bf16[8,112,2048]{2,1,0:T(8,128)(2,1)}, u32[]{:S(2)}) copy-start(bf16[8,112,2048]{2,1,0:T(8,128)(2,1)} %rows_out.2) | copy-start | bytes 11010052
  199.2 8.6 %copy-start.48 = (bf16[2048,16]{0,1:T(8,128)(2,1)S(1)}, bf16[2048,16]{0,1:T(8,128)(2,1)}, u32[]{:S(2)}) copy-start(bf16[2048,16]{0,1:T(8,128)(2,1)} %param.25) | copy-start | bytes 196612
  208.9 6.4 copy-start.32
  273.3 5.6 copy-start.20
  273.3 5.6 copy-start.75
  278.9 3.0 copy-start.18
  278.9 3.0 copy-start.74
  288.1 6.4 copy-start.29
  288.1 6.4 copy-start.30
  399.8 3.9 copy-start.62
  399.8 4.0 copy-start.69
  399.9 4.0 copy-start.79
  399.9 4.0 copy-start.80
  403.8 5.0 copy-start.67
  408.8 83.5 %copy-start.38 = (bf16[2,320,128]{2,1,0:T(8,128)(2,1)S(1)}, bf16[2,320,128]{2,1,0:T(8,128)(2,1)}, u32[]{:S(2)}) copy-start(bf16[2,320,128]{2,1,0:T(8,128)(2,1)} %swap_cores.2) | copy-start | bytes 491524
  494.0 6.3 copy-start.56
  500.0 311.4 %reduce-scatter.17.cloned.1.call-start = ((), (), s32[]{:S(2)}) async-start(), calls=%async_computation.7 | async-start | bytes 3342336
  509.8 303.5 %reduce-scatter.11.cloned.1.call-start = ((), (), s32[]{:S(2)}) async-start(), calls=%async_computation.4 | async-start | bytes 3342336 | tf_op jit(solution)/shard_map/reduce_scatter | solution.py:705
  539.2 7.3 copy-start.35
  539.2 12.2 %slice-start = ((s8[13107200]{0:T(1024)(128)(4,1)}), s8[524288]{0:T(1024)(128)(4,1)S(1)}, s32[]{:S(2)}) async-start(s8[13107200]{0:T(1024)(128)(4,1)} %bitcast.294), calls=%async_computation.8 | async-start | bytes 1048576
  539.2 12.2 %slice-start.1 = ((s8[13107200]{0:T(1024)(128)(4,1)}), s8[4194304]{0:T(1024)(128)(4,1)S(1)}, s32[]{:S(2)}) async-start(s8[13107200]{0:T(1024)(128)(4,1)} %bitcast.294), calls=%async_computation.9 | async-start | bytes 8388608
  539.2 12.2 %slice-start.2 = ((s8[13107200]{0:T(1024)(128)(4,1)}), s8[4194304]{0:T(1024)(128)(4,1)S(1)}, s32[]{:S(2)}) async-start(s8[13107200]{0:T(1024)(128)(4,1)} %bitcast.294), calls=%async_computation.10 | async-start | bytes 8388608
  546.5 4.9 slice-start.3
  551.4 8.1 copy-start.77
  559.6 6.6 copy-start.27
  629.0 3.3 copy-start.37
  629.0 3.3 copy-start.43
  638.1 177.1 %reduce-scatter.15.cloned.1.call-start = ((), (), s32[]{:S(2)}) async-start(), calls=%async_computation.6 | async-start | bytes 6127616
  653.9 6.3 copy-start.68
  653.9 6.3 copy-start.64
  660.5 66.3 %copy-start.25 = (bf16[2048,896]{1,0:T(8,128)(2,1)S(1)}, bf16[2048,896]{1,0:T(8,128)(2,1)}, u32[]{:S(2)}) copy-start(bf16[2048,896]{1,0:T(8,128)(2,1)} %copy.70) | copy-start | bytes 11010052
  662.9 63.6 %copy-start.6 = (bf16[8,40,2048]{2,1,0:T(8,128)(2,1)S(1)}, bf16[8,40,2048]{2,1,0:T(8,128)(2,1)}, u32[]{:S(2)}) copy-start(bf16[8,40,2048]{2,1,0:T(8,128)(2,1)} %copy-done.4) | copy-start | bytes 3932164
  662.9 63.8 %copy-start.34 = (f32[896,16]{0,1:T(8,128)S(1)}, f32[896,16]{0,1:T(8,128)}, u32[]{:S(2)}) copy-start(f32[896,16]{0,1:T(8,128)} %copy-done.32) | copy-start | bytes 172036
  662.9 63.8 %copy-start.51 = (f32[896]{0:T(1024)S(1)}, f32[896]{0:T(1024)}, u32[]{:S(2)}) copy-start(f32[896]{0:T(1024)} %copy-done.50) | copy-start | bytes 10756
  662.9 63.8 %copy-start.66 = (f32[16]{0:T(128)S(1)}, f32[16]{0:T(128)}, u32[]{:S(2)}) copy-start(f32[16]{0:T(128)} %compare_convert_fusion) | copy-start | bytes 196
  753.7 2.8 copy-start.31
  755.0 3.2 copy-start.19
  755.0 51.4 %collective-permute-start.2 = (bf16[2048,2,176]{0,2,1:T(8,128)(2,1)}, bf16[2048,2,176]{0,2,1:T(8,128)(2,1)}, u32[]{:S(2)}, u32[]{:S(2)}) collective-permute-start(bf16[2048,2,176]{0,2,1:T(8,128)(2,1)} %convert_element_type.228), channel_id=1, source_target_pairs={{0,1},{1,0},{2,3},{3,2},{4,5},{5,4},{6,7},{7,6},{8,9},{9,8},{10,11... | collective-permute-start | bytes 4325384 | tf_op jit(solution)/shard_map/ppermute | solution.py:605
  762.8 40.5 %copy-start.22 = (bf16[8,112,2048]{2,1,0:T(8,128)(2,1)S(1)}, bf16[8,112,2048]{2,1,0:T(8,128)(2,1)}, u32[]{:S(2)}) copy-start(bf16[8,112,2048]{2,1,0:T(8,128)(2,1)} %rows_out.3) | copy-start | bytes 11010052
  762.8 40.5 %collective-permute-start.3 = (bf16[176,2048]{1,0:T(8,128)(2,1)}, bf16[176,2048]{1,0:T(8,128)(2,1)S(1)}, u32[]{:S(2)}, u32[]{:S(2)}) collective-permute-start(bf16[176,2048]{1,0:T(8,128)(2,1)} %convolution_convert_fusion.6), channel_id=1, source_target_pairs={{0,1},{1,0},{2,3},{3,2},{4,5},{5,4},{6,7},{7,6},{8,9},{9,8},{10,11... | collective-permute-start | bytes 2162696 | tf_op jit(solution)/shard_map/ppermute | solution.py:606
  767.7 38.8 %copy-start.28 = (f32[2048,352]{0,1:S(1)}, f32[2048,352]{0,1}, u32[]{:S(2)}) copy-start(f32[2048,352]{0,1} %fusion.95) | copy-start | bytes 8650756
  (27 other events, 39.6 us)
Sparse Core Ops, SparseCore 0:
  500.1 58.8 reduce-scatter.12
  561.6 78.2 reduce-scatter.16
  642.5 73.1 reduce-scatter.10
  718.0 78.5 reduce-scatter.14

commit v2 on v0

v2 whole, which is shorter than its diff:
```python
import math

import jax
import jax.numpy as jnp
from jax import lax
from jax.experimental import pallas as pl
from jax.experimental.pallas import tpu as pltpu
from jax.sharding import PartitionSpec as P

DBLOCK = 256
EPSILON = 1e-06
THETA = 1000000.0
NEG_FILL = -1e30
MESH = pl.DeviceIdType.MESH
f32 = jnp.float32
bf16 = jnp.bfloat16
N_DP = 16
N_T = 8
SLOTS = 112
LIMIT = 48 * 1024 * 1024
CODE = 1 << 16

HBM = pl.BlockSpec(memory_space=pl.ANY)
VMEM = pl.BlockSpec(memory_space=pltpu.VMEM)


def greet(peers, more=None):
    barrier = pltpu.get_barrier_semaphore()
    for peer in peers:
        pl.semaphore_signal(barrier, inc=1, device_id=peer, device_id_type=MESH)
    count = len(peers)
    if more is not None:
        count = count + more.greet()
    pl.semaphore_wait(barrier, count)


def remote(src, dst, send, recv, device):
    return pltpu.make_async_remote_copy(
        src_ref=src,
        dst_ref=dst,
        send_sem=send,
        recv_sem=recv,
        device_id=device,
        device_id_type=MESH,
    )


def dma(*shape):
    return pltpu.SemaphoreType.DMA(shape)


def cost(micros):
    return pl.CostEstimate(flops=0, bytes_accessed=int(micros * 3e6), transcendentals=0)


def comm_params(number, limit=None):
    return pltpu.CompilerParams(
        collective_id=number, has_side_effects=True, vmem_limit_bytes=limit
    )


GROUPS = 4
ORDER = (4, 12, 2, 5, 13, 3, 8, 6, 14, 9, 7, 15, 10, 11, 1)
STEPS = (1, 3, 2, 4, 5, 7, 6)
CHUNKS = ((0, 48), (48, 64))


def sems(*counts):
    return [dma(*c) if isinstance(c, tuple) else dma(c) for c in counts]


def dp_peers():
    me = lax.axis_index("dp")
    return [{"dp": me ^ k} for k in range(1, N_DP)]


def tensor_peers():
    me = lax.axis_index("tensor")
    return [{"tensor": me ^ k} for k in range(1, N_T)]


def coordinates():
    d, t = lax.axis_index("dp"), lax.axis_index("tensor")
    return d, d // 4, t // 4, t % 4


def route_plane():
    d, z, _, y = coordinates()
    plane = 2 * ((z + d // 2) % 2) + d % 2
    return plane, y ^ plane


class Rows:
    def __init__(self, x_ref, out_ref, send, recv, local, back=False):
        self.x, self.out, self.send, self.recv, self.local, self.back = x_ref, out_ref, send, recv, local, back
        d, z, half, y = coordinates()
        plane, offset = route_plane()
        if back:
            experts = [{"dp": 4 * k + offset, "tensor": 4 * half + plane} for k in range(GROUPS)]
            target = y ^ (d % 4)
        else:
            experts = [{"dp": 4 * (z ^ offset) + j, "tensor": 4 * half + plane} for j in range(GROUPS)]
        groups = [
            {
                "dp": 4 * g + 2 * ((y // 2 + g) % 2) + y % 2,
                "tensor": 4 * half + (target if back else y ^ g ^ z),
            }
            for g in range(GROUPS)
        ]
        self.peers, self.sources = (groups, experts) if back else (experts, groups)
        self.slot = z
        self.mine = z if back else d % 4
        self.own = offset == 0
        if back:
            self.own = jnp.logical_and(self.own, d % 4 == 0)
        self.d = d

    def is_own(self, j):
        return jnp.logical_and(self.own, self.mine == j)

    def greet(self):
        barrier = pltpu.get_barrier_semaphore()
        for j in range(GROUPS):
            source = self.sources[j]

            @pl.when(jnp.logical_not(jnp.logical_and(self.own, self.slot == j)))
            def _():
                pl.semaphore_signal(barrier, inc=1, device_id=source, device_id_type=MESH)

        return GROUPS - self.own.astype(jnp.int32)

    def copy(self, j, c):
        rows = pl.ds(*CHUNKS[c])
        return remote(
            self.x.at[j, rows],
            self.out.at[self.slot, rows],
            self.send.at[c, j],
            self.recv.at[c, self.slot],
            self.peers[j],
        )

    def arrival(self, j, c):
        rows = pl.ds(*CHUNKS[c])
        return remote(
            self.x.at[j, rows],
            self.out.at[j, rows],
            self.send.at[c, j],
            self.recv.at[c, j],
            self.peers[j],
        )

    def inside(self):
        return pltpu.make_async_copy(self.x.at[self.mine], self.out.at[self.slot], self.local.at[0])

    def start(self):
        for c in range(len(CHUNKS)):
            for j in range(GROUPS):

                @pl.when(jnp.logical_not(self.is_own(j)))
                def _():
                    self.copy(j, c).start()

        @pl.when(self.own)
        def _():
            self.inside().start()

    def wait(self):
        @pl.when(self.own)
        def _():
            self.inside().wait()

        for c in range(len(CHUNKS)):
            for j in range(GROUPS):

                @pl.when(jnp.logical_not(self.is_own(j)))
                def _():
                    self.copy(j, c).wait_send()

                @pl.when(jnp.logical_not(jnp.logical_and(self.own, self.slot == j)))
                def _():
                    self.arrival(j, c).wait_recv()


ROW_SEMS = sems((len(CHUNKS), GROUPS), (len(CHUNKS), GROUPS), 1)


class Exchange:
    def __init__(self, x_ref, out_ref, send, recv, local):
        me = lax.axis_index("dp")
        self.copies = [
            remote(x_ref.at[me ^ k], out_ref.at[me], send.at[k], recv.at[k], {"dp": me ^ k})
            for k in ORDER
        ]
        self.copies.append(pltpu.make_async_copy(x_ref.at[me], out_ref.at[me], local.at[0]))

    def start(self):
        for copy in self.copies:
            copy.start()

    def wait(self):
        for copy in self.copies:
            copy.wait()


DP_SEMS = sems(N_DP, N_DP, 1)


class Swap:
    def __init__(self, x_ref, out_ref, send, recv, local):
        me = lax.axis_index("dp")
        core = lax.rem(me, 2)
        self.copies = [
            remote(x_ref.at[1 - core], out_ref.at[core], send.at[0], recv.at[0], {"dp": me ^ 1}),
            pltpu.make_async_copy(x_ref.at[core], out_ref.at[core], local.at[0]),
        ]

    start = Exchange.start
    wait = Exchange.wait


SWAP_SEMS = sems(1, 1, 1)


class DirectScatter:
    def __init__(self, part_ref, got, send, recv):
        self.me = lax.axis_index("tensor")
        self.part, self.got = part_ref, got
        self.copies = [
            remote(
                part_ref.at[self.me ^ k], got.at[k], send.at[k], recv.at[k], {"tensor": self.me ^ k}
            )
            for k in STEPS
        ]

    def start(self):
        for copy in self.copies:
            copy.start()

    def total(self):
        value = self.part[self.me].astype(f32)
        for k, copy in zip(STEPS, self.copies):
            copy.wait_recv()
            value = value + self.got[k].astype(f32)
        return value

    def wait_send(self):
        for copy in self.copies:
            copy.wait_send()


class DirectGather:
    def __init__(self, mine, full_ref, send, recv, local):
        me = lax.axis_index("tensor")
        self.mine = mine
        self.copies = [
            remote(mine, full_ref.at[me], send.at[k], recv.at[k], {"tensor": me ^ k}) for k in STEPS
        ]
        self.copies.append(pltpu.make_async_copy(mine, full_ref.at[me], local.at[0]))

    def start(self, value):
        self.mine[...] = value.astype(bf16)
        for copy in self.copies:
            copy.start()

    def wait(self):
        for copy in self.copies:
            copy.wait()


def direct_scratch(rows, width):
    return [
        pltpu.VMEM((N_T, rows, width), bf16),
        pltpu.VMEM((rows, width), bf16),
    ] + sems(N_T, N_T, N_T, N_T, 1)


N_DIRECT = 7


def direct_parts(part_ref, full_ref, scratch):
    got, mine, send, recv, asend, arecv, local = scratch
    return DirectScatter(part_ref, got, send, recv), DirectGather(mine, full_ref, asend, arecv, local)


class Scatter:
    def __init__(self, part_ref, got, mid, last, send, recv):
        t = lax.axis_index("tensor")
        y, half = t % 4, t // 4
        self.part, self.got, self.mid, self.last = part_ref, got, mid, last
        self.slots = (4 * (1 - half) + y, t)
        self.copies = [
            [
                remote(
                    part_ref.at[slot ^ k],
                    got.at[a, k],
                    send.at[a, k],
                    recv.at[a, k],
                    {"tensor": t ^ k},
                )
                for k in (1, 3, 2)
            ]
            for a, slot in enumerate(self.slots)
        ]
        self.across = remote(mid, last, send.at[0, 0], recv.at[0, 0], {"tensor": t ^ 4})

    def start(self):
        for copies in self.copies:
            for copy in copies:
                copy.start()

    def over_y(self, a):
        value = self.part[self.slots[a]].astype(f32)
        for k, copy in zip((1, 3, 2), self.copies[a]):
            copy.wait_recv()
            value = value + self.got[a, k].astype(f32)
        return value

    def middle(self):
        self.mid[...] = self.over_y(0).astype(bf16)
        self.across.start()

    def total(self):
        value = self.over_y(1)
        self.across.wait_recv()
        return value + self.last[...].astype(f32)

    def wait_send(self):
        for copies in self.copies:
            for copy in copies:
                copy.wait_send()
        self.across.wait_send()


class Gather:
    def __init__(self, mine, full_ref, send, recv, local):
        t = lax.axis_index("tensor")
        self.mine = mine
        self.across = remote(
            mine, full_ref.at[t], send.at[0, 0], recv.at[0, 0], {"tensor": t ^ 4}
        )
        self.first = [
            remote(mine, full_ref.at[t], send.at[0, k], recv.at[0, k], {"tensor": t ^ k})
            for k in (1, 3, 2)
        ]
        self.second = [
            remote(
                full_ref.at[t ^ 4],
                full_ref.at[t ^ 4],
                send.at[1, k],
                recv.at[1, k],
                {"tensor": t ^ k},
            )
            for k in (1, 3, 2)
        ]
        self.own = pltpu.make_async_copy(mine, full_ref.at[t], local.at[0])

    def start(self, value):
        self.mine[...] = value.astype(bf16)
        for copy in [self.across] + self.first + [self.own]:
            copy.start()

    def relay(self):
        self.across.wait_recv()
        for copy in self.second:
            copy.start()

    def wait(self):
        self.across.wait_send()
        for copy in self.first + self.second + [self.own]:
            copy.wait()


JOIN_SEMS = sems((2, 4), (2, 4), (2, 4), (2, 4), 1)


def join_scratch(rows, width):
    return [
        pltpu.VMEM((2, 4, rows, width), bf16),
        pltpu.VMEM((rows, width), bf16),
        pltpu.VMEM((rows, width), bf16),
        pltpu.VMEM((rows, width), bf16),
    ] + JOIN_SEMS


N_JOIN = 9


def join_parts(part_ref, full_ref, scratch):
    got, mid, last, mine, send, recv, asend, arecv, local = scratch
    return Scatter(part_ref, got, mid, last, send, recv), Gather(mine, full_ref, asend, arecv, local)


class Sends:
    def __init__(self, messages, send, recv):
        self.copies = [
            remote(src, dst, send.at[i], recv.at[i], peer) for i, (src, dst, peer) in enumerate(messages)
        ]

    start = Exchange.start
    wait = Exchange.wait


def struct(shape, dtype):
    return jax.ShapeDtypeStruct(shape, dtype)


def column_sum(value):
    return jnp.sum(value, axis=0, keepdims=True)


def second_moment(value):
    return lax.rsqrt(jnp.mean(value * value, axis=1, keepdims=True) + EPSILON)


def gather_keys(k, v, q, number):
    tok, size = k.shape[1:]

    def kernel(k_ref, v_ref, q_ref, keys_ref, values_ref, pair_ref, send, recv, local, *more):
        me = lax.axis_index("dp")
        core = lax.rem(me, 2)
        greet(dp_peers())
        swap = Swap(q_ref, pair_ref, *more)
        swap.start()
        rows = pl.ds(pl.multiple_of(me * tok, tok), tok)
        copies = []
        for i, (own, full) in enumerate(((k_ref, keys_ref), (v_ref, values_ref))):
            for step in ORDER:
                head = core if step % 2 == 0 else 1 - core
                copies.append(
                    remote(
                        own.at[head],
                        full.at[rows],
                        send.at[i, step],
                        recv.at[i, step],
                        {"dp": me ^ step},
                    )
                )
            copies.append(pltpu.make_async_copy(own.at[core], full.at[rows], local.at[i]))
        for copy in copies:
            copy.start()
        swap.wait()
        for copy in copies:
            copy.wait()

    return pl.pallas_call(
        kernel,
        out_shape=(
            struct((N_DP * tok, size), bf16),
            struct((N_DP * tok, size), bf16),
            struct(q.shape, bf16),
        ),
        in_specs=[HBM] * 3,
        out_specs=(HBM,) * 3,
        scratch_shapes=sems((2, N_DP), (2, N_DP), 2) + SWAP_SEMS,
        compiler_params=comm_params(number),
        name="gather_keys",
        cost_estimate=cost(41),
    )(k, v, q)


def swap_cores(x, number):
    def kernel(x_ref, out_ref, *scratch):
        greet([{"dp": lax.axis_index("dp") ^ 1}])
        swap = Swap(x_ref, out_ref, *scratch)
        swap.start()
        swap.wait()

    return pl.pallas_call(
        kernel,
        out_shape=struct(x.shape, x.dtype),
        in_specs=[HBM],
        out_specs=HBM,
        scratch_shapes=SWAP_SEMS,
        compiler_params=comm_params(number),
        name="swap_cores",
        cost_estimate=cost(4),
    )(x)


def rows_out(xs, number):
    count = len(xs)

    def kernel(*refs):
        rows = [
            Rows(refs[i], refs[count + i], *refs[2 * count + 3 * i : 2 * count + 3 * i + 3])
            for i in range(count)
        ]
        greet([], rows[0])
        for one in rows:
            one.start()
        for one in rows:
            one.wait()

    return pl.pallas_call(
        kernel,
        out_shape=tuple(struct(x.shape, x.dtype) for x in xs),
        in_specs=[HBM] * count,
        out_specs=(HBM,) * count,
        scratch_shapes=ROW_SEMS * count,
        compiler_params=comm_params(number),
        name="rows_out",
        cost_estimate=cost(42),
    )(*xs)


def rows_back(xs, weights, number):
    count, n = len(xs), len(xs) + len(weights)

    def kernel(*refs):
        d = lax.axis_index("dp")
        scratch = refs[2 * n :]
        rows = [
            Rows(refs[i], refs[n + i], *scratch[3 * i : 3 * i + 3], back=True) for i in range(count)
        ]
        greet([{"dp": d ^ 1}], rows[0])
        sides = Sends(
            [
                (refs[i].at[chip, 1 - lax.rem(d, 2)], refs[n + i].at[chip], {"dp": d ^ 1})
                for i in range(count, n)
                for chip in range(8)
            ],
            *scratch[3 * count :],
        )
        for one in rows:
            one.start()
        sides.start()
        for one in rows:
            one.wait()
        sides.wait()

    return pl.pallas_call(
        kernel,
        out_shape=tuple(struct(x.shape, x.dtype) for x in xs)
        + tuple(struct((w.shape[0],) + w.shape[2:], w.dtype) for w in weights),
        in_specs=[HBM] * n,
        out_specs=(HBM,) * n,
        scratch_shapes=ROW_SEMS * count + sems(8 * len(weights), 8 * len(weights)),
        compiler_params=comm_params(number),
        name="rows_back",
        cost_estimate=cost(42),
    )(*xs, *weights)


def join_attn(part, layer_input, gain, number):
    _, rows, width = part.shape

    def kernel(part_ref, x_ref, gain_ref, full_ref, middle_ref, stats_ref, *scratch):
        greet(tensor_peers())
        scatter, gather = direct_parts(part_ref, full_ref, scratch)
        scatter.start()
        resid = x_ref[lax.axis_index("tensor")].astype(f32)
        attn_out = scatter.total()
        middle = resid + attn_out
        gather.start(middle * second_moment(middle) * gain_ref[...])
        middle_ref[...] = middle
        stats_ref[0:1] = column_sum(resid * resid)
        stats_ref[1:2] = column_sum(attn_out * attn_out)
        stats_ref[2:3] = column_sum(middle * middle)
        scatter.wait_send()
        gather.wait()

    return pl.pallas_call(
        kernel,
        out_shape=(struct(part.shape, bf16), struct((rows, width), f32), struct((8, width), f32)),
        in_specs=[VMEM] * 3,
        out_specs=(HBM, VMEM, VMEM),
        scratch_shapes=direct_scratch(rows, width),
        compiler_params=comm_params(number, LIMIT),
        name="join_attn",
        cost_estimate=cost(40),
    )(part, layer_input, gain)


def join_ffn(part, cotangent, middle, gain, weights, number):
    _, rows, width = part.shape
    n = len(weights)

    def kernel(part_ref, up_ref, middle_ref, gain_ref, *refs):
        w_refs, (full_ref, d_ref, sums_ref), got_refs = refs[:n], refs[n : n + 3], refs[n + 3 : 2 * n + 3]
        scratch = refs[2 * n + 3 :]
        d, z, _, _ = coordinates()
        greet(tensor_peers() + [{"dp": d ^ (4 * k)} for k in (1, 2, 3)])
        scatter, gather = direct_parts(part_ref, full_ref, scratch[:N_DIRECT])
        scatter.start()
        sides = Sends(
            [
                (w_ref.at[z ^ k], got_ref.at[k], {"dp": d ^ (4 * k)})
                for k in (1, 3, 2)
                for w_ref, got_ref in zip(w_refs, got_refs)
            ],
            *scratch[N_DIRECT:],
        )
        sides.start()
        middle = middle_ref[...]
        inv = second_moment(middle)
        d_normed = scatter.total()
        scaled = d_normed * gain_ref[...]
        d_middle = (
            up_ref[lax.axis_index("tensor")].astype(f32)
            + inv * scaled
            - middle * (inv * inv * inv) * jnp.mean(scaled * middle, axis=1, keepdims=True)
        )
        gather.start(d_middle)
        d_ref[...] = d_middle
        sums_ref[0:1] = column_sum(d_normed * middle * inv)
        scatter.wait_send()
        gather.wait()
        sides.wait()

    return pl.pallas_call(
        kernel,
        out_shape=(
            struct(part.shape, bf16),
            struct((rows, width), f32),
            struct((8, width), f32),
        )
        + tuple(struct(w.shape, w.dtype) for w in weights),
        in_specs=[VMEM] * 4 + [HBM] * n,
        out_specs=(HBM, VMEM, VMEM) + (HBM,) * n,
        scratch_shapes=direct_scratch(rows, width) + sems(3 * n, 3 * n),
        compiler_params=comm_params(number, LIMIT),
        name="join_ffn",
        cost_estimate=cost(50),
    )(part, cotangent, middle, gain, *weights)


def scatter_keys(dk, dv, out_part, dq, weights, number):
    n = len(weights)

    def kernel(dk_ref, dv_ref, part_ref, dq_ref, *refs):
        w_refs, (k_ref, v_ref, sum_ref, pair_ref), x_refs = refs[:n], refs[n : n + 4], refs[n + 4 : 2 * n + 4]
        scratch = refs[2 * n + 4 :]
        d = lax.axis_index("dp")
        greet(dp_peers())
        moves = [
            Exchange(dk_ref, k_ref, *scratch[:3]),
            Exchange(dv_ref, v_ref, *scratch[3:6]),
            Swap(dq_ref, pair_ref, *scratch[6:9]),
            Exchange(part_ref, sum_ref, *scratch[9:12]),
            Sends(
                [
                    (w_ref.at[1 - (d // 2) % 2], x_ref, {"dp": d ^ 2})
                    for w_ref, x_ref in zip(w_refs, x_refs)
                ],
                *scratch[12:],
            ),
        ]
        for move in moves:
            move.start()
        for move in moves:
            move.wait()

    return pl.pallas_call(
        kernel,
        out_shape=(
            struct(dk.shape, bf16),
            struct(dv.shape, bf16),
            struct(out_part.shape, out_part.dtype),
            struct(dq.shape, dq.dtype),
        )
        + tuple(struct(w.shape[1:], w.dtype) for w in weights),
        in_specs=[HBM] * (4 + n),
        out_specs=(HBM,) * (4 + n),
        scratch_shapes=DP_SEMS * 2 + SWAP_SEMS + DP_SEMS + sems(n, n),
        compiler_params=comm_params(number),
        name="scatter_keys",
        cost_estimate=cost(50),
    )(dk, dv, out_part, dq, *weights)


def join_tail(part, moe_part, layer_input, middle, d_middle, gain, qkv_part, pack, number):
    _, rows, width = part.shape
    small = pack.shape[1]

    def kernel(part_ref, moe_ref, x_ref, middle_ref, d_ref, gain_ref, qkv_ref, pack_ref, *refs):
        full_ref, out_ref, got_ref, one_ref, both_ref = refs[:5]
        scratch = refs[5:]
        greet(tensor_peers() + dp_peers())
        scatter, gather = join_parts(part_ref, full_ref, scratch[:N_JOIN])
        scatter_moe, gather_moe = join_parts(moe_ref, out_ref, scratch[N_JOIN : 2 * N_JOIN])
        scatter.start()
        scatter_moe.start()
        weights = Exchange(qkv_ref, got_ref, *scratch[2 * N_JOIN : 2 * N_JOIN + 3])
        weights.start()
        own, few, mine, more, send, recv, tsend, trecv = scratch[2 * N_JOIN + 3 :]
        me, t = lax.axis_index("dp"), lax.axis_index("tensor")
        resid = x_ref[t].astype(f32)
        inv = second_moment(resid)
        scatter.middle()
        d_normed = scatter.total()
        scaled = d_normed * gain_ref[...]
        gather.start(
            d_ref[...]
            + inv * scaled
            - resid * (inv * inv * inv) * jnp.mean(scaled * resid, axis=1, keepdims=True)
        )
        gain_grad = column_sum(d_normed * resid * inv)
        scatter_moe.middle()
        moe_out = scatter_moe.total()
        output = middle_ref[...] + moe_out
        gather_moe.start(output)

        def folded(value):
            row = column_sum(value)
            return sum(row[:, i * 128 : (i + 1) * 128] for i in range(width // 128))

        moe_row, out_row = folded(moe_out * moe_out), folded(output * output)
        own[...] = pack_ref[...]
        for i in range(N_DP):
            own[i, small - 3 : small - 2] = moe_row
            own[i, small - 2 : small - 1] = out_row
            own[i, small - 1 : small] = gain_grad[:, i * 128 : (i + 1) * 128]
        firsts = [
            remote(own.at[me ^ k], few.at[k], send.at[k], recv.at[k], {"dp": me ^ k})
            for k in range(1, N_DP)
        ]
        for copy in firsts:
            copy.start()
        gather.relay()
        gather_moe.relay()
        value = own[me]
        for k in range(1, N_DP):
            firsts[k - 1].wait_recv()
            value = value + few[k]
        one_ref[...] = value
        mine[...] = value
        seconds = [
            remote(mine, more.at[k], tsend.at[k], trecv.at[k], {"tensor": t ^ k}) for k in range(1, N_T)
        ]
        for copy in seconds:
            copy.start()
        for k in range(1, N_T):
            seconds[k - 1].wait_recv()
            value = value + more[k]
        both_ref[...] = value
        for copy in firsts + seconds:
            copy.wait_send()
        scatter.wait_send()
        scatter_moe.wait_send()
        gather.wait()
        gather_moe.wait()
        weights.wait()

    return pl.pallas_call(
        kernel,
        out_shape=(
            struct(part.shape, bf16),
            struct(part.shape, bf16),
            struct(qkv_part.shape, qkv_part.dtype),
            struct((small, 128), f32),
            struct((small, 128), f32),
        ),
        in_specs=[VMEM] * 6 + [HBM, VMEM],
        out_specs=(HBM, HBM, HBM, VMEM, VMEM),
        scratch_shapes=join_scratch(rows, width) * 2
        + DP_SEMS
        + [
            pltpu.VMEM((N_DP, small, 128), f32),
            pltpu.VMEM((N_DP, small, 128), f32),
            pltpu.VMEM((small, 128), f32),
            pltpu.VMEM((N_T, small, 128), f32),
        ]
        + sems(N_DP, N_DP, N_T, N_T),
        compiler_params=comm_params(number, LIMIT),
        name="join_tail",
        cost_estimate=cost(60),
    )(part, moe_part, layer_input, middle, d_middle, gain, qkv_part, pack)


KEYS = 256
NT = (((1,), (1,)), ((), ()))
TN = (((0,), (0,)), ((), ()))


def mm(a, b, dims=(((1,), (0,)), ((), ()))):
    return lax.dot_general(a, b, dims, preferred_element_type=f32)


def attend(queries, keys, values, codes, bounds):
    count, size = queries.shape
    stream = keys.shape[0]
    factor = size ** (-0.5) * math.log2(math.e)

    def kernel(q_ref, k_ref, v_ref, code_ref, bound_ref, low_ref, wide_ref, log_ref):
        q = q_ref[...]
        lowest, highest = bound_ref[0:1], bound_ref[1:2]

        def step(i, carry):
            peak, total, acc = carry
            rows = pl.ds(pl.multiple_of(i * KEYS, KEYS), KEYS)
            scores = mm(k_ref[rows], q, NT) * factor
            code = code_ref[rows][:, 0:1]
            seen = (code >= lowest) & (code <= highest)
            scores = jnp.where(seen, scores, NEG_FILL)
            new_peak = jnp.maximum(peak, jnp.max(scores, axis=0, keepdims=True))
            terms = jnp.exp2(scores - new_peak)
            shrink = jnp.exp2(peak - new_peak)
            total = total * shrink + jnp.sum(terms, axis=0, keepdims=True)
            acc = acc * shrink + mm(v_ref[rows], terms.astype(bf16), TN)
            return new_peak, total, acc

        peak, total, acc = lax.fori_loop(
            0,
            stream // KEYS,
            step,
            (
                jnp.full((1, count), NEG_FILL, f32),
                jnp.zeros((1, count), f32),
                jnp.zeros((size, count), f32),
            ),
        )
        out = (acc / total).T
        wide_ref[...] = out
        low_ref[...] = out.astype(bf16)
        log_ref[...] = jnp.broadcast_to(peak + jnp.log2(total), (8, count))

    return pl.pallas_call(
        kernel,
        out_shape=(struct((count, size), bf16), struct((count, size), f32), struct((8, count), f32)),
        in_specs=[VMEM] * 5,
        out_specs=(VMEM,) * 3,
        compiler_params=pltpu.CompilerParams(vmem_limit_bytes=LIMIT),
        name="attend",
        cost_estimate=cost(12),
    )(queries, keys, values, codes, bounds)


def attend_back(queries, keys, values, codes, bounds, wide, logs, d_heads):
    count, size = queries.shape
    stream = keys.shape[0]
    scale = size ** (-0.5)
    factor = scale * math.log2(math.e)

    def kernel(q_ref, k_ref, v_ref, code_ref, bound_ref, wide_ref, log_ref, d_ref, dq_ref, dk_ref, dv_ref):
        q, d_out = q_ref[...], d_ref[...]
        lowest, highest = bound_ref[0:1], bound_ref[1:2]
        log = log_ref[0:1]
        delta = jnp.sum((wide_ref[...] * d_out.astype(f32)).T, axis=0, keepdims=True)

        def step(i, acc):
            rows = pl.ds(pl.multiple_of(i * KEYS, KEYS), KEYS)
            k = k_ref[rows]
            scores = mm(k, q, NT) * factor
            code = code_ref[rows][:, 0:1]
            seen = (code >= lowest) & (code <= highest)
            probs = jnp.where(seen, jnp.exp2(scores - log), 0.0)
            d_probs = mm(v_ref[rows], d_out, NT)
            d_scores = (probs * (d_probs - delta)).astype(bf16)
            dv_ref[rows] = mm(probs.astype(bf16), d_out).astype(bf16)
            dk_ref[rows] = (mm(d_scores, q) * scale).astype(bf16)
            return acc + mm(k, d_scores, TN)

        acc = lax.fori_loop(0, stream // KEYS, step, jnp.zeros((size, count), f32))
        dq_ref[...] = (acc.T * scale).astype(bf16)

    return pl.pallas_call(
        kernel,
        out_shape=(struct((count, size), bf16), struct((stream, size), bf16), struct((stream, size), bf16)),
        in_specs=[VMEM] * 8,
        out_specs=(VMEM,) * 3,
        compiler_params=pltpu.CompilerParams(vmem_limit_bytes=LIMIT),
        name="attend_back",
        cost_estimate=cost(15),
    )(queries, keys, values, codes, bounds, wide, logs, d_heads)


def doc_layout(lengths, token_index):
    doc_ends = jnp.cumsum(lengths)
    starts = doc_ends - lengths
    seq_ids = jnp.sum((token_index[:, None] >= doc_ends[None, :]).astype(jnp.int32), axis=1)
    member = seq_ids[:, None] == jnp.arange(lengths.shape[0], dtype=jnp.int32)[None, :]
    begins = jnp.sum(jnp.where(member, starts[None, :], 0), axis=1)
    offsets = token_index - begins
    return (seq_ids, offsets, offsets // DBLOCK)


def rope_tables(offsets, head_dim):
    half_dim = head_dim // 2
    frequencies = jnp.exp(
        jnp.arange(half_dim, dtype=f32) * (-2.0 * math.log(THETA) / head_dim)
    )
    angles = offsets.astype(f32)[:, None] * frequencies[None, :]
    return (jnp.cos(angles)[:, None, :], jnp.sin(angles)[:, None, :])


def rotate(vectors, cosine, sine):
    half_dim = vectors.shape[-1] // 2
    front, back = vectors[..., :half_dim], vectors[..., half_dim:]
    return jnp.concatenate([front * cosine - back * sine, back * cosine + front * sine], axis=-1)


def silu_back(gate_part, up_part, d_hidden):
    sigmoid_gate = jax.nn.sigmoid(gate_part)
    d_gate = d_hidden * up_part * sigmoid_gate * (1.0 + gate_part * (1.0 - sigmoid_gate))
    d_up = d_hidden * gate_part * sigmoid_gate
    return d_gate, d_up


def dot(pattern, a, b):
    return jnp.einsum(pattern, a, b, preferred_element_type=f32)


def on_device(
    layer_input,
    doc_lengths,
    expert_ids,
    attn_gain,
    qkv_weight,
    qkv_bias,
    out_weight,
    ffn_gain,
    router_weight,
    shared_gate,
    shared_in,
    shared_out,
    expert_in,
    expert_out,
    cotangent,
):
    tok, width = layer_input.shape
    dp, tn = lax.axis_index("dp"), lax.axis_index("tensor")
    experts = router_weight.shape[1]
    head_dim = qkv_weight.shape[3]
    stream = tok * N_DP
    part_rows = tok // N_T
    score_scale = head_dim ** (-0.5)
    eff = expert_out.shape[1]

    def permute(x, bits):
        return lax.ppermute(x, "tensor", [(i, i ^ bits) for i in range(N_T)])

    pieces = range(GROUPS)
    all_in = [expert_in[0]] + [permute(expert_in[0], i) for i in pieces[1:]]
    all_out = [expert_out[0]] + [permute(expert_out[0], i) for i in pieces[1:]]

    hot = jnp.sum(
        (expert_ids[:, :, None] == jnp.arange(experts, dtype=jnp.int32)[None, None, :]).astype(f32),
        axis=1,
    )
    before = (jnp.arange(tok)[:, None] > jnp.arange(tok)[None, :]).astype(bf16)
    rank = dot("ts,se->te", before, hot.astype(bf16))
    place = jnp.where(hot > 0, rank, -1.0).astype(jnp.int32).T
    _, offset = route_plane()
    served = lax.dynamic_slice_in_dim(place, GROUPS * ((dp // 4) ^ offset), GROUPS, 0)
    places = (
        (served[:, None, :] == jnp.arange(SLOTS, dtype=jnp.int32)[None, :, None])
        .astype(bf16)
        .reshape(GROUPS * SLOTS, tok)
    )
    returned = lax.dynamic_index_in_dim(place.reshape(GROUPS, 4, tok), offset, 1, keepdims=False)
    places_back = (
        (returned[:, None, :] == jnp.arange(SLOTS, dtype=jnp.int32)[None, :, None])
        .astype(bf16)
        .reshape(GROUPS * SLOTS, tok)
    )
    by_group = (GROUPS, SLOTS, width)
    up_send = dot("rt,td->rd", places, cotangent).astype(bf16)

    local_index = dp * tok + jnp.arange(tok, dtype=jnp.int32)
    pair_index = (dp // 2) * (2 * tok) + jnp.arange(2 * tok, dtype=jnp.int32)
    every_index = jnp.arange(stream, dtype=jnp.int32)
    _, pos_local, _ = doc_layout(doc_lengths, local_index)
    seq_pair, _, blk_pair = doc_layout(doc_lengths, pair_index)
    seq_all, _, blk_all = doc_layout(doc_lengths, every_index)
    codes = jnp.broadcast_to((seq_all * CODE + blk_all)[:, None], (stream, 128))
    bounds = jnp.stack([seq_pair * CODE, seq_pair * CODE + blk_pair] + [seq_pair] * 6)
    cosine, sine = rope_tables(pos_local, head_dim)
    residual = layer_input.astype(f32)
    inv_first = lax.rsqrt(jnp.mean(residual * residual, axis=1, keepdims=True) + EPSILON)
    normed_one = (residual * inv_first * attn_gain).astype(bf16)
    projected = dot("td,dshe->tshe", normed_one, qkv_weight) + qkv_bias.astype(f32)[None]
    q_own = rotate(projected[:, 0], cosine, sine).astype(bf16).transpose(1, 0, 2)
    k_own = rotate(projected[:, 1], cosine, sine).astype(bf16).transpose(1, 0, 2)
    v_own = projected[:, 2].astype(bf16).transpose(1, 0, 2)
    keys, values, queries = gather_keys(k_own, v_own, q_own, 1)
    queries = queries.reshape(2 * tok, head_dim)

    pair_out, pair_wide, logs = attend(queries, keys, values, codes, bounds)
    heads_out = swap_cores(pair_out.reshape(2, tok, head_dim), 3)
    heads_out = jnp.concatenate([heads_out[0], heads_out[1]], axis=1)
    out_flat = out_weight.reshape(2 * head_dim, width)
    attn_part = dot("qf,fd->qd", heads_out, out_flat).astype(bf16)
    by_slice = (N_T, part_rows, width)
    normed_two, middle, stats_one = join_attn(
        attn_part.reshape(by_slice), layer_input.reshape(by_slice), ffn_gain.reshape(1, width), 4
    )
    normed_two = normed_two.reshape(tok, width)

    row_send = dot("rt,td->rd", places, normed_two).astype(bf16)
    exp_rows, up_rows = rows_out([row_send.reshape(by_group), up_send.reshape(by_group)], 5)
    exp_rows, up_rows = exp_rows.reshape(-1, width), up_rows.reshape(-1, width)

    gate_value = jax.nn.sigmoid(dot("td,d->t", normed_two, shared_gate))
    shared_gu = dot("td,dsf->tsf", normed_two, shared_in)
    shared_hidden = (jax.nn.silu(shared_gu[:, 0]) * shared_gu[:, 1]).astype(bf16)
    shared_part = dot("tf,fd->td", shared_hidden, shared_out)
    upstream = cotangent.astype(f32)
    d_shared = (gate_value[:, None] * upstream).astype(bf16)
    gate_partial = jnp.sum(upstream * shared_part, axis=1) * gate_value * (1.0 - gate_value)
    d_shared_hidden = dot("td,fd->tf", d_shared, shared_out)
    d_gate, d_up = silu_back(shared_gu[:, 0], shared_gu[:, 1], d_shared_hidden)
    d_shared_gu = jnp.stack([d_gate, d_up], axis=1).astype(bf16)
    shared_out_part = dot("td,tf->df", d_shared, shared_hidden).astype(bf16)
    shared_in_part = dot("td,tf->df", normed_two, d_shared_gu.reshape(tok, -1)).astype(bf16)
    shared_d_normed = (
        dot("tsf,dsf->td", d_shared_gu, shared_in)
        + gate_partial[:, None] * shared_gate.astype(f32)[None, :]
    )
    gate_vec_part = jnp.einsum(
        "t,td->d", gate_partial, normed_two.astype(f32), precision=lax.Precision.HIGHEST
    )

    w_in = jnp.concatenate(all_in, axis=2)
    w_out = jnp.concatenate(all_out, axis=0)
    row_logits = dot("rd,de->re", exp_rows, router_weight)
    row_probs = jax.nn.softmax(row_logits, axis=1)
    own_expert = (jnp.arange(experts, dtype=jnp.int32) == dp).astype(f32)[None, :]
    row_gate = jnp.sum(row_probs * own_expert, axis=1, keepdims=True)
    expert_gu = dot("rd,dsf->rsf", exp_rows, w_in)
    expert_hidden = (jax.nn.silu(expert_gu[:, 0]) * expert_gu[:, 1]).astype(bf16)
    expert_part = (row_gate * dot("rf,fd->rd", expert_hidden, w_out)).astype(bf16)

    raw_hidden = dot("rd,fd->rf", up_rows, w_out)
    d_gate_row = jnp.sum(expert_hidden.astype(f32) * raw_hidden, axis=1, keepdims=True)
    d_row_logits = (d_gate_row * row_gate * (own_expert - row_probs)).astype(bf16)
    d_gate, d_up = silu_back(expert_gu[:, 0], expert_gu[:, 1], row_gate * raw_hidden)
    d_expert_gu = jnp.stack([d_gate, d_up], axis=1).astype(bf16)
    d_rows = (
        dot("rsf,dsf->rd", d_expert_gu, w_in) + dot("re,de->rd", d_row_logits, router_weight)
    ).astype(bf16)
    router_part = dot("re,rd->ed", d_row_logits, exp_rows)
    gated_hidden = (expert_hidden.astype(f32) * row_gate).astype(bf16)

    def piece_grads(i):
        units = slice(i * eff, (i + 1) * eff)
        return (
            dot("rd,rsf->dsf", exp_rows, d_expert_gu[:, :, units]),
            dot("rf,rd->fd", gated_hidden[:, units], up_rows),
        )

    sent = [tuple(g.astype(bf16) for g in piece_grads(i)) for i in pieces[1:]]

    def sum_of(own, other):
        return (own.astype(f32) + other.astype(f32)).astype(bf16)

    by_chip = [
        g.reshape(8, 2, width // N_DP, -1) for g in (shared_in_part, shared_out_part)
    ]
    back_grads, back_out, *got = rows_back(
        [d_rows.reshape(by_group), expert_part.reshape(by_group)], by_chip, 6
    )
    core, z_index, x_index = dp % 2, dp // 4, (dp // 2) % 2

    def pick(x, index, axis=0):
        return lax.dynamic_index_in_dim(x, index, axis, keepdims=False)

    by_z = [
        sum_of(pick(own, core, 1), other).reshape(4, 2, width // N_DP, -1)
        for own, other in zip(by_chip, got)
    ]

    def combine(rows):
        return dot("rt,rd->td", places_back, rows.reshape(-1, width))

    d_normed_part = (shared_d_normed + combine(back_grads)).astype(bf16)
    d_attn, d_middle, stats_two, *got = join_ffn(
        d_normed_part.reshape(by_slice),
        cotangent.reshape(by_slice),
        middle,
        ffn_gain.reshape(1, width),
        by_z,
        7,
    )
    d_attn, sent = lax.optimization_barrier((d_attn, sent))
    received = [tuple(permute(g, i) for g in pair) for i, pair in zip(pieces[1:], sent)]
    by_x = [
        (pick(own, z_index).astype(f32) + sum(other[k].astype(f32) for k in (1, 2, 3))).astype(bf16)
        for own, other in zip(by_z, got)
    ]
    d_attn = d_attn.reshape(tok, width)
    moe_part = (gate_value[:, None] * shared_part + combine(back_out)).astype(bf16)

    outproj_part = dot("qd,qf->df", d_attn, heads_out).astype(bf16)
    d_heads = dot("qd,fd->qf", d_attn, out_flat).astype(bf16)
    d_heads = jnp.stack([d_heads[:, :head_dim], d_heads[:, head_dim:]])
    d_heads = swap_cores(d_heads, 8).reshape(2 * tok, head_dim)
    d_queries, d_keys, d_values = attend_back(
        queries, keys, values, codes, bounds, pair_wide, logs, d_heads
    )
    got_k, got_v, got_out_part, d_queries, *got = scatter_keys(
        d_keys.reshape(N_DP, tok, head_dim),
        d_values.reshape(N_DP, tok, head_dim),
        outproj_part.reshape(N_DP, width // N_DP, -1),
        d_queries.reshape(2, tok, head_dim),
        by_x,
        9,
    )
    got_k, received = lax.optimization_barrier((got_k, received))
    shared_in_grad, shared_out_grad = [
        pick(own, x_index).astype(f32) + other.astype(f32) for own, other in zip(by_x, got)
    ]
    outproj_grad = jnp.sum(got_out_part.astype(f32), axis=0)
    def summed(x):
        x = jnp.sum(x.astype(f32).reshape(8, 2, tok, head_dim), axis=0)
        return x[0], x[1]

    cosine, sine = cosine[:, 0], sine[:, 0]
    d_proj = jnp.concatenate(
        [rotate(d_queries[h].astype(f32), cosine, -sine) for h in range(2)]
        + [rotate(x, cosine, -sine) for x in summed(got_k)]
        + list(summed(got_v)),
        axis=1,
    ).astype(bf16)
    d_normed_one = dot("tf,df->td", d_proj, qkv_weight.reshape(width, -1)).astype(bf16)
    qkv_part = dot("td,tf->df", normed_one, d_proj).astype(bf16)
    bias_part = jnp.sum(d_proj.astype(f32), axis=0)

    def slices(row):
        return row.reshape(-1, N_DP, 128).transpose(1, 0, 2)

    three = jnp.sum(stats_one[:3], axis=1)
    pack = jnp.concatenate(
        [
            slices(router_part),
            slices(gate_vec_part),
            slices(stats_two[0]),
            jnp.broadcast_to(jnp.pad(three, (0, 125))[None, None], (N_DP, 1, 128)),
            jnp.pad(
                bias_part.reshape(6, N_DP, 8).transpose(1, 0, 2).reshape(N_DP, 1, 48),
                ((0, 0), (0, 4), (0, 80)),
            ),
        ],
        axis=1,
    )
    input_grad, output, got_qkv, over_dp, over_both = join_tail(
        d_normed_one.reshape(by_slice),
        moe_part.reshape(by_slice),
        layer_input.reshape(by_slice),
        middle,
        d_middle,
        attn_gain.reshape(1, width),
        qkv_part.reshape(N_DP, width // N_DP, -1),
        pack,
        10,
    )
    bias_grad = over_dp[19, :48].reshape(3, 2, 8)
    five = jnp.concatenate([over_both[18, :3], jnp.sum(over_both[21:23], axis=1)])
    rms_stats = jnp.sqrt(five / (stream * width))
    qkv_grad = jnp.sum(got_qkv.astype(f32), axis=0)

    expert_in_grad, expert_out_grad = piece_grads(0)
    for got_in, got_out in received:
        expert_in_grad = expert_in_grad + got_in.astype(f32)
        expert_out_grad = expert_out_grad + got_out.astype(f32)

    return (
        output.reshape(tok, width),
        input_grad.reshape(tok, width).astype(f32),
        qkv_grad.reshape(width // N_DP, 3, 2, head_dim),
        bias_grad,
        outproj_grad.T.reshape(2, head_dim, width // N_DP),
        over_both[23],
        over_both[17],
        over_both[:16].T,
        over_both[16],
        shared_in_grad.reshape(width // N_DP, 2, -1),
        shared_out_grad.T,
        expert_in_grad[None],
        expert_out_grad[None],
        rms_stats,
    )


def solution(mesh):
    in_specs = (
        P("dp", None),
        P(),
        P("dp", None),
        P(),
        P(None, None, "tensor", None),
        P(None, "tensor", None),
        P("tensor", None, None),
        P(),
        P(),
        P(),
        P(None, None, "tensor"),
        P("tensor", None),
        P("dp", None, None, "tensor"),
        P("dp", "tensor", None),
        P("dp", None),
    )
    out_specs = (
        P("dp", None),
        P("dp", None),
        P("dp", None, "tensor", None),
        P(None, "tensor", "dp"),
        P("tensor", None, "dp"),
        P("dp"),
        P("dp"),
        P("dp", None),
        P("dp"),
        P("dp", None, "tensor"),
        P("tensor", "dp"),
        P("dp", None, None, "tensor"),
        P("dp", "tensor", None),
        P(),
    )
    return jax.shard_map(
        on_device, mesh=mesh, in_specs=in_specs, out_specs=out_specs, check_vma=False
    )
```

time: 2270 us -> 634 us (0.28)
  waiting for transfers between devices: 1420 us -> 11.2 us
  Pallas kernels: 0 us -> 420 us
  blocking collectives: 336 us -> 0 us
  local copies, waits for them, and re-layouts: 200 us -> 45.9 us
  other arithmetic: 127 us -> 48.5 us
  matrix products: 146 us -> 81.4 us
    psum x5 -> x0, waiting for transfers between devices: 634 us -> none  [the longest x1 350 us: on_device(): lax.psum((d_normed_two, router_part, gate_vec_part), 'tensor')]
    reduce_scatter x7 -> x0, waiting for transfers between devices: 447 us -> none  [the longest x1 132 us: on_device(): lax.psum_scatter(shared_in_part, 'dp', scatter_dimension=0, tiled=True)]
    pallas_call x0 -> x11, Pallas kernels: none -> 420 us  [the longest x1 85.4 us: join_tail(): pl.pallas_call(kernel, out_shape=(struct(part.shape, bf16), struct(part.s...]
    all_to_all x2 -> x0, waiting for transfers between devices: 298 us -> none  [the longest x1 187 us: on_device(): lax.all_to_all(d_rows.reshape(data_size, capacity, model_width), 'dp', sp...]
    all_to_all x2 -> x0, blocking collectives: 261 us -> none  [the longest x1 168 us: on_device(): lax.all_to_all(send_grads.reshape(experts, capacity, model_width), 'dp',...]
    reshape x11 -> x5, local copies, waits for them, and re-layouts: 104 us -> 9.15 us  [the longest x1 8.05 us: on_device(): qkv_weight.reshape(width, -1)]
    dot_general x27 -> x30, matrix products: 132 us -> 74.3 us  [the longest x29 73.6 us: dot(): return jnp.einsum(pattern, a, b, preferred_element_type=f32)]
    unnamed x1 -> x0, blocking collectives: 54.2 us -> none
  transfers between devices with their start and end apart: 16 -> 12, of which waited for: 14 -> 1; matrix products, arithmetic and copies ran while one was open for 12% -> 13% of each run, Pallas kernels for 0% -> 36%
where the time goes in v2:
time: 634 us; the launch traced here: 628 us
  Pallas kernels  420 us (66%)
  matrix products  81.4 us (13%)
  other arithmetic  48.5 us (8%)
  local copies, waits for them, and re-layouts  45.9 us (7%)
  starting transfers between devices  18.4 us (3%)
  waiting for transfers between devices  11.2 us (2%)
    pallas_call x1, Pallas kernels, join_tail(): pl.pallas_call(kernel, out_shape=(struct(part.shape, bf16), struct(part.s...  85.4 us
    dot_general x29, matrix products, dot(): return jnp.einsum(pattern, a, b, preferred_element_type=f32)  73.6 us
    pallas_call x1, Pallas kernels, join_ffn(): pl.pallas_call(kernel, out_shape=(struct(part.shape, bf16), struct((rows,...  65.1 us
    pallas_call x1, Pallas kernels, scatter_keys(): pl.pallas_call(kernel, out_shape=(struct(dk.shape, bf16), struct(dv.shape...  57 us
    pallas_call x1, Pallas kernels, rows_out(): pl.pallas_call(kernel, out_shape=tuple((struct(x.shape, x.dtype) for x in...  50.5 us
    pallas_call x1, Pallas kernels, join_attn(): pl.pallas_call(kernel, out_shape=(struct(part.shape, bf16), struct((rows,...  46.5 us
    pallas_call x1, Pallas kernels, rows_back(): pl.pallas_call(kernel, out_shape=tuple((struct(x.shape, x.dtype) for x in...  40.7 us
    pallas_call x1, Pallas kernels, gather_keys(): pl.pallas_call(kernel, out_shape=(struct((N_DP * tok, size), bf16), struc...  39.9 us
  transfers between devices with their start and end apart: 12, of which 1 were waited for; matrix products, arithmetic and copies ran while one was open for 13% of the time, Pallas kernels for 36%

profile of v2, /device:TPU:1, one launch (start us, length us, event | category | flops | bytes accessed | tf_op | source)
XLA Modules:
  0.0 627.8 jit_solution(15596386017896144234)
XLA Ops:
  0.7 2.2 collective-permute-start.3
  2.9 2.6 collective-permute-start.4
  5.5 3.8 collective-permute-start.1
  9.4 1.7 fusion.10
  11.7 3.6 fusion.24
  18.2 1.3 multiply_cosine_fusion
  19.6 1.4 subtract_convert_fusion
  21.9 39.9 %gather_keys.1 = (bf16[5120,128]{1,0:T(8,128)(2,1)}, bf16[5120,128]{1,0:T(8,128)(2,1)}, bf16[2,320,128]{2,1,0:T(8,128)(2,1)}) custom-call(bf16[2,320,128]{2,1,0:T(8,128)(2,1)} %get-tuple-element.222.k_ref, bf16[2,320,128]{2,1,0:T(8,128)(2,1)} %fusion.83.v_ref, bf16[2,320,128]{2,1,0:T(8,128)(2,1)} %get-tuple-element.223.q_ref), custom_call_target="tpu_custom_call" | custom-call | bytes 123000000 | tf_op jit(solution)/shard_map/gather_keys/pallas_call | solution.py:445
  64.4 12.3 %attend.1 = (bf16[640,128]{1,0:T(8,128)(2,1)S(1)}, f32[640,128]{1,0:T(8,128)S(1)}, f32[8,640]{1,0:T(8,128)S(1)}) custom-call(bf16[640,128]{1,0:T(8,128)(2,1)S(1)} %bitcast.293, bf16[5120,128]{1,0:T(8,128)(2,1)S(1)} %copy-done.10, bf16[5120,128]{1,0:T(8,128)(2,1)S(1)} %copy-done.12, s32[5120,128]{1,0:T(8,128)S(1)} %broadcast_in_dim.54.code_ref, ...), custom_call_target="tpu_custom_call" | custom-call | bytes 36000000 | tf_op jit(solution)/shard_map/attend/pallas_call | solution.py:817
  77.5 3.6 swap_cores.2
  83.4 1.8 convolution_convert_fusion.6
  85.3 46.5 %join_attn.1 = (bf16[8,40,2048]{2,1,0:T(8,128)(2,1)S(1)}, f32[40,2048]{1,0:T(8,128)S(1)}, f32[8,2048]{1,0:T(8,128)S(1)}) custom-call(bf16[8,40,2048]{2,1,0:T(8,128)(2,1)S(1)} %bitcast.287, bf16[8,40,2048]{2,1,0:T(8,128)(2,1)S(1)} %bitcast.279, f32[1,2048]{1,0:T(1,128)S(1)} %bitcast.298), custom_call_target="tpu_custom_call" | custom-call | bytes 120000000 | tf_op jit(solution)/shard_map/join_attn/pallas_call | solution.py:562
  131.9 2.4 convolution_convert_fusion.4
  134.8 2.4 convolution_convert_fusion.3
  137.1 2.2 fusion.103
  139.4 2.5 fusion.44
  141.9 3.3 fusion.14
  145.2 50.5 %rows_out.1 = (bf16[4,112,2048]{2,1,0:T(8,128)(2,1)}, bf16[4,112,2048]{2,1,0:T(8,128)(2,1)}) custom-call(bf16[4,112,2048]{2,1,0:T(8,128)(2,1)} %bitcast.332, bf16[4,112,2048]{2,1,0:T(8,128)(2,1)} %bitcast.333), custom_call_target="tpu_custom_call" | custom-call | bytes 126000000 | tf_op jit(solution)/shard_map/rows_out/pallas_call | solution.py:494
  195.8 2.2 fusion.100
  198.4 4.4 convolution_convert_fusion.2
  203.0 1.4 collective-permute-start.2
  204.4 8.0 %reshape.495 = bf16[2048,768]{1,0:T(8,128)(2,1)} reshape(bf16[2048,3,2,128]{3,2,1,0:T(2,128)(2,1)} %param.19) | data formatting | bytes 6291456 | tf_op jit(solution)/shard_map/reshape | solution.py:1114
  214.1 4.7 copy.68
  220.0 5.2 convolution_convert_fusion
  225.2 3.5 fusion.42
  228.8 5.3 fusion.36
  235.3 1.5 convolution_convert_fusion.10
  236.8 1.5 convolution_convert_fusion.8
  238.4 1.5 convolution_convert_fusion.9
  240.9 1.4 fusion.48
  242.3 4.7 multiply_convert_fusion
  247.0 5.8 fusion.1
  252.8 40.7 %rows_back.1 = (bf16[4,112,2048]{2,1,0:T(8,128)(2,1)}, bf16[4,112,2048]{2,1,0:T(8,128)(2,1)}, bf16[8,128,1408]{2,1,0:T(8,128)(2,1)}, bf16[8,128,704]{2,1,0:T(8,128)(2,1)}) custom-call(bf16[4,112,2048]{2,1,0:T(8,128)(2,1)} %bitcast.331, bf16[4,112,2048]{2,1,0:T(8,128)(2,1)} %bitcast.330, bf16[8,2,128,1408]{3,2,1,0:T(8,128)(2,1)} %bitcast.319, ...), custom_call_target="tpu_custom_call" | custom-call | bytes 126000000 | tf_op jit(solution)/shard_map/rows_back/pallas_call | solution.py:531
  293.5 3.6 fusion.2
  297.2 4.1 fusion
  301.3 1.9 copy.70
  303.2 1.9 fusion.105
  307.3 1.9 fusion.106
  315.3 2.3 fusion.9
  317.6 65.1 %join_ffn.1 = (bf16[8,40,2048]{2,1,0:T(8,128)(2,1)S(1)}, f32[40,2048]{1,0:T(8,128)S(1)}, f32[8,2048]{1,0:T(8,128)S(1)}, bf16[4,2,128,1408]{3,2,1,0:T(8,128)(2,1)}, bf16[4,2,128,704]{3,2,1,0:T(8,128)(2,1)}) custom-call(bf16[8,40,2048]{2,1,0:T(8,128)(2,1)S(1)} %bitcast.292, bf16[8,40,2048]{2,1,0:T(8,128)(2,1)S(1)} %bitcast.280, ...), custom_call_target="tpu_custom_call" | custom-call | bytes 150000000 | tf_op jit(solution)/shard_map/join_ffn/pallas_call | solution.py:610
  382.8 1.7 convolution_convert_fusion.7
  385.1 2.2 add_convert_fusion.1
  387.4 2.5 add_convert_fusion
  390.6 3.6 swap_cores.3
  395.2 2.9 collective-permute-start.8
  400.3 15.2 %attend_back.1 = (bf16[640,128]{1,0:T(8,128)(2,1)S(1)}, bf16[5120,128]{1,0:T(8,128)(2,1)S(1)}, bf16[5120,128]{1,0:T(8,128)(2,1)S(1)}) custom-call(bf16[640,128]{1,0:T(8,128)(2,1)S(1)} %bitcast.294, bf16[5120,128]{1,0:T(8,128)(2,1)S(1)} %copy-done.11, bf16[5120,128]{1,0:T(8,128)(2,1)S(1)} %copy-done.13, s32[5120,128]{1,0:T(8,128)} %copy-done.2, ...), custom_call_target="tpu_custom_call" | custom-call | bytes 45000000 | tf_op jit(solution)/shard_map/attend_back/pallas_call | solution.py:856
  418.3 57.0 %scatter_keys.1 = (bf16[16,320,128]{2,1,0:T(8,128)(2,1)}, bf16[16,320,128]{2,1,0:T(8,128)(2,1)}, bf16[16,128,256]{2,1,0:T(8,128)(2,1)}, bf16[2,320,128]{2,1,0:T(...) custom-call(bf16[16,320,128]{2,1,0:T(8,128)(2,1)} %bitcast.290, bf16[16,320,128]{2,1,0:T(8,128)(2,1)} %bitcast.291, ...), custom_call_target="tpu_custom_call" | custom-call | bytes 150000000 | tf_op jit(solution)/shard_map/scatter_keys/pallas_call | solution.py:653
  476.4 1.6 reduce
  480.6 2.0 convert_add_fusion.2
  482.6 2.2 copy.75
  484.8 1.4 convert_reduce_fusion.2
  489.0 2.7 fusion.62
  491.7 3.3 collective-permute-start.9
  495.0 2.5 fusion.107
  499.5 11.2 %collective-permute-done.9 = bf16[176,2048]{1,0:T(8,128)(2,1)S(1)} collective-permute-done((bf16[176,2048]{1,0:T(8,128)(2,1)S(1)}, bf16[176,2048]{1,0:T(8,128)(2,1)S(1)}, u32[]{:S(2)}, u32[]{:S(2)}) %collective-permute-start.9) | collective-permute-done | bytes 720928 | tf_op jit(solution)/shard_map/ppermute | solution.py:930
  510.9 1.6 fusion.82
  512.6 1.9 concatenate.32
  515.7 4.6 convolution_convert_fusion.1
  521.2 3.3 convolution_convert_fusion.5
  524.5 1.8 concatenate.33.pack_ref
  526.3 85.4 %join_tail.1 = (bf16[8,40,2048]{2,1,0:T(8,128)(2,1)S(1)}, bf16[8,40,2048]{2,1,0:T(8,128)(2,1)S(1)}, bf16[16,128,768]{2,1,0:T(8,128)(2,1)}, f32[24,128]{1,0:T(8,128)S(1)}, f32[24,128]{1,0:T(8,128)S(1)}) custom-call(bf16[8,40,2048]{2,1,0:T(8,128)(2,1)S(1)} %bitcast.288, bf16[8,40,2048]{2,1,0:T(8,128)(2,1)S(1)} %bitcast.286, bf16[8,40,2048]{2,1,0:T(8,128)(2,1)} %bitcast.278, ...), custom_call_target="tpu_custom_call" | custom-call | bytes 180000000 | tf_op jit(solution)/shard_map/join_tail/pallas_call | solution.py:744
  613.1 1.9 bitcast_convert_fusion
  618.6 3.0 add_bitcast_fusion.1
  621.6 4.9 add_bitcast_fusion
  (290 shorter events, 48.0 us)
Async XLA Ops:
  0.6 138.8 %copy-start = (bf16[704,2048]{1,0:T(8,128)(2,1)S(1)}, bf16[704,2048]{1,0:T(8,128)(2,1)}, u32[]{:S(2)}) copy-start(bf16[704,2048]{1,0:T(8,128)(2,1)} %param.26) | copy-start | bytes 8650756
  0.7 228.1 %collective-permute-start.3 = (bf16[2048,2,176]{0,2,1:T(8,128)(2,1)}, bf16[2048,2,176]{0,2,1:T(8,128)(2,1)}, u32[]{:S(2)}, u32[]{:S(2)}) collective-permute-start(bf16[2048,2,176]{0,2,1:T(8,128)(2,1)} %bitcast.359), channel_id=1, source_target_pairs={{0,1},{1,0},{2,3},{3,2},{4,5},{5,4},{6,7},{7,6},{8,9},{9,8},{10,11... | collective-permute-start | bytes 4325384 | tf_op jit(solution)/shard_map/ppermute | solution.py:930
  2.9 225.9 %collective-permute-start.4 = (bf16[2048,2,176]{0,2,1:T(8,128)(2,1)}, bf16[2048,2,176]{0,2,1:T(8,128)(2,1)}, u32[]{:S(2)}, u32[]{:S(2)}) collective-permute-start(bf16[2048,2,176]{0,2,1:T(8,128)(2,1)} %bitcast.360), channel_id=1, source_target_pairs={{0,2},{1,3},{2,0},{3,1},{4,6},{5,7},{6,4},{7,5},{8,10},{9,11},{10,... | collective-permute-start | bytes 4325384 | tf_op jit(solution)/shard_map/ppermute | solution.py:930
  5.5 223.3 %collective-permute-start.5 = (bf16[2048,2,176]{0,2,1:T(8,128)(2,1)}, bf16[2048,2,176]{0,2,1:T(8,128)(2,1)}, u32[]{:S(2)}, u32[]{:S(2)}) collective-permute-start(bf16[2048,2,176]{0,2,1:T(8,128)(2,1)} %bitcast.361), channel_id=1, source_target_pairs={{0,3},{1,2},{2,1},{3,0},{4,7},{5,6},{6,5},{7,4},{8,11},{9,10},{10,... | collective-permute-start | bytes 4325384 | tf_op jit(solution)/shard_map/ppermute | solution.py:930
  5.5 197.5 %collective-permute-start = (bf16[176,2048]{1,0:T(8,128)(2,1)}, bf16[176,2048]{1,0:T(8,128)(2,1)}, u32[]{:S(2)}, u32[]{:S(2)}) collective-permute-start(bf16[176,2048]{1,0:T(8,128)(2,1)} %bitcast.33), channel_id=1, source_target_pairs={{0,1},{1,0},{2,3},{3,2},{4,5},{5,4},{6,7},{7,6},{8,9},{9,8},{10,11... | collective-permute-start | bytes 2162696 | tf_op jit(solution)/shard_map/ppermute | solution.py:930
  5.5 219.7 %collective-permute-start.1 = (bf16[176,2048]{1,0:T(8,128)(2,1)}, bf16[176,2048]{1,0:T(8,128)(2,1)}, u32[]{:S(2)}, u32[]{:S(2)}) collective-permute-start(bf16[176,2048]{1,0:T(8,128)(2,1)} %bitcast.33), channel_id=1, source_target_pairs={{0,2},{1,3},{2,0},{3,1},{4,6},{5,7},{6,4},{7,5},{8,10},{9,11},{10,... | collective-permute-start | bytes 2162696 | tf_op jit(solution)/shard_map/ppermute | solution.py:930
  9.4 8.9 %copy-start.79 = (f32[64]{0:T(128)}, f32[64]{0:T(128)S(1)}, u32[]{:S(2)}) copy-start(f32[64]{0:T(128)S(1)} %multiply_exponential_fusion) | copy-start | bytes 772
  11.0 4.3 copy-start.81
  11.7 5.6 copy-start.86
  19.6 43.0 %copy-start.23 = (s32[8,640]{1,0:T(8,128)}, s32[8,640]{1,0:T(8,128)S(1)}, u32[]{:S(2)}) copy-start(s32[8,640]{1,0:T(8,128)S(1)} %stack.44.bound_ref) | copy-start | bytes 61444
  64.4 12.4 %copy-start.2 = (s32[5120,128]{1,0:T(8,128)}, s32[5120,128]{1,0:T(8,128)S(1)}, u32[]{:S(2)}) copy-start(s32[5120,128]{1,0:T(8,128)S(1)} %broadcast_in_dim.54.code_ref) | copy-start | bytes 7864324
  64.4 17.7 %copy-start.76 = (s32[320,4]{0,1:T(4,128)S(1)}, s32[320,4]{0,1:T(4,128)}, u32[]{:S(2)}) copy-start(s32[320,4]{0,1:T(4,128)} %param.17) | copy-start | bytes 15364
  64.4 18.9 %copy-start.70 = (bf16[2048]{0:T(1024)(128)(2,1)S(1)}, bf16[2048]{0:T(1024)(128)(2,1)}, u32[]{:S(2)}) copy-start(bf16[2048]{0:T(1024)(128)(2,1)} %param.24) | copy-start | bytes 12292
  77.5 7.8 %copy-start.28 = (f32[8,640]{1,0:T(8,128)}, f32[8,640]{1,0:T(8,128)S(1)}, u32[]{:S(2)}) copy-start(f32[8,640]{1,0:T(8,128)S(1)} %get-tuple-element.66.log_ref) | copy-start | bytes 61444
  77.5 7.8 %copy-start.27 = (f32[2048]{0:T(1024)S(1)}, f32[2048]{0:T(1024)}, u32[]{:S(2)}) copy-start(f32[2048]{0:T(1024)} %param.22) | copy-start | bytes 24580
  85.2 46.6 %copy-start.67 = (pred[4,112,320]{2,1,0:T(8,128)(4,1)S(1)}, pred[4,112,320]{2,1,0:T(8,128)(4,1)}, u32[]{:S(2)}) copy-start(pred[4,112,320]{2,1,0:T(8,128)(4,1)} %iota_compare_fusion) | copy-start | bytes 430084
  85.3 51.8 %slice-start = ((s8[5767168]{0:T(1024)(128)(4,1)}), s8[4194304]{0:T(1024)(128)(4,1)S(1)}, s32[]{:S(2)}) async-start(s8[5767168]{0:T(1024)(128)(4,1)} %bitcast.355), calls=%async_computation | async-start | bytes 8388608
  131.9 5.3 copy-start.8
  131.9 5.3 slice-start.1
  134.8 4.7 copy-start.73
  141.9 3.3 copy-start.56
  145.2 50.6 %copy-start.65 = (bf16[2048,16]{0,1:T(8,128)(2,1)S(1)}, bf16[2048,16]{0,1:T(8,128)(2,1)}, u32[]{:S(2)}) copy-start(bf16[2048,16]{0,1:T(8,128)(2,1)} %param.23) | copy-start | bytes 196612
  198.4 4.4 copy-start.31
  198.4 5.9 copy-start.71
  203.0 22.2 %collective-permute-start.2 = (bf16[176,2048]{1,0:T(8,128)(2,1)}, bf16[176,2048]{1,0:T(8,128)(2,1)}, u32[]{:S(2)}, u32[]{:S(2)}) collective-permute-start(bf16[176,2048]{1,0:T(8,128)(2,1)} %bitcast.33), channel_id=1, source_target_pairs={{0,3},{1,2},{2,1},{3,0},{4,7},{5,6},{6,5},{7,4},{8,11},{9,10},{10,... | collective-permute-start | bytes 2162696 | tf_op jit(solution)/shard_map/ppermute | solution.py:930
  214.1 5.3 copy-start.9
  220.0 5.2 copy-start.36
  225.2 3.6 copy-start.34
  225.2 3.6 copy-start.85
  293.5 3.7 copy-start.44
  310.7 4.4 slice-start.2
  311.7 3.4 slice-start.3
  317.6 65.2 %copy-start.62 = (bf16[320,128]{1,0:T(8,128)(2,1)S(1)}, bf16[320,128]{1,0:T(8,128)(2,1)}, u32[]{:S(2)}) copy-start(bf16[320,128]{1,0:T(8,128)(2,1)} %copy-done.61) | copy-start | bytes 245764
  317.6 65.2 %copy-start.64 = (bf16[320,128]{1,0:T(8,128)(2,1)S(1)}, bf16[320,128]{1,0:T(8,128)(2,1)}, u32[]{:S(2)}) copy-start(bf16[320,128]{1,0:T(8,128)(2,1)} %copy-done.63) | copy-start | bytes 245764
  387.4 11.9 %copy-start.11 = (bf16[5120,128]{1,0:T(8,128)(2,1)S(1)}, bf16[5120,128]{1,0:T(8,128)(2,1)}, u32[]{:S(2)}) copy-start(bf16[5120,128]{1,0:T(8,128)(2,1)} %get-tuple-element.63.k_ref) | copy-start | bytes 3932164
  387.4 11.9 %copy-start.13 = (bf16[5120,128]{1,0:T(8,128)(2,1)S(1)}, bf16[5120,128]{1,0:T(8,128)(2,1)}, u32[]{:S(2)}) copy-start(bf16[5120,128]{1,0:T(8,128)(2,1)} %get-tuple-element.64.v_ref) | copy-start | bytes 3932164
  387.4 12.0 %copy-start.19 = (bf16[2,320,128]{2,1,0:T(8,128)(2,1)S(1)}, bf16[2,320,128]{2,1,0:T(8,128)(2,1)}, u32[]{:S(2)}) copy-start(bf16[2,320,128]{2,1,0:T(8,128)(2,1)} %get-tuple-element.62) | copy-start | bytes 491524
  387.4 12.0 %copy-start.24 = (s32[8,640]{1,0:T(8,128)S(1)}, s32[8,640]{1,0:T(8,128)}, u32[]{:S(2)}) copy-start(s32[8,640]{1,0:T(8,128)} %copy-done.23) | copy-start | bytes 61444
  387.4 12.0 %copy-start.29 = (f32[8,640]{1,0:T(8,128)S(1)}, f32[8,640]{1,0:T(8,128)}, u32[]{:S(2)}) copy-start(f32[8,640]{1,0:T(8,128)} %copy-done.28) | copy-start | bytes 61444
  394.2 116.5 %collective-permute-start.10 = (bf16[2048,2,176]{0,2,1:T(8,128)(2,1)}, bf16[2048,2,176]{0,2,1:T(8,128)(2,1)}, u32[]{:S(2)}, u32[]{:S(2)}) collective-permute-start(bf16[2048,2,176]{0,2,1:T(8,128)(2,1)} %convert_element_type.319), channel_id=1, source_target_pairs={{0,3},{1,2},{2,1},{3,0},{4,7},{5,6},{6,5},{7,4},{8,11},{9,10},{10,... | collective-permute-start | bytes 4325384 | tf_op jit(solution)/shard_map/ppermute | solution.py:930
  395.2 115.4 %collective-permute-start.6 = (bf16[2048,2,176]{0,2,1:T(8,128)(2,1)}, bf16[2048,2,176]{0,2,1:T(8,128)(2,1)}, u32[]{:S(2)}, u32[]{:S(2)}) collective-permute-start(bf16[2048,2,176]{0,2,1:T(8,128)(2,1)} %convert_element_type.314), channel_id=1, source_target_pairs={{0,1},{1,0},{2,3},{3,2},{4,5},{5,4},{6,7},{7,6},{8,9},{9,8},{10,11... | collective-permute-start | bytes 4325384 | tf_op jit(solution)/shard_map/ppermute | solution.py:930
  395.2 115.4 %collective-permute-start.8 = (bf16[2048,2,176]{0,2,1:T(8,128)(2,1)}, bf16[2048,2,176]{0,2,1:T(8,128)(2,1)}, u32[]{:S(2)}, u32[]{:S(2)}) collective-permute-start(bf16[2048,2,176]{0,2,1:T(8,128)(2,1)} %convert_element_type.317), channel_id=1, source_target_pairs={{0,2},{1,3},{2,0},{3,1},{4,6},{5,7},{6,4},{7,5},{8,10},{9,11},{10,... | collective-permute-start | bytes 4325384 | tf_op jit(solution)/shard_map/ppermute | solution.py:930
  398.1 93.6 %collective-permute-start.11 = (bf16[176,2048]{1,0:T(8,128)(2,1)}, bf16[176,2048]{1,0:T(8,128)(2,1)}, u32[]{:S(2)}, u32[]{:S(2)}) collective-permute-start(bf16[176,2048]{1,0:T(8,128)(2,1)} %convolution_convert_fusion.8), channel_id=1, source_target_pairs={{0,3},{1,2},{2,1},{3,0},{4,7},{5,6},{6,5},{7,4},{8,11},{9,10},{10,... | collective-permute-start | bytes 2162696 | tf_op jit(solution)/shard_map/ppermute | solution.py:930
  399.1 100.4 %collective-permute-start.7 = (bf16[176,2048]{1,0:T(8,128)(2,1)}, bf16[176,2048]{1,0:T(8,128)(2,1)}, u32[]{:S(2)}, u32[]{:S(2)}) collective-permute-start(bf16[176,2048]{1,0:T(8,128)(2,1)} %convolution_convert_fusion.10), channel_id=1, source_target_pairs={{0,1},{1,0},{2,3},{3,2},{4,5},{5,4},{6,7},{7,6},{8,9},{9,8},{10,11... | collective-permute-start | bytes 2162696 | tf_op jit(solution)/shard_map/ppermute | solution.py:930
  475.3 3.4 copy-start.46
  475.3 4.3 copy-start.45
  475.3 4.3 copy-start.66
  476.4 4.2 copy-start.41
  480.5 7.4 %copy-start.35 = (bf16[4,112,2048]{2,1,0:T(8,128)(2,1)S(1)}, bf16[4,112,2048]{2,1,0:T(8,128)(2,1)}, u32[]{:S(2)}) copy-start(bf16[4,112,2048]{2,1,0:T(8,128)(2,1)} %get-tuple-element.69) | copy-start | bytes 5505028
  480.6 7.4 %copy-start.78 = (f32[16]{0:T(128)S(1)}, f32[16]{0:T(128)}, u32[]{:S(2)}) copy-start(f32[16]{0:T(128)} %compare_convert_fusion) | copy-start | bytes 196
  489.0 6.0 copy-start.49
  491.7 18.9 %collective-permute-start.9 = (bf16[176,2048]{1,0:T(8,128)(2,1)S(1)}, bf16[176,2048]{1,0:T(8,128)(2,1)S(1)}, u32[]{:S(2)}, u32[]{:S(2)}) collective-permute-start(bf16[176,2048]{1,0:T(8,128)(2,1)S(1)} %copy-done.55), channel_id=1, source_target_pairs={{0,2},{1,3},{2,0},{3,1},{4,6},{5,7},{6,4},{7,5},{8,10},{9,11},{10,... | collective-permute-start | bytes 2162696 | tf_op jit(solution)/shard_map/ppermute | solution.py:930
  495.0 3.3 copy-start.47
  495.0 3.3 copy-start.75
  498.3 12.4 %copy-start.50 = (bf16[16,320,128]{2,1,0:T(8,128)(2,1)S(1)}, bf16[16,320,128]{2,1,0:T(8,128)(2,1)}, u32[]{:S(2)}) copy-start(bf16[16,320,128]{2,1,0:T(8,128)(2,1)} %get-tuple-element.90) | copy-start | bytes 3932164
  499.4 11.5 %copy-start.80 = (f32[64]{0:T(128)S(1)}, f32[64]{0:T(128)}, u32[]{:S(2)}) copy-start(f32[64]{0:T(128)} %copy-done.79) | copy-start | bytes 772
  510.9 4.7 copy-start.4
  510.9 4.7 copy-start.32
  510.9 4.7 copy-start.82
  521.2 3.3 copy-start.83
  521.2 5.1 copy-start.22
  611.7 3.3 copy-start.14
  621.6 4.9 copy-start.15
  621.6 5.9 copy-start.1
  (39 other events, 84.8 us)

commit v3 on v2

--- a/solution.py
+++ b/solution.py
@@ -57,6 +57,14 @@
     return pltpu.CompilerParams(
         collective_id=number, has_side_effects=True, vmem_limit_bytes=limit
     )
+
+
+NT = (((1,), (1,)), ((), ()))
+TN = (((0,), (0,)), ((), ()))
+
+
+def mm(a, b, dims=(((1,), (0,)), ((), ()))):
+    return lax.dot_general(a, b, dims, preferred_element_type=f32)
 
 
 GROUPS = 4
@@ -477,68 +485,223 @@
     )(x)
 
 
-def rows_out(xs, number):
+def sigmoid(x):
+    return 1.0 / (1.0 + jnp.exp(-x))
+
+
+TILE = 176
+
+
+def shared_expert(x_ref, up_ref, in_ref, out_ref, vec_ref, part_ref, d_ref, grads_ref, row_ref, low_ref):
+    hidden = out_ref.shape[0]
+    x = x_ref[...]
+    vec = vec_ref[...]
+    gate = sigmoid(jnp.sum(x.astype(f32) * vec, axis=1, keepdims=True))
+    low_ref[...] = (gate * up_ref[...].astype(f32)).astype(bf16)
+    part_ref[...] = jnp.zeros_like(part_ref)
+    d_ref[...] = jnp.zeros_like(d_ref)
+
+    def tile(i, carry):
+        rows = [pl.ds(pl.multiple_of(i * TILE + k * hidden, 16), TILE) for k in range(3)]
+        w_gate, w_up, w_out = in_ref[rows[0]], in_ref[rows[1]], out_ref[rows[0]]
+        x, d_out = x_ref[...], low_ref[...]
+        gate_part = mm(w_gate, x, NT)
+        up_part = mm(w_up, x, NT)
+        sig = sigmoid(gate_part)
+        act = gate_part * sig
+        unit = (act * up_part).astype(bf16)
+        d_unit = mm(w_out, d_out, NT)
+        d_gate = (d_unit * up_part * sig * (1.0 + gate_part * (1.0 - sig))).astype(bf16)
+        d_up = (d_unit * act).astype(bf16)
+
+        def block(j, carry):
+            cols = pl.ds(pl.multiple_of(j * 256, 256), 256)
+            xs, ds = x_ref[:, cols], low_ref[:, cols]
+            part_ref[:, cols] += mm(unit, out_ref[rows[0], cols], TN)
+            d_ref[:, cols] += mm(d_gate, in_ref[rows[0], cols], TN) + mm(d_up, in_ref[rows[1], cols], TN)
+            for k, grad in enumerate((mm(d_gate, xs), mm(d_up, xs), mm(unit, ds))):
+                grad = grad.astype(bf16)
+                grads_ref[j, 0, rows[k]] = grad[:, :128]
+                grads_ref[j, 1, rows[k]] = grad[:, 128:]
+            return carry
+
+        return lax.fori_loop(0, x.shape[1] // 256, block, carry)
+
+    lax.fori_loop(0, hidden // TILE, tile, 0)
+    total = part_ref[...]
+    d_logit = jnp.sum(up_ref[...].astype(f32) * total, axis=1, keepdims=True) * gate * (1.0 - gate)
+    part_ref[...] = gate * total
+    d_ref[...] += d_logit * vec
+    row_ref[...] = column_sum(d_logit * x_ref[...].astype(f32))
+
+
+def rows_out(xs, tokens, upstream, w_in, w_out, vec, number):
     count = len(xs)
+    tok, width = tokens.shape
+    hidden = w_out.shape[0]
 
     def kernel(*refs):
-        rows = [
-            Rows(refs[i], refs[count + i], *refs[2 * count + 3 * i : 2 * count + 3 * i + 3])
-            for i in range(count)
-        ]
+        n_in, n_out = count + 5, count + 4
+        outs = refs[n_in : n_in + n_out]
+        low = refs[n_in + n_out]
+        scratch = refs[n_in + n_out + 1 :]
+        rows = [Rows(refs[i], outs[i], *scratch[3 * i : 3 * i + 3]) for i in range(count)]
         greet([], rows[0])
         for one in rows:
             one.start()
+        shared_expert(*refs[count:n_in], *outs[count:], low)
         for one in rows:
             one.wait()
 
     return pl.pallas_call(
         kernel,
-        out_shape=tuple(struct(x.shape, x.dtype) for x in xs),
-        in_specs=[HBM] * count,
-        out_specs=(HBM,) * count,
-        scratch_shapes=ROW_SEMS * count,
-        compiler_params=comm_params(number),
+        out_shape=tuple(struct(x.shape, x.dtype) for x in xs)
+        + (
+            struct((tok, width), f32),
+            struct((tok, width), f32),
+            struct((8, 2, 3 * hidden, 128), bf16),
+            struct((1, width), f32),
+        ),
+        in_specs=[HBM] * count + [VMEM] * 5,
+        out_specs=(HBM,) * count + (VMEM,) * 4,
+        scratch_shapes=[pltpu.VMEM((tok, width), bf16)] + ROW_SEMS * count,
+        compiler_params=comm_params(number, LIMIT),
         name="rows_out",
-        cost_estimate=cost(42),
-    )(*xs)
-
-
-def rows_back(xs, weights, number):
-    count, n = len(xs), len(xs) + len(weights)
+        cost_estimate=cost(45),
+    )(*xs, tokens, upstream, w_in, w_out, vec)
+
+
+def routed_expert(x, up, weights, router, own):
+    rows, width = x.shape
+    units = weights[0].shape[0] // 3
+
+    def kernel(x_ref, up_ref, w0, w1, w2, w3, router_ref, own_ref, *refs):
+        out_ref, d_ref, dgu_ref, unit_ref, router_grad_ref, w_ref, out_acc, d_acc, sem = refs
+        loads = [
+            pltpu.make_async_copy(w, w_ref.at[i], sem.at[i]) for i, w in enumerate((w0, w1, w2, w3))
+        ]
+        for load in loads:
+            load.start()
+        own = own_ref[:, 0:1]
+        logits = mm(router_ref[...], x_ref[...], NT)
+        terms = jnp.exp(logits - jnp.max(logits, axis=0, keepdims=True))
+        probs = terms / jnp.sum(terms, axis=0, keepdims=True)
+        gate = jnp.sum(probs * own, axis=0, keepdims=True)
+        out_acc[...] = jnp.zeros_like(out_acc)
+        d_acc[...] = jnp.zeros_like(d_acc)
+        for load in loads:
+            load.wait()
+
+        def piece(i, d_gate_row):
+            w = w_ref.at[i]
+            gate_part = mm(w[0:units], x_ref[...], NT)
+            up_part = mm(w[units : 2 * units], x_ref[...], NT)
+            raw = mm(w[2 * units : 3 * units], up_ref[...], NT)
+            sig = sigmoid(gate_part)
+            act = gate_part * sig
+            unit = (act * up_part).astype(bf16).astype(f32)
+            d_unit = gate * raw
+            gated = (unit * gate).astype(bf16)
+            d_gate = (d_unit * up_part * sig * (1.0 + gate_part * (1.0 - sig))).astype(bf16)
+            d_up = (d_unit * act).astype(bf16)
+            unit_ref[i] = gated
+            dgu_ref[i, 0:units] = d_gate
+            dgu_ref[i, units : 2 * units] = d_up
+
+            def block(j, carry):
+                cols = pl.ds(pl.multiple_of(j * 512, 512), 512)
+                out_acc[:, cols] += mm(gated, w_ref[i, 2 * units : 3 * units, cols], TN)
+                d_acc[:, cols] += mm(d_gate, w_ref[i, 0:units, cols], TN) + mm(
+                    d_up, w_ref[i, units : 2 * units, cols], TN
+                )
+                return carry
+
+            lax.fori_loop(0, width // 512, block, 0)
+            return d_gate_row + jnp.sum(unit * raw, axis=0, keepdims=True)
+
+        d_gate_row = lax.fori_loop(0, GROUPS, piece, jnp.zeros((1, rows), f32))
+        d_logits = (d_gate_row * gate * (own - probs)).astype(bf16)
+        router_grad_ref[...] = mm(d_logits, x_ref[...])
+        out_ref[...] = out_acc[...].astype(bf16)
+        d_ref[...] = (d_acc[...] + mm(d_logits, router_ref[...], TN)).astype(bf16)
+
+    return pl.pallas_call(
+        kernel,
+        out_shape=(
+            struct((rows, width), bf16),
+            struct((rows, width), bf16),
+            struct((GROUPS, 2 * units, rows), bf16),
+            struct((GROUPS, units, rows), bf16),
+            struct((router.shape[0], width), f32),
+        ),
+        in_specs=[VMEM] * 2 + [HBM] * GROUPS + [VMEM] * 2,
+        out_specs=(VMEM,) * 5,
+        scratch_shapes=[
+            pltpu.VMEM((GROUPS, 3 * units, width), bf16),
+            pltpu.VMEM((rows, width), f32),
+            pltpu.VMEM((rows, width), f32),
+            dma(GROUPS),
+        ],
+        compiler_params=pltpu.CompilerParams(vmem_limit_bytes=LIMIT),
+        name="routed_expert",
+        cost_estimate=cost(22),
+    )(x, up, *weights, router, own)
+
+
+def rows_back(xs, shared, d_gu, units, x, up, number):
+    count = len(xs)
+    n_hidden, width = units.shape[1], x.shape[1]
 
     def kernel(*refs):
         d = lax.axis_index("dp")
-        scratch = refs[2 * n :]
-        rows = [
-            Rows(refs[i], refs[n + i], *scratch[3 * i : 3 * i + 3], back=True) for i in range(count)
-        ]
+        n_in, n_out = count + 5, count + 3
+        shared_ref, d_gu_ref, units_ref, x_ref, up_ref = refs[count:n_in]
+        outs = refs[n_in : n_in + n_out]
+        got_ref, mine_ref, others_ref = outs[count:]
+        scratch = refs[n_in + n_out :]
+        rows = [Rows(refs[i], outs[i], *scratch[3 * i : 3 * i + 3], back=True) for i in range(count)]
         greet([{"dp": d ^ 1}], rows[0])
-        sides = Sends(
+        side = Sends(
             [
-                (refs[i].at[chip, 1 - lax.rem(d, 2)], refs[n + i].at[chip], {"dp": d ^ 1})
-                for i in range(count, n)
+                (shared_ref.at[chip, 1 - lax.rem(d, 2)], got_ref.at[chip], {"dp": d ^ 1})
                 for chip in range(8)
             ],
             *scratch[3 * count :],
         )
         for one in rows:
             one.start()
-        sides.start()
+        side.start()
+
+        def block(j, carry):
+            cols = pl.ds(pl.multiple_of(j * 256, 256), 256)
+            xs, ups = x_ref[:, cols], up_ref[:, cols]
+            mine_ref[0 : 2 * n_hidden, cols] = mm(d_gu_ref[0], xs)
+            mine_ref[2 * n_hidden :, cols] = mm(units_ref[0], ups)
+            for i in range(1, GROUPS):
+                others_ref[i - 1, 0 : 2 * n_hidden, cols] = mm(d_gu_ref[i], xs).astype(bf16)
+                others_ref[i - 1, 2 * n_hidden :, cols] = mm(units_ref[i], ups).astype(bf16)
+            return carry
+
+        lax.fori_loop(0, width // 256, block, 0)
         for one in rows:
             one.wait()
-        sides.wait()
+        side.wait()
 
     return pl.pallas_call(
         kernel,
-        out_shape=tuple(struct(x.shape, x.dtype) for x in xs)
-        + tuple(struct((w.shape[0],) + w.shape[2:], w.dtype) for w in weights),
-        in_specs=[HBM] * n,
-        out_specs=(HBM,) * n,
-        scratch_shapes=ROW_SEMS * count + sems(8 * len(weights), 8 * len(weights)),
-        compiler_params=comm_params(number),
+        out_shape=tuple(struct(r.shape, r.dtype) for r in xs)
+        + (
+            struct((8,) + shared.shape[2:], bf16),
+            struct((3 * n_hidden, width), f32),
+            struct((GROUPS - 1, 3 * n_hidden, width), bf16),
+        ),
+        in_specs=[HBM] * (count + 1) + [VMEM] * 4,
+        out_specs=(HBM,) * (count + 1) + (VMEM,) * 2,
+        scratch_shapes=ROW_SEMS * count + sems(8, 8),
+        compiler_params=comm_params(number, LIMIT),
         name="rows_back",
-        cost_estimate=cost(42),
-    )(*xs, *weights)
+        cost_estimate=cost(50),
+    )(*xs, shared, d_gu, units, x, up)
 
 
 def join_attn(part, layer_input, gain, number):
@@ -571,26 +734,21 @@
     )(part, layer_input, gain)
 
 
-def join_ffn(part, cotangent, middle, gain, weights, number):
+def join_ffn(part, moe_part, cotangent, middle, gain, weights, number):
     _, rows, width = part.shape
-    n = len(weights)
-
-    def kernel(part_ref, up_ref, middle_ref, gain_ref, *refs):
-        w_refs, (full_ref, d_ref, sums_ref), got_refs = refs[:n], refs[n : n + 3], refs[n + 3 : 2 * n + 3]
-        scratch = refs[2 * n + 3 :]
+
+    def kernel(part_ref, moe_ref, up_ref, middle_ref, gain_ref, w_ref, full_ref, out_ref, d_ref, sums_ref, got_ref, *scratch):
         d, z, _, _ = coordinates()
         greet(tensor_peers() + [{"dp": d ^ (4 * k)} for k in (1, 2, 3)])
         scatter, gather = direct_parts(part_ref, full_ref, scratch[:N_DIRECT])
         scatter.start()
-        sides = Sends(
-            [
-                (w_ref.at[z ^ k], got_ref.at[k], {"dp": d ^ (4 * k)})
-                for k in (1, 3, 2)
-                for w_ref, got_ref in zip(w_refs, got_refs)
-            ],
-            *scratch[N_DIRECT:],
+        side = Sends(
+            [(w_ref.at[z ^ k], got_ref.at[k], {"dp": d ^ (4 * k)}) for k in (1, 3, 2)],
+            *scratch[2 * N_DIRECT :],
         )
-        sides.start()
+        side.start()
+        scatter_moe, gather_moe = direct_parts(moe_ref, out_ref, scratch[N_DIRECT : 2 * N_DIRECT])
+        scatter_moe.start()
         middle = middle_ref[...]
         inv = second_moment(middle)
         d_normed = scatter.total()
@@ -603,25 +761,33 @@
         gather.start(d_middle)
         d_ref[...] = d_middle
         sums_ref[0:1] = column_sum(d_normed * middle * inv)
+        moe_out = scatter_moe.total()
+        output = middle_ref[...] + moe_out
+        gather_moe.start(output)
+        sums_ref[1:2] = column_sum(moe_out * moe_out)
+        sums_ref[2:3] = column_sum(output * output)
         scatter.wait_send()
+        scatter_moe.wait_send()
         gather.wait()
-        sides.wait()
+        gather_moe.wait()
+        side.wait()
 
     return pl.pallas_call(
         kernel,
         out_shape=(
             struct(part.shape, bf16),
+            struct(part.shape, bf16),
             struct((rows, width), f32),
             struct((8, width), f32),
-        )
-        + tuple(struct(w.shape, w.dtype) for w in weights),
-        in_specs=[VMEM] * 4 + [HBM] * n,
-        out_specs=(HBM, VMEM, VMEM) + (HBM,) * n,
-        scratch_shapes=direct_scratch(rows, width) + sems(3 * n, 3 * n),
+            struct(weights.shape, weights.dtype),
+        ),
+        in_specs=[VMEM] * 5 + [HBM],
+        out_specs=(HBM, HBM, VMEM, VMEM, HBM),
+        scratch_shapes=direct_scratch(rows, width) * 2 + sems(3, 3),
         compiler_params=comm_params(number, LIMIT),
         name="join_ffn",
-        cost_estimate=cost(50),
-    )(part, cotangent, middle, gain, *weights)
+        cost_estimate=cost(60),
+    )(part, moe_part, cotangent, middle, gain, weights)
 
 
 def scatter_keys(dk, dv, out_part, dq, weights, number):
@@ -668,21 +834,19 @@
     )(dk, dv, out_part, dq, *weights)
 
 
-def join_tail(part, moe_part, layer_input, middle, d_middle, gain, qkv_part, pack, number):
+def join_tail(part, layer_input, d_middle, gain, qkv_part, pack, number):
     _, rows, width = part.shape
     small = pack.shape[1]
 
-    def kernel(part_ref, moe_ref, x_ref, middle_ref, d_ref, gain_ref, qkv_ref, pack_ref, *refs):
-        full_ref, out_ref, got_ref, one_ref, both_ref = refs[:5]
-        scratch = refs[5:]
+    def kernel(part_ref, x_ref, d_ref, gain_ref, qkv_ref, pack_ref, *refs):
+        full_ref, got_ref, one_ref, both_ref = refs[:4]
+        scratch = refs[4:]
         greet(tensor_peers() + dp_peers())
         scatter, gather = join_parts(part_ref, full_ref, scratch[:N_JOIN])
-        scatter_moe, gather_moe = join_parts(moe_ref, out_ref, scratch[N_JOIN : 2 * N_JOIN])
         scatter.start()
-        scatter_moe.start()
-        weights = Exchange(qkv_ref, got_ref, *scratch[2 * N_JOIN : 2 * N_JOIN + 3])
+        weights = Exchange(qkv_ref, got_ref, *scratch[N_JOIN : N_JOIN + 3])
         weights.start()
-        own, few, mine, more, send, recv, tsend, trecv = scratch[2 * N_JOIN + 3 :]
+        own, few, mine, more, send, recv, tsend, trecv = scratch[N_JOIN + 3 :]
         me, t = lax.axis_index("dp"), lax.axis_index("tensor")
         resid = x_ref[t].astype(f32)
         inv = second_moment(resid)
@@ -695,20 +859,8 @@
             - resid * (inv * inv * inv) * jnp.mean(scaled * resid, axis=1, keepdims=True)
         )
         gain_grad = column_sum(d_normed * resid * inv)
-        scatter_moe.middle()
-        moe_out = scatter_moe.total()
-        output = middle_ref[...] + moe_out
-        gather_moe.start(output)
-
-        def folded(value):
-            row = column_sum(value)
-            return sum(row[:, i * 128 : (i + 1) * 128] for i in range(width // 128))
-
-        moe_row, out_row = folded(moe_out * moe_out), folded(output * output)
         own[...] = pack_ref[...]
         for i in range(N_DP):
-            own[i, small - 3 : small - 2] = moe_row
-            own[i, small - 2 : small - 1] = out_row
             own[i, small - 1 : small] = gain_grad[:, i * 128 : (i + 1) * 128]
         firsts = [
             remote(own.at[me ^ k], few.at[k], send.at[k], recv.at[k], {"dp": me ^ k})
@@ -717,7 +869,6 @@
         for copy in firsts:
             copy.start()
         gather.relay()
-        gather_moe.relay()
         value = own[me]
         for k in range(1, N_DP):
             firsts[k - 1].wait_recv()
@@ -736,23 +887,20 @@
         for copy in firsts + seconds:
             copy.wait_send()
         scatter.wait_send()
-        scatter_moe.wait_send()
         gather.wait()
-        gather_moe.wait()
         weights.wait()
 
     return pl.pallas_call(
         kernel,
         out_shape=(
-            struct(part.shape, bf16),
             struct(part.shape, bf16),
             struct(qkv_part.shape, qkv_part.dtype),
             struct((small, 128), f32),
             struct((small, 128), f32),
         ),
-        in_specs=[VMEM] * 6 + [HBM, VMEM],
-        out_specs=(HBM, HBM, HBM, VMEM, VMEM),
-        scratch_shapes=join_scratch(rows, width) * 2
+        in_specs=[VMEM] * 4 + [HBM, VMEM],
+        out_specs=(HBM, HBM, VMEM, VMEM),
+        scratch_shapes=join_scratch(rows, width)
         + DP_SEMS
         + [
             pltpu.VMEM((N_DP, small, 128), f32),
@@ -764,16 +912,10 @@
         compiler_params=comm_params(number, LIMIT),
         name="join_tail",
         cost_estimate=cost(60),
-    )(part, moe_part, layer_input, middle, d_middle, gain, qkv_part, pack)
+    )(part, layer_input, d_middle, gain, qkv_part, pack)
 
 
 KEYS = 256
-NT = (((1,), (1,)), ((), ()))
-TN = (((0,), (0,)), ((), ()))
-
-
-def mm(a, b, dims=(((1,), (0,)), ((), ()))):
-    return lax.dot_general(a, b, dims, preferred_element_type=f32)
 
 
 def attend(queries, keys, values, codes, bounds):
@@ -887,13 +1029,6 @@
     half_dim = vectors.shape[-1] // 2
     front, back = vectors[..., :half_dim], vectors[..., half_dim:]
     return jnp.concatenate([front * cosine - back * sine, back * cosine + front * sine], axis=-1)
-
-
-def silu_back(gate_part, up_part, d_hidden):
-    sigmoid_gate = jax.nn.sigmoid(gate_part)
-    d_gate = d_hidden * up_part * sigmoid_gate * (1.0 + gate_part * (1.0 - sigmoid_gate))
-    d_up = d_hidden * gate_part * sigmoid_gate
-    return d_gate, d_up
 
 
 def dot(pattern, a, b):
@@ -929,9 +1064,11 @@
     def permute(x, bits):
         return lax.ppermute(x, "tensor", [(i, i ^ bits) for i in range(N_T)])
 
-    pieces = range(GROUPS)
-    all_in = [expert_in[0]] + [permute(expert_in[0], i) for i in pieces[1:]]
-    all_out = [expert_out[0]] + [permute(expert_out[0], i) for i in pieces[1:]]
+    pieces = range(1, GROUPS)
+    own_weights = jnp.concatenate(
+        [expert_in[0].transpose(1, 2, 0).reshape(2 * eff, width), expert_out[0]], axis=0
+    )
+    weights = [own_weights] + [permute(own_weights, i) for i in pieces]
 
     hot = jnp.sum(
         (expert_ids[:, :, None] == jnp.arange(experts, dtype=jnp.int32)[None, None, :]).astype(f32),
@@ -987,84 +1124,50 @@
     normed_two = normed_two.reshape(tok, width)
 
     row_send = dot("rt,td->rd", places, normed_two).astype(bf16)
-    exp_rows, up_rows = rows_out([row_send.reshape(by_group), up_send.reshape(by_group)], 5)
+    router_rows = router_weight.T
+    exp_rows, up_rows, mixed, shared_d_normed, shared_grads, gate_vec_part = rows_out(
+        [row_send.reshape(by_group), up_send.reshape(by_group)],
+        normed_two,
+        cotangent,
+        shared_in.transpose(1, 2, 0).reshape(-1, width),
+        shared_out,
+        shared_gate.astype(f32).reshape(1, width),
+        5,
+    )
     exp_rows, up_rows = exp_rows.reshape(-1, width), up_rows.reshape(-1, width)
 
-    gate_value = jax.nn.sigmoid(dot("td,d->t", normed_two, shared_gate))
-    shared_gu = dot("td,dsf->tsf", normed_two, shared_in)
-    shared_hidden = (jax.nn.silu(shared_gu[:, 0]) * shared_gu[:, 1]).astype(bf16)
-    shared_part = dot("tf,fd->td", shared_hidden, shared_out)
-    upstream = cotangent.astype(f32)
-    d_shared = (gate_value[:, None] * upstream).astype(bf16)
-    gate_partial = jnp.sum(upstream * shared_part, axis=1) * gate_value * (1.0 - gate_value)
-    d_shared_hidden = dot("td,fd->tf", d_shared, shared_out)
-    d_gate, d_up = silu_back(shared_gu[:, 0], shared_gu[:, 1], d_shared_hidden)
-    d_shared_gu = jnp.stack([d_gate, d_up], axis=1).astype(bf16)
-    shared_out_part = dot("td,tf->df", d_shared, shared_hidden).astype(bf16)
-    shared_in_part = dot("td,tf->df", normed_two, d_shared_gu.reshape(tok, -1)).astype(bf16)
-    shared_d_normed = (
-        dot("tsf,dsf->td", d_shared_gu, shared_in)
-        + gate_partial[:, None] * shared_gate.astype(f32)[None, :]
-    )
-    gate_vec_part = jnp.einsum(
-        "t,td->d", gate_partial, normed_two.astype(f32), precision=lax.Precision.HIGHEST
-    )
-
-    w_in = jnp.concatenate(all_in, axis=2)
-    w_out = jnp.concatenate(all_out, axis=0)
-    row_logits = dot("rd,de->re", exp_rows, router_weight)
-    row_probs = jax.nn.softmax(row_logits, axis=1)
-    own_expert = (jnp.arange(experts, dtype=jnp.int32) == dp).astype(f32)[None, :]
-    row_gate = jnp.sum(row_probs * own_expert, axis=1, keepdims=True)
-    expert_gu = dot("rd,dsf->rsf", exp_rows, w_in)
-    expert_hidden = (jax.nn.silu(expert_gu[:, 0]) * expert_gu[:, 1]).astype(bf16)
-    expert_part = (row_gate * dot("rf,fd->rd", expert_hidden, w_out)).astype(bf16)
-
-    raw_hidden = dot("rd,fd->rf", up_rows, w_out)
-    d_gate_row = jnp.sum(expert_hidden.astype(f32) * raw_hidden, axis=1, keepdims=True)
-    d_row_logits = (d_gate_row * row_gate * (own_expert - row_probs)).astype(bf16)
-    d_gate, d_up = silu_back(expert_gu[:, 0], expert_gu[:, 1], row_gate * raw_hidden)
-    d_expert_gu = jnp.stack([d_gate, d_up], axis=1).astype(bf16)
-    d_rows = (
-        dot("rsf,dsf->rd", d_expert_gu, w_in) + dot("re,de->rd", d_row_logits, router_weight)
-    ).astype(bf16)
-    router_part = dot("re,rd->ed", d_row_logits, exp_rows)
-    gated_hidden = (expert_hidden.astype(f32) * row_gate).astype(bf16)
-
-    def piece_grads(i):
-        units = slice(i * eff, (i + 1) * eff)
-        return (
-            dot("rd,rsf->dsf", exp_rows, d_expert_gu[:, :, units]),
-            dot("rf,rd->fd", gated_hidden[:, units], up_rows),
-        )
-
-    sent = [tuple(g.astype(bf16) for g in piece_grads(i)) for i in pieces[1:]]
-
-    def sum_of(own, other):
-        return (own.astype(f32) + other.astype(f32)).astype(bf16)
-
-    by_chip = [
-        g.reshape(8, 2, width // N_DP, -1) for g in (shared_in_part, shared_out_part)
-    ]
-    back_grads, back_out, *got = rows_back(
-        [d_rows.reshape(by_group), expert_part.reshape(by_group)], by_chip, 6
+    own_expert = jnp.broadcast_to(
+        (jnp.arange(experts, dtype=jnp.int32) == dp).astype(f32)[:, None], (experts, 128)
+    )
+    expert_part, d_rows, d_expert_gu, gated_hidden, router_part = routed_expert(
+        exp_rows, up_rows, weights, router_rows, own_expert
+    )
+
+    back_grads, back_out, got, own_grads, sent = rows_back(
+        [d_rows.reshape(by_group), expert_part.reshape(by_group)],
+        shared_grads,
+        d_expert_gu,
+        gated_hidden,
+        exp_rows,
+        up_rows,
+        6,
     )
     core, z_index, x_index = dp % 2, dp // 4, (dp // 2) % 2
 
     def pick(x, index, axis=0):
         return lax.dynamic_index_in_dim(x, index, axis, keepdims=False)
 
-    by_z = [
-        sum_of(pick(own, core, 1), other).reshape(4, 2, width // N_DP, -1)
-        for own, other in zip(by_chip, got)
-    ]
+    by_z = (pick(shared_grads, core, 1).astype(f32) + got.astype(f32)).astype(bf16)
+    by_z = by_z.reshape((4, 2) + by_z.shape[1:])
 
     def combine(rows):
         return dot("rt,rd->td", places_back, rows.reshape(-1, width))
 
     d_normed_part = (shared_d_normed + combine(back_grads)).astype(bf16)
-    d_attn, d_middle, stats_two, *got = join_ffn(
+    moe_part = (mixed + combine(back_out)).astype(bf16)
+    d_attn, output, d_middle, stats_two, got = join_ffn(
         d_normed_part.reshape(by_slice),
+        moe_part.reshape(by_slice),
         cotangent.reshape(by_slice),
         middle,
         ffn_gain.reshape(1, width),
@@ -1072,13 +1175,9 @@
         7,
     )
     d_attn, sent = lax.optimization_barrier((d_attn, sent))
-    received = [tuple(permute(g, i) for g in pair) for i, pair in zip(pieces[1:], sent)]
-    by_x = [
-        (pick(own, z_index).astype(f32) + sum(other[k].astype(f32) for k in (1, 2, 3))).astype(bf16)
-        for own, other in zip(by_z, got)
-    ]
+    received = [permute(sent[i - 1], i) for i in pieces]
+    by_x = (pick(by_z, z_index).astype(f32) + sum(got[k].astype(f32) for k in (1, 2, 3))).astype(bf16)
     d_attn = d_attn.reshape(tok, width)
-    moe_part = (gate_value[:, None] * shared_part + combine(back_out)).astype(bf16)
 
     outproj_part = dot("qd,qf->df", d_attn, heads_out).astype(bf16)
     d_heads = dot("qd,fd->qf", d_attn, out_flat).astype(bf16)
@@ -1087,18 +1186,17 @@
     d_queries, d_keys, d_values = attend_back(
         queries, keys, values, codes, bounds, pair_wide, logs, d_heads
     )
-    got_k, got_v, got_out_part, d_queries, *got = scatter_keys(
+    got_k, got_v, got_out_part, d_queries, got = scatter_keys(
         d_keys.reshape(N_DP, tok, head_dim),
         d_values.reshape(N_DP, tok, head_dim),
         outproj_part.reshape(N_DP, width // N_DP, -1),
         d_queries.reshape(2, tok, head_dim),
-        by_x,
+        [by_x],
         9,
     )
     got_k, received = lax.optimization_barrier((got_k, received))
-    shared_in_grad, shared_out_grad = [
-        pick(own, x_index).astype(f32) + other.astype(f32) for own, other in zip(by_x, got)
-    ]
+    shared_grads = pick(by_x, x_index).astype(f32) + got.astype(f32)
+    n_shared = shared_in.shape[2]
     outproj_grad = jnp.sum(got_out_part.astype(f32), axis=0)
     def summed(x):
         x = jnp.sum(x.astype(f32).reshape(8, 2, tok, head_dim), axis=0)
@@ -1118,13 +1216,13 @@
     def slices(row):
         return row.reshape(-1, N_DP, 128).transpose(1, 0, 2)
 
-    three = jnp.sum(stats_one[:3], axis=1)
+    five = jnp.sum(jnp.concatenate([stats_one[:3], stats_two[1:3]]), axis=1)
     pack = jnp.concatenate(
         [
             slices(router_part),
-            slices(gate_vec_part),
+            slices(gate_vec_part[0]),
             slices(stats_two[0]),
-            jnp.broadcast_to(jnp.pad(three, (0, 125))[None, None], (N_DP, 1, 128)),
+            jnp.broadcast_to(jnp.pad(five, (0, 123))[None, None], (N_DP, 1, 128)),
             jnp.pad(
                 bias_part.reshape(6, N_DP, 8).transpose(1, 0, 2).reshape(N_DP, 1, 48),
                 ((0, 0), (0, 4), (0, 80)),
@@ -1132,11 +1230,9 @@
         ],
         axis=1,
     )
-    input_grad, output, got_qkv, over_dp, over_both = join_tail(
+    input_grad, got_qkv, over_dp, over_both = join_tail(
         d_normed_one.reshape(by_slice),
-        moe_part.reshape(by_slice),
         layer_input.reshape(by_slice),
-        middle,
         d_middle,
         attn_gain.reshape(1, width),
         qkv_part.reshape(N_DP, width // N_DP, -1),
@@ -1144,14 +1240,10 @@
         10,
     )
     bias_grad = over_dp[19, :48].reshape(3, 2, 8)
-    five = jnp.concatenate([over_both[18, :3], jnp.sum(over_both[21:23], axis=1)])
-    rms_stats = jnp.sqrt(five / (stream * width))
+    rms_stats = jnp.sqrt(over_both[18, :5] / (stream * width))
     qkv_grad = jnp.sum(got_qkv.astype(f32), axis=0)
 
-    expert_in_grad, expert_out_grad = piece_grads(0)
-    for got_in, got_out in received:
-        expert_in_grad = expert_in_grad + got_in.astype(f32)
-        expert_out_grad = expert_out_grad + got_out.astype(f32)
+    expert_grads = own_grads + sum(g.astype(f32) for g in received)
 
     return (
         output.reshape(tok, width),
@@ -1163,10 +1255,10 @@
         over_both[17],
         over_both[:16].T,
         over_both[16],
-        shared_in_grad.reshape(width // N_DP, 2, -1),
-        shared_out_grad.T,
-        expert_in_grad[None],
-        expert_out_grad[None],
+        shared_grads[: 2 * n_shared].reshape(2, n_shared, -1).transpose(2, 0, 1),
+        shared_grads[2 * n_shared :],
+        expert_grads[: 2 * eff].reshape(2, eff, width).transpose(2, 0, 1)[None],
+        expert_grads[2 * eff :][None],
         rms_stats,
     )
 

time: 634 us -> 574 us (0.905)
  matrix products: 81.4 us -> 20.4 us
  Pallas kernels: 420 us -> 457 us
  other arithmetic: 48.5 us -> 29.8 us
  waiting for transfers between devices: 11.2 us -> 0.02 us
    dot_general x29 -> x11, matrix products: 73.6 us -> 20.4 us  [dot(): return jnp.einsum(pattern, a, b, preferred_element_type=f32)]
    pallas_call x3 -> x4, Pallas kernels: 191 us -> 213 us  [the longest x1 75.1 us: join_ffn(): pl.pallas_call(kernel, out_shape=(struct(part.shape, bf16), struct(part.s...]
    ppermute x12 -> x6, waiting for transfers between devices: 11.2 us -> 0.02 us  [permute(): return lax.ppermute(x, 'tensor', [(i, i ^ bits) for i in range(N_T)])]
    pallas_call x1, Pallas kernels: 50.5 us -> 58.8 us  [rows_out(): pl.pallas_call(kernel, out_shape=tuple((struct(x.shape, x.dtype) for x in...]
    broadcast_in_dim x2 -> x0, other arithmetic: 7.89 us -> none  [the longest x1 4.88 us: on_device(): expert_in_grad[None]]
    unnamed x4 -> x0, matrix products: 7.18 us -> none
    another operation x8 -> x4, other arithmetic: 10.6 us -> 4.27 us
    unnamed x187 -> x103, local copies, waits for them, and re-layouts: 12.3 us -> 17.7 us
  transfers between devices with their start and end apart: 12 -> 6, of which waited for: 1 -> 0; matrix products, arithmetic and copies ran while one was open for 13% -> 6% of each run, Pallas kernels for 36% -> 43%
where the time goes in v3:
time: 574 us; the launch traced here: 564 us
  Pallas kernels  457 us (80%)
  local copies, waits for them, and re-layouts  42.2 us (7%)
  other arithmetic  29.8 us (5%)
  matrix products  20.4 us (4%)
  starting transfers between devices  13 us (2%)
    pallas_call x1, Pallas kernels, join_ffn(): pl.pallas_call(kernel, out_shape=(struct(part.shape, bf16), struct(part.s...  75.1 us
    pallas_call x1, Pallas kernels, join_tail(): pl.pallas_call(kernel, out_shape=(struct(part.shape, bf16), struct(qkv_pa...  65.4 us
    pallas_call x1, Pallas kernels, rows_out(): pl.pallas_call(kernel, out_shape=tuple((struct(x.shape, x.dtype) for x in...  58.8 us
    pallas_call x1, Pallas kernels, scatter_keys(): pl.pallas_call(kernel, out_shape=(struct(dk.shape, bf16), struct(dv.shape...  58.2 us
    pallas_call x1, Pallas kernels, join_attn(): pl.pallas_call(kernel, out_shape=(struct(part.shape, bf16), struct((rows,...  52.4 us
    pallas_call x1, Pallas kernels, rows_back(): pl.pallas_call(kernel, out_shape=tuple((struct(r.shape, r.dtype) for r in...  48.1 us
    pallas_call x1, Pallas kernels, gather_keys(): pl.pallas_call(kernel, out_shape=(struct((N_DP * tok, size), bf16), struc...  39.2 us
    pallas_call x1, Pallas kernels, routed_expert(): pl.pallas_call(kernel, out_shape=(struct((rows, width), bf16), struct((ro...  24 us
  transfers between devices with their start and end apart: 6, of which 0 were waited for; matrix products, arithmetic and copies ran while one was open for 6% of the time, Pallas kernels for 43%

profile of v3, /device:TPU:1, one launch (start us, length us, event | category | flops | bytes accessed | tf_op | source)
XLA Modules:
  0.0 564.0 jit_solution(2436276536820390036)
XLA Ops:
  0.7 3.3 pad_maximum_fusion.w0
  4.0 2.1 collective-permute-start
  6.2 2.6 collective-permute-start.1
  9.2 1.3 fusion.11
  10.6 0.7 fusion.45.v_ref
  11.3 8.1 %reshape.466 = bf16[2048,768]{1,0:T(8,128)(2,1)} reshape(bf16[2048,3,2,128]{3,2,1,0:T(2,128)(2,1)} %param.19) | data formatting | bytes 6291456 | tf_op jit(solution)/shard_map/reshape | solution.py:1212
  20.2 0.6 multiply_cosine_fusion
  21.2 0.9 maximum_bitcast_fusion
  22.1 39.2 %gather_keys.1 = (bf16[5120,128]{1,0:T(8,128)(2,1)}, bf16[5120,128]{1,0:T(8,128)(2,1)}, bf16[2,320,128]{2,1,0:T(8,128)(2,1)}) custom-call(bf16[2,320,128]{2,1,0:T(8,128)(2,1)} %get-tuple-element.180.k_ref, bf16[2,320,128]{2,1,0:T(8,128)(2,1)} %fusion.45.v_ref, bf16[2,320,128]{2,1,0:T(8,128)(2,1)} %get-tuple-element.181.q_ref), custom_call_target="tpu_custom_call" | custom-call | bytes 123000000 | tf_op jit(solution)/shard_map/gather_keys/pallas_call | solution.py:453
  61.4 0.7 broadcast_in_dim.57.code_ref
  63.1 0.9 copy-done.19
  64.0 12.3 %attend.1 = (bf16[640,128]{1,0:T(8,128)(2,1)S(1)}, f32[640,128]{1,0:T(8,128)S(1)}, f32[8,640]{1,0:T(8,128)S(1)}) custom-call(bf16[640,128]{1,0:T(8,128)(2,1)S(1)} %bitcast.187, bf16[5120,128]{1,0:T(8,128)(2,1)S(1)} %copy-done.6, bf16[5120,128]{1,0:T(8,128)(2,1)S(1)} %copy-done.8, s32[5120,128]{1,0:T(8,128)S(1)} %broadcast_in_dim.57.code_ref, ...), custom_call_target="tpu_custom_call" | custom-call | bytes 36000000 | tf_op jit(solution)/shard_map/attend/pallas_call | solution.py:959
  76.3 0.7 copy-done.23
  77.0 3.6 swap_cores.2
  81.0 0.9 slice_bitcast_fusion.13
  82.5 52.4 %join_attn.1 = (bf16[8,40,2048]{2,1,0:T(8,128)(2,1)S(1)}, f32[40,2048]{1,0:T(8,128)S(1)}, f32[8,2048]{1,0:T(8,128)S(1)}) custom-call(bf16[8,40,2048]{2,1,0:T(8,128)(2,1)S(1)} %bitcast.178, bf16[8,40,2048]{2,1,0:T(8,128)(2,1)S(1)} %bitcast.171, f32[1,2048]{1,0:T(1,128)S(1)} %bitcast.193), custom_call_target="tpu_custom_call" | custom-call | bytes 120000000 | tf_op jit(solution)/shard_map/join_attn/pallas_call | solution.py:725
  134.9 1.0 copy-done.12
  136.8 3.8 convolution_convert_fusion.1
  140.7 2.3 convolution_convert_fusion.2
  143.0 58.8 %rows_out.1 = (bf16[4,112,2048]{2,1,0:T(8,128)(2,1)S(1)}, bf16[4,112,2048]{2,1,0:T(8,128)(2,1)}, f32[320,2048]{1,0:T(8,128)}, f32[320,2048]{1,0:T(8,128)}, bf16[...) custom-call(bf16[4,112,2048]{2,1,0:T(8,128)(2,1)} %bitcast.213, bf16[4,112,2048]{2,1,0:T(8,128)(2,1)} %bitcast.212, ...), custom_call_target="tpu_custom_call" | custom-call | bytes 135000000 | tf_op jit(solution)/shard_map/rows_out/pallas_call | solution.py:556
  201.8 1.3 copy-done.4
  203.2 24.0 %routed_expert.1 = (bf16[448,2048]{1,0:T(8,128)(2,1)S(1)}, bf16[448,2048]{1,0:T(8,128)(2,1)S(1)}, bf16[4,352,448]{2,1,0:T(8,128)(2,1)S(1)}, bf16[4,176,448]{2,1,0:T(8,128)(2,1)S(1)}, f32[16,2048]{1,0:T(8,128)S(1)}) custom-call(bf16[448,2048]{1,0:T(8,128)(2,1)} %bitcast.173, bf16[448,2048]{1,0:T(8,128)(2,1)} %bitcast.202, ...), custom_call_target="tpu_custom_call" | custom-call | bytes 66000000 | tf_op jit(solution)/shard_map/routed_expert/pallas_call | solution.py:628
  227.2 1.2 copy-done.10
  228.5 1.2 copy-done.11
  229.7 48.1 %rows_back.1 = (bf16[4,112,2048]{2,1,0:T(8,128)(2,1)S(1)}, bf16[4,112,2048]{2,1,0:T(8,128)(2,1)S(1)}, bf16[8,2112,128]{2,1,0:T(8,128)(2,1)}, f32[528,2048]{1,0:T(8,128)}, bf16[3,528,2048]{2,1,0:T(8,128)(2,1)}) custom-call(bf16[4,112,2048]{2,1,0:T(8,128)(2,1)} %bitcast.180, bf16[4,112,2048]{2,1,0:T(8,128)(2,1)} %bitcast.179, ...), custom_call_target="tpu_custom_call" | custom-call | bytes 150000000 | tf_op jit(solution)/shard_map/rows_back/pallas_call | solution.py:690
  277.8 6.8 %fusion = bf16[8,2112,128]{2,1,0:T(8,128)(2,1)} fusion(bf16[8,2112,128]{2,1,0:T(8,128)(2,1)} %get-tuple-element.79, s32[]{:T(128)S(6)} %select_n.103, bf16[8,2,2112,128]{3,2,1,0:T(8,128)(2,1)} %get-tuple-element.72.refs_2_), kind=kLoop, calls=%fused_computation.1 | loop fusion | flops 8650752 | bytes 12976132 | tf_op jit(solution)/shard_map/convert_element_type | solution.py:1160
  284.7 1.1 fusion.5
  285.8 0.6 copy-done.32
  286.4 1.1 fusion.6
  287.5 75.1 %join_ffn.1 = (bf16[8,40,2048]{2,1,0:T(8,128)(2,1)S(1)}, bf16[8,40,2048]{2,1,0:T(8,128)(2,1)S(1)}, f32[40,2048]{1,0:T(8,128)S(1)}, f32[8,2048]{1,0:T(8,128)S(1)}, bf16[4,2,2112,128]{3,2,1,0:T(8,128)(2,1)}) custom-call(bf16[8,40,2048]{2,1,0:T(8,128)(2,1)S(1)} %bitcast.177, bf16[8,40,2048]{2,1,0:T(8,128)(2,1)S(1)} %bitcast.176, ...), custom_call_target="tpu_custom_call" | custom-call | bytes 180000000 | tf_op jit(solution)/shard_map/join_ffn/pallas_call | solution.py:775
  363.3 3.4 slice_bitcast_fusion
  366.9 5.9 %collective-permute-start.3 = (bf16[528,2048]{1,0:T(8,128)(2,1)}, bf16[528,2048]{1,0:T(8,128)(2,1)}, u32[]{:S(2)}, u32[]{:S(2)}) collective-permute-start(bf16[528,2048]{1,0:T(8,128)(2,1)} %get-tuple-element.140), channel_id=1, source_target_pairs={{0,1},{1,0},{2,3},{3,2},{4,5},{5,4},{6,7},{7,6},{8,9},{9,8},{10,11... | collective-permute-start | bytes 6488072 | tf_op jit(solution)/shard_map/ppermute | solution.py:1065
  373.0 2.2 collective-permute-start.5
  375.2 2.9 add_convert_fusion
  378.2 0.7 pad_maximum_fusion.2.x_ref
  378.8 3.6 swap_cores.3
  382.5 1.3 copy-done.7
  383.8 1.3 copy-done.9
  385.1 0.9 copy-done.21
  386.0 15.8 %attend_back.1 = (bf16[640,128]{1,0:T(8,128)(2,1)S(1)}, bf16[5120,128]{1,0:T(8,128)(2,1)S(1)}, bf16[5120,128]{1,0:T(8,128)(2,1)S(1)}) custom-call(bf16[640,128]{1,0:T(8,128)(2,1)S(1)} %bitcast.188, bf16[5120,128]{1,0:T(8,128)(2,1)S(1)} %copy-done.7, bf16[5120,128]{1,0:T(8,128)(2,1)S(1)} %copy-done.9, s32[5120,128]{1,0:T(8,128)} %copy-done.2, ...), custom_call_target="tpu_custom_call" | custom-call | bytes 45000000 | tf_op jit(solution)/shard_map/attend_back/pallas_call | solution.py:998
  401.8 1.0 copy-done.16
  402.8 1.1 copy-done.17
  403.9 1.8 convolution_convert_fusion.5
  405.7 58.2 %scatter_keys.1 = (bf16[16,320,128]{2,1,0:T(8,128)(2,1)}, bf16[16,320,128]{2,1,0:T(8,128)(2,1)}, bf16[16,128,256]{2,1,0:T(8,128)(2,1)}, bf16[2,320,128]{2,1,0:T(8,128)(2,1)}, bf16[2112,128]{1,0:T(8,128)(2,1)}) custom-call(bf16[16,320,128]{2,1,0:T(8,128)(2,1)} %bitcast.184, bf16[16,320,128]{2,1,0:T(8,128)(2,1)} %bitcast.185, bf16[16,128,256]{2,1,0:T(8,128)(2,1)} %bitcast.217, ...), custom_call_target="tpu_custom_call" | custom-call | bytes 150000000 | tf_op jit(solution)/shard_map/scatter_keys/pallas_call | solution.py:819
  464.0 1.4 convert_add_fusion.1
  465.4 0.9 slice.200
  466.3 0.8 slice.201
  467.0 0.8 slice.168
  468.0 0.8 copy.52
  468.8 1.5 reduce
  470.5 0.8 slice_bitcast_fusion.15
  471.4 5.5 add_add_fusion
  477.0 1.8 slice.202
  478.8 1.2 slice_bitcast_fusion.3
  479.9 0.6 copy-done.34
  480.8 0.8 fusion.44
  482.1 3.6 convolution_convert_fusion
  486.0 4.2 convolution_convert_fusion.3
  490.2 1.3 copy-done.18
  491.5 65.4 %join_tail.1 = (bf16[8,40,2048]{2,1,0:T(8,128)(2,1)S(1)}, bf16[16,128,768]{2,1,0:T(8,128)(2,1)}, f32[24,128]{1,0:T(8,128)S(1)}, f32[24,128]{1,0:T(8,128)S(1)}) custom-call(bf16[8,40,2048]{2,1,0:T(8,128)(2,1)S(1)} %bitcast.186, bf16[8,40,2048]{2,1,0:T(8,128)(2,1)S(1)} %bitcast.172, f32[40,2048]{1,0:T(8,128)S(1)} %get-tuple-element.95.d_ref, ...), custom_call_target="tpu_custom_call" | custom-call | bytes 180000000 | tf_op jit(solution)/shard_map/join_tail/pallas_call | solution.py:893
  558.6 1.9 bitcast_convert_fusion
  560.9 0.9 reshape.472
  561.9 0.7 reshape_squeeze.3
  562.5 1.1 copy.67
  (155 shorter events, 8.8 us)
Async XLA Ops:
  0.6 81.3 %copy-start = (bf16[2,128,2048]{2,1,0:T(8,128)(2,1)S(1)}, bf16[2,128,2048]{2,1,0:T(8,128)(2,1)}, u32[]{:S(2)}) copy-start(bf16[2,128,2048]{2,1,0:T(8,128)(2,1)} %param.21) | copy-start | bytes 3145732
  0.7 8.1 %copy-start.3 = (bf16[320,2048]{1,0:T(8,128)(2,1)S(1)}, bf16[320,2048]{1,0:T(8,128)(2,1)}, u32[]{:S(2)}) copy-start(bf16[320,2048]{1,0:T(8,128)(2,1)} %param.15) | copy-start | bytes 3932164
  0.7 8.5 %copy-start.44 = (bf16[3,2,128]{2,1,0:T(2,128)(2,1)S(1)}, bf16[3,2,128]{2,1,0:T(2,128)(2,1)}, u32[]{:S(2)}) copy-start(bf16[3,2,128]{2,1,0:T(2,128)(2,1)} %param.20) | copy-start | bytes 4612
  0.7 8.5 %copy-start.27 = (f32[2048]{0:T(1024)S(1)}, f32[2048]{0:T(1024)}, u32[]{:S(2)}) copy-start(f32[2048]{0:T(1024)} %param.18) | copy-start | bytes 24580
  0.7 8.5 %copy-start.30 = (bf16[2048,3,2,128]{3,2,1,0:T(2,128)(2,1)S(1)}, bf16[2048,3,2,128]{3,2,1,0:T(2,128)(2,1)}, u32[]{:S(2)}) copy-start(bf16[2048,3,2,128]{3,2,1,0:T(2,128)(2,1)} %param.19) | copy-start | bytes 9437188
  4.0 199.1 %collective-permute-start = (bf16[528,2048]{1,0:T(8,128)(2,1)}, bf16[528,2048]{1,0:T(8,128)(2,1)}, u32[]{:S(2)}, u32[]{:S(2)}) collective-permute-start(bf16[528,2048]{1,0:T(8,128)(2,1)} %pad_maximum_fusion.w0), channel_id=1, source_target_pairs={{0,1},{1,0},{2,3},{3,2},{4,5},{5,4},{6,7},{7,6},{8,9},{9,8},{10,11... | collective-permute-start | bytes 6488072 | tf_op jit(solution)/shard_map/ppermute | solution.py:1065
  6.2 197.0 %collective-permute-start.1 = (bf16[528,2048]{1,0:T(8,128)(2,1)}, bf16[528,2048]{1,0:T(8,128)(2,1)}, u32[]{:S(2)}, u32[]{:S(2)}) collective-permute-start(bf16[528,2048]{1,0:T(8,128)(2,1)} %pad_maximum_fusion.w0), channel_id=1, source_target_pairs={{0,2},{1,3},{2,0},{3,1},{4,6},{5,7},{6,4},{7,5},{8,10},{9,11},{10,... | collective-permute-start | bytes 6488072 | tf_op jit(solution)/shard_map/ppermute | solution.py:1065
  8.8 194.3 %collective-permute-start.2 = (bf16[528,2048]{1,0:T(8,128)(2,1)}, bf16[528,2048]{1,0:T(8,128)(2,1)}, u32[]{:S(2)}, u32[]{:S(2)}) collective-permute-start(bf16[528,2048]{1,0:T(8,128)(2,1)} %pad_maximum_fusion.w0), channel_id=1, source_target_pairs={{0,3},{1,2},{2,1},{3,0},{4,7},{5,6},{6,5},{7,4},{8,11},{9,10},{10,... | collective-permute-start | bytes 6488072 | tf_op jit(solution)/shard_map/ppermute | solution.py:1065
  11.3 8.1 %copy-start.45 = (s32[4]{0:T(128)S(1)}, s32[4]{0:T(128)}, u32[]{:S(2)}) copy-start(s32[4]{0:T(128)} %param.16) | copy-start | bytes 52
  61.4 1.3 copy-start.6
  61.4 1.7 copy-start.8
  63.1 0.9 copy-start.19
  64.0 12.3 %copy-start.2 = (s32[5120,128]{1,0:T(8,128)}, s32[5120,128]{1,0:T(8,128)S(1)}, u32[]{:S(2)}) copy-start(s32[5120,128]{1,0:T(8,128)S(1)} %broadcast_in_dim.57.code_ref) | copy-start | bytes 7864324
  64.0 16.7 %copy-start.43 = (bf16[2048]{0:T(1024)(128)(2,1)S(1)}, bf16[2048]{0:T(1024)(128)(2,1)}, u32[]{:S(2)}) copy-start(bf16[2048]{0:T(1024)(128)(2,1)} %param.24) | copy-start | bytes 12292
  64.0 16.7 %copy-start.42 = (s32[320,4]{0,1:T(4,128)S(1)}, s32[320,4]{0,1:T(4,128)}, u32[]{:S(2)}) copy-start(s32[320,4]{0,1:T(4,128)} %param.17) | copy-start | bytes 15364
  76.3 0.7 copy-start.23
  77.0 5.5 copy-start.25
  81.9 53.0 %copy-start.36 = (bf16[320,128]{1,0:T(8,128)(2,1)}, bf16[320,128]{1,0:T(8,128)(2,1)S(1)}, u32[]{:S(2)}) copy-start(bf16[320,128]{1,0:T(8,128)(2,1)S(1)} %get-tuple-element.165) | copy-start | bytes 245764
  81.9 53.0 %copy-start.38 = (bf16[320,128]{1,0:T(8,128)(2,1)}, bf16[320,128]{1,0:T(8,128)(2,1)S(1)}, u32[]{:S(2)}) copy-start(bf16[320,128]{1,0:T(8,128)(2,1)S(1)} %get-tuple-element.166) | copy-start | bytes 245764
  134.9 1.1 copy-start.12
  136.8 3.8 copy-start.13
  140.7 2.3 copy-start.5
  143.0 60.2 %copy-start.24 = (bf16[2048,16]{0,1:T(8,128)(2,1)S(1)}, bf16[2048,16]{0,1:T(8,128)(2,1)}, u32[]{:S(2)}) copy-start(bf16[2048,16]{0,1:T(8,128)(2,1)} %param.23) | copy-start | bytes 196612
  201.8 1.3 copy-start.4
  227.2 1.2 copy-start.10
  228.5 1.2 copy-start.11
  277.8 6.8 %copy-start.33 = (f32[320,2048]{1,0:T(8,128)S(1)}, f32[320,2048]{1,0:T(8,128)}, u32[]{:S(2)}) copy-start(f32[320,2048]{1,0:T(8,128)} %get-tuple-element.76) | copy-start | bytes 7864324
  284.7 1.7 copy-start.32
  286.4 76.9 %slice-start = ((s8[6488064]{0:T(1024)(128)(4,1)}), s8[4194304]{0:T(1024)(128)(4,1)S(1)}, s32[]{:S(2)}) async-start(s8[6488064]{0:T(1024)(128)(4,1)} %bitcast.205), calls=%async_computation | async-start | bytes 8388608
  287.5 75.8 %slice-start.1 = ((s8[6488064]{0:T(1024)(128)(4,1)}), s8[2293760]{0:T(1024)(128)(4,1)S(1)}, s32[]{:S(2)}) async-start(s8[6488064]{0:T(1024)(128)(4,1)} %bitcast.205), calls=%async_computation.1 | async-start | bytes 4587520
  362.7 4.1 copy-start.14
  362.7 4.1 copy-start.26
  362.7 4.2 copy-start.28
  363.3 11.9 %slice-start.2 = ((s8[4325376]{0:T(1024)(128)(4,1)}), s8[4194304]{0:T(1024)(128)(4,1)S(1)}, s32[]{:S(2)}) async-start(s8[4325376]{0:T(1024)(128)(4,1)} %bitcast.210), calls=%async_computation.2 | async-start | bytes 8388608
  363.3 11.9 %slice-start.3 = ((s8[4325376]{0:T(1024)(128)(4,1)}), s8[131072]{0:T(1024)(128)(4,1)S(1)}, s32[]{:S(2)}) async-start(s8[4325376]{0:T(1024)(128)(4,1)} %bitcast.210), calls=%async_computation.3 | async-start | bytes 262144
  366.9 104.5 %collective-permute-start.3 = (bf16[528,2048]{1,0:T(8,128)(2,1)}, bf16[528,2048]{1,0:T(8,128)(2,1)}, u32[]{:S(2)}, u32[]{:S(2)}) collective-permute-start(bf16[528,2048]{1,0:T(8,128)(2,1)} %get-tuple-element.140), channel_id=1, source_target_pairs={{0,1},{1,0},{2,3},{3,2},{4,5},{5,4},{6,7},{7,6},{8,9},{9,8},{10,11... | collective-permute-start | bytes 6488072 | tf_op jit(solution)/shard_map/ppermute | solution.py:1065
  372.8 98.6 %collective-permute-start.4 = (bf16[528,2048]{1,0:T(8,128)(2,1)}, bf16[528,2048]{1,0:T(8,128)(2,1)}, u32[]{:S(2)}, u32[]{:S(2)}) collective-permute-start(bf16[528,2048]{1,0:T(8,128)(2,1)} %get-tuple-element.139), channel_id=1, source_target_pairs={{0,2},{1,3},{2,0},{3,1},{4,6},{5,7},{6,4},{7,5},{8,10},{9,11},{10,... | collective-permute-start | bytes 6488072 | tf_op jit(solution)/shard_map/ppermute | solution.py:1065
  373.0 98.5 %collective-permute-start.5 = (bf16[528,2048]{1,0:T(8,128)(2,1)}, bf16[528,2048]{1,0:T(8,128)(2,1)}, u32[]{:S(2)}, u32[]{:S(2)}) collective-permute-start(bf16[528,2048]{1,0:T(8,128)(2,1)} %get-tuple-element.138), channel_id=1, source_target_pairs={{0,3},{1,2},{2,1},{3,0},{4,7},{5,6},{6,5},{7,4},{8,11},{9,10},{10,... | collective-permute-start | bytes 6488072 | tf_op jit(solution)/shard_map/ppermute | solution.py:1065
  375.2 7.2 %copy-start.20 = (bf16[2,320,128]{2,1,0:T(8,128)(2,1)S(1)}, bf16[2,320,128]{2,1,0:T(8,128)(2,1)}, u32[]{:S(2)}) copy-start(bf16[2,320,128]{2,1,0:T(8,128)(2,1)} %get-tuple-element.62) | copy-start | bytes 491524
  382.5 1.3 copy-start.7
  383.8 1.3 copy-start.9
  385.1 0.9 copy-start.21
  386.0 17.9 %copy-start.29 = (bf16[8,40,2048]{2,1,0:T(8,128)(2,1)S(1)}, bf16[8,40,2048]{2,1,0:T(8,128)(2,1)}, u32[]{:S(2)}) copy-start(bf16[8,40,2048]{2,1,0:T(8,128)(2,1)} %copy-done.28) | copy-start | bytes 3932164
  386.0 17.9 %copy-start.37 = (bf16[320,128]{1,0:T(8,128)(2,1)S(1)}, bf16[320,128]{1,0:T(8,128)(2,1)}, u32[]{:S(2)}) copy-start(bf16[320,128]{1,0:T(8,128)(2,1)} %copy-done.36) | copy-start | bytes 245764
  386.0 17.9 %copy-start.39 = (bf16[320,128]{1,0:T(8,128)(2,1)S(1)}, bf16[320,128]{1,0:T(8,128)(2,1)}, u32[]{:S(2)}) copy-start(bf16[320,128]{1,0:T(8,128)(2,1)} %copy-done.38) | copy-start | bytes 245764
  401.8 1.1 copy-start.16
  402.8 1.1 copy-start.17
  403.9 1.8 copy-start.22
  464.0 3.9 copy-start.35
  466.3 4.0 copy-start.41
  466.3 5.1 copy-start.40
  478.8 1.8 copy-start.34
  490.2 1.3 copy-start.18
  556.9 3.5 copy-start.31
  560.5 2.1 copy-start.15
  560.5 3.1 copy-start.1

commit v4 on v3

v4 whole, which is shorter than its diff:
```python
import math

import jax
import jax.numpy as jnp
from jax import lax
from jax.experimental import pallas as pl
from jax.experimental.pallas import tpu as pltpu
from jax.sharding import PartitionSpec as P

DBLOCK = 256
EPSILON = 1e-06
THETA = 1000000.0
NEG_FILL = -1e30
MESH = pl.DeviceIdType.MESH
f32 = jnp.float32
bf16 = jnp.bfloat16
N_DP = 16
N_T = 8
SLOTS = 112
LIMIT = 48 * 1024 * 1024
CODE = 1 << 16

HBM = pl.BlockSpec(memory_space=pl.ANY)
VMEM = pl.BlockSpec(memory_space=pltpu.VMEM)


def greet(peers, *more):
    barrier = pltpu.get_barrier_semaphore()
    for peer in peers:
        pl.semaphore_signal(barrier, inc=1, device_id=peer, device_id_type=MESH)
    count = len(peers)
    for rows in more:
        count = count + rows.greet()
    pl.semaphore_wait(barrier, count)


def remote(src, dst, send, recv, device):
    return pltpu.make_async_remote_copy(
        src_ref=src,
        dst_ref=dst,
        send_sem=send,
        recv_sem=recv,
        device_id=device,
        device_id_type=MESH,
    )


def dma(*shape):
    return pltpu.SemaphoreType.DMA(shape)


def cost(micros):
    return pl.CostEstimate(flops=0, bytes_accessed=int(micros * 3e6), transcendentals=0)


def comm_params(number, limit=None):
    return pltpu.CompilerParams(
        collective_id=number, has_side_effects=True, vmem_limit_bytes=limit
    )


NT = (((1,), (1,)), ((), ()))
TN = (((0,), (0,)), ((), ()))


def mm(a, b, dims=(((1,), (0,)), ((), ()))):
    return lax.dot_general(a, b, dims, preferred_element_type=f32)


GROUPS = 4
ORDER = (4, 12, 2, 5, 13, 3, 8, 6, 14, 9, 7, 15, 10, 11, 1)
STEPS = (1, 3, 2, 4, 5, 7, 6)
CHUNKS = ((0, 48), (48, 64))


def sems(*counts):
    return [dma(*c) if isinstance(c, tuple) else dma(c) for c in counts]


def dp_peers():
    me = lax.axis_index("dp")
    return [{"dp": me ^ k} for k in range(1, N_DP)]


def tensor_peers():
    me = lax.axis_index("tensor")
    return [{"tensor": me ^ k} for k in range(1, N_T)]


def coordinates():
    d, t = lax.axis_index("dp"), lax.axis_index("tensor")
    return d, d // 4, t // 4, t % 4


def route_plane():
    d, z, _, y = coordinates()
    plane = 2 * ((z + d // 2) % 2) + d % 2
    return plane, y ^ plane


class Rows:
    def __init__(self, x_ref, out_ref, send, recv, local, back=False):
        self.x, self.out, self.send, self.recv, self.local, self.back = x_ref, out_ref, send, recv, local, back
        d, z, half, y = coordinates()
        plane, offset = route_plane()
        if back:
            experts = [{"dp": 4 * k + offset, "tensor": 4 * half + plane} for k in range(GROUPS)]
            target = y ^ (d % 4)
        else:
            experts = [{"dp": 4 * (z ^ offset) + j, "tensor": 4 * half + plane} for j in range(GROUPS)]
        groups = [
            {
                "dp": 4 * g + 2 * ((y // 2 + g) % 2) + y % 2,
                "tensor": 4 * half + (target if back else y ^ g ^ z),
            }
            for g in range(GROUPS)
        ]
        self.peers, self.sources = (groups, experts) if back else (experts, groups)
        self.slot = z
        self.mine = z if back else d % 4
        self.own = offset == 0
        if back:
            self.own = jnp.logical_and(self.own, d % 4 == 0)
        self.d = d

    def is_own(self, j):
        return jnp.logical_and(self.own, self.mine == j)

    def greet(self):
        barrier = pltpu.get_barrier_semaphore()
        for j in range(GROUPS):
            source = self.sources[j]

            @pl.when(jnp.logical_not(jnp.logical_and(self.own, self.slot == j)))
            def _():
                pl.semaphore_signal(barrier, inc=1, device_id=source, device_id_type=MESH)

        return GROUPS - self.own.astype(jnp.int32)

    def copy(self, j, c):
        rows = pl.ds(*CHUNKS[c])
        return remote(
            self.x.at[j, rows],
            self.out.at[self.slot, rows],
            self.send.at[c, j],
            self.recv.at[c, self.slot],
            self.peers[j],
        )

    def arrival(self, j, c):
        rows = pl.ds(*CHUNKS[c])
        return remote(
            self.x.at[j, rows],
            self.out.at[j, rows],
            self.send.at[c, j],
            self.recv.at[c, j],
            self.peers[j],
        )

    def inside(self):
        return pltpu.make_async_copy(self.x.at[self.mine], self.out.at[self.slot], self.local.at[0])

    def start(self):
        for c in range(len(CHUNKS)):
            for j in range(GROUPS):

                @pl.when(jnp.logical_not(self.is_own(j)))
                def _():
                    self.copy(j, c).start()

        @pl.when(self.own)
        def _():
            self.inside().start()

    def wait(self):
        @pl.when(self.own)
        def _():
            self.inside().wait()

        for c in range(len(CHUNKS)):
            for j in range(GROUPS):

                @pl.when(jnp.logical_not(self.is_own(j)))
                def _():
                    self.copy(j, c).wait_send()

                @pl.when(jnp.logical_not(jnp.logical_and(self.own, self.slot == j)))
                def _():
                    self.arrival(j, c).wait_recv()


ROW_SEMS = sems((len(CHUNKS), GROUPS), (len(CHUNKS), GROUPS), 1)


class Exchange:
    def __init__(self, x_ref, out_ref, send, recv, local):
        me = lax.axis_index("dp")
        self.copies = [
            remote(x_ref.at[me ^ k], out_ref.at[me], send.at[k], recv.at[k], {"dp": me ^ k})
            for k in ORDER
        ]
        self.copies.append(pltpu.make_async_copy(x_ref.at[me], out_ref.at[me], local.at[0]))

    def start(self):
        for copy in self.copies:
            copy.start()

    def wait(self):
        for copy in self.copies:
            copy.wait()


DP_SEMS = sems(N_DP, N_DP, 1)


class Swap:
    def __init__(self, x_ref, out_ref, send, recv, local):
        me = lax.axis_index("dp")
        core = lax.rem(me, 2)
        self.copies = [
            remote(x_ref.at[1 - core], out_ref.at[core], send.at[0], recv.at[0], {"dp": me ^ 1}),
            pltpu.make_async_copy(x_ref.at[core], out_ref.at[core], local.at[0]),
        ]

    start = Exchange.start
    wait = Exchange.wait


SWAP_SEMS = sems(1, 1, 1)


class DirectScatter:
    def __init__(self, part_ref, got, send, recv):
        self.me = lax.axis_index("tensor")
        self.part, self.got = part_ref, got
        self.copies = [
            remote(
                part_ref.at[self.me ^ k], got.at[k], send.at[k], recv.at[k], {"tensor": self.me ^ k}
            )
            for k in STEPS
        ]

    def start(self):
        for copy in self.copies:
            copy.start()

    def total(self):
        value = self.part[self.me].astype(f32)
        for k, copy in zip(STEPS, self.copies):
            copy.wait_recv()
            value = value + self.got[k].astype(f32)
        return value

    def wait_send(self):
        for copy in self.copies:
            copy.wait_send()


class DirectGather:
    def __init__(self, mine, full_ref, send, recv, local):
        me = lax.axis_index("tensor")
        self.mine = mine
        self.copies = [
            remote(mine, full_ref.at[me], send.at[k], recv.at[k], {"tensor": me ^ k}) for k in STEPS
        ]
        self.copies.append(pltpu.make_async_copy(mine, full_ref.at[me], local.at[0]))

    def start(self, value):
        self.mine[...] = value.astype(bf16)
        for copy in self.copies:
            copy.start()

    def wait(self):
        for copy in self.copies:
            copy.wait()


def direct_scratch(rows, width):
    return [
        pltpu.VMEM((N_T, rows, width), bf16),
        pltpu.VMEM((rows, width), bf16),
    ] + sems(N_T, N_T, N_T, N_T, 1)


N_DIRECT = 7


def direct_parts(part_ref, full_ref, scratch):
    got, mine, send, recv, asend, arecv, local = scratch
    return DirectScatter(part_ref, got, send, recv), DirectGather(mine, full_ref, asend, arecv, local)


class Scatter:
    def __init__(self, part_ref, got, mid, last, send, recv):
        t = lax.axis_index("tensor")
        y, half = t % 4, t // 4
        self.part, self.got, self.mid, self.last = part_ref, got, mid, last
        self.slots = (4 * (1 - half) + y, t)
        self.copies = [
            [
                remote(
                    part_ref.at[slot ^ k],
                    got.at[a, k],
                    send.at[a, k],
                    recv.at[a, k],
                    {"tensor": t ^ k},
                )
                for k in (1, 3, 2)
            ]
            for a, slot in enumerate(self.slots)
        ]
        self.across = remote(mid, last, send.at[0, 0], recv.at[0, 0], {"tensor": t ^ 4})

    def start(self):
        for copies in self.copies:
            for copy in copies:
                copy.start()

    def over_y(self, a):
        value = self.part[self.slots[a]].astype(f32)
        for k, copy in zip((1, 3, 2), self.copies[a]):
            copy.wait_recv()
            value = value + self.got[a, k].astype(f32)
        return value

    def middle(self):
        self.mid[...] = self.over_y(0).astype(bf16)
        self.across.start()

    def total(self):
        value = self.over_y(1)
        self.across.wait_recv()
        return value + self.last[...].astype(f32)

    def wait_send(self):
        for copies in self.copies:
            for copy in copies:
                copy.wait_send()
        self.across.wait_send()


class Gather:
    def __init__(self, mine, full_ref, send, recv, local):
        t = lax.axis_index("tensor")
        self.mine = mine
        self.across = remote(
            mine, full_ref.at[t], send.at[0, 0], recv.at[0, 0], {"tensor": t ^ 4}
        )
        self.first = [
            remote(mine, full_ref.at[t], send.at[0, k], recv.at[0, k], {"tensor": t ^ k})
            for k in (1, 3, 2)
        ]
        self.second = [
            remote(
                full_ref.at[t ^ 4],
                full_ref.at[t ^ 4],
                send.at[1, k],
                recv.at[1, k],
                {"tensor": t ^ k},
            )
            for k in (1, 3, 2)
        ]
        self.own = pltpu.make_async_copy(mine, full_ref.at[t], local.at[0])

    def start(self, value):
        self.mine[...] = value.astype(bf16)
        for copy in [self.across] + self.first + [self.own]:
            copy.start()

    def relay(self):
        self.across.wait_recv()
        for copy in self.second:
            copy.start()

    def wait(self):
        self.across.wait_send()
        for copy in self.first + self.second + [self.own]:
            copy.wait()


JOIN_SEMS = sems((2, 4), (2, 4), (2, 4), (2, 4), 1)


def join_scratch(rows, width):
    return [
        pltpu.VMEM((2, 4, rows, width), bf16),
        pltpu.VMEM((rows, width), bf16),
        pltpu.VMEM((rows, width), bf16),
        pltpu.VMEM((rows, width), bf16),
    ] + JOIN_SEMS


N_JOIN = 9


def join_parts(part_ref, full_ref, scratch):
    got, mid, last, mine, send, recv, asend, arecv, local = scratch
    return Scatter(part_ref, got, mid, last, send, recv), Gather(mine, full_ref, asend, arecv, local)


class Sends:
    def __init__(self, messages, send, recv):
        self.copies = [
            remote(src, dst, send.at[i], recv.at[i], peer) for i, (src, dst, peer) in enumerate(messages)
        ]

    start = Exchange.start
    wait = Exchange.wait


def struct(shape, dtype):
    return jax.ShapeDtypeStruct(shape, dtype)


def column_sum(value):
    return jnp.sum(value, axis=0, keepdims=True)


def second_moment(value):
    return lax.rsqrt(jnp.mean(value * value, axis=1, keepdims=True) + EPSILON)


def attend(q, rows, state, k, v, code, bounds, factor):
    peak, total, acc = state
    scores = mm(k, q, NT) * factor
    seen = (code >= bounds[0:1]) & (code <= bounds[1:2])
    scores = jnp.where(seen, scores, NEG_FILL)
    new_peak = jnp.maximum(peak, jnp.max(scores, axis=0, keepdims=True))
    terms = jnp.exp2(scores - new_peak)
    shrink = jnp.exp2(peak - new_peak)
    total = total * shrink + jnp.sum(terms, axis=0, keepdims=True)
    acc = acc * shrink + mm(v, terms.astype(bf16), TN)
    return new_peak, total, acc


def along_y(shift):
    t = lax.axis_index("tensor")
    return {"tensor": 4 * (t // 4) + (t + shift) % 4}


def weights_along_y(weight_refs, n_rows, results, send, recv):
    messages = []
    for result, shift in zip(results, (1, 3)):
        at = 0
        for ref, count in zip(weight_refs, n_rows):
            messages.append((ref, result.at[pl.ds(at, count)], along_y(shift)))
            at += count
    return Sends(messages, send, recv)


def attend_forward(k, v, q, codes, bounds, out_weight, layer_input, gain, weights, number):
    _, tok, size = q.shape
    n_rows = [w.shape[0] for w in weights]
    stream, count = N_DP * tok, 2 * tok
    _, rows, width = layer_input.shape
    factor = size ** (-0.5) * math.log2(math.e)

    def kernel(k_ref, v_ref, q_ref, code_ref, bound_ref, w_ref, x_ref, gain_ref, *refs):
        weight_refs, outs, scratch = refs[:2], refs[2:13], refs[13:]
        keys_ref, values_ref, pair_ref, wide_ref, log_ref, heads_ref, full_ref, middle_ref, stats_ref = outs[:9]
        keys, values, pair, own_out, heads, part = scratch[:6]
        send, recv, local = scratch[6:9]
        swap_sems, out_sems, store_sems, weight_sems = scratch[9:12], scratch[12:14], scratch[14], scratch[15:17]
        join = scratch[17:]
        me = lax.axis_index("dp")
        core = lax.rem(me, 2)
        greet(tensor_peers() + dp_peers())
        both = weights_along_y(weight_refs, n_rows, outs[9:], *weight_sems)
        both.start()
        swap = Swap(q_ref, pair, *swap_sems)
        swap.start()

        def place(group):
            return pl.ds(pl.multiple_of(group * tok, tok), tok)

        def copies(step, head):
            return [
                remote(
                    own.at[head],
                    full.at[place(me)],
                    send.at[i, step],
                    recv.at[i, step],
                    {"dp": me ^ step},
                )
                for i, (own, full) in enumerate(((k_ref, keys), (v_ref, values)))
            ]

        for step in ORDER:
            for copy in copies(step, core if step % 2 == 0 else 1 - core):
                copy.start()
        locals_ = [
            pltpu.make_async_copy(own.at[core], full.at[place(me)], local.at[i])
            for i, (own, full) in enumerate(((k_ref, keys), (v_ref, values)))
        ]
        for copy in locals_:
            copy.start()
        swap.wait()
        for copy in locals_:
            copy.wait()
        queries = pair[...].reshape(count, size)
        limits = bound_ref[...]

        def block(group, state):
            at = place(group)
            return attend(
                queries, at, state, keys[at], values[at], code_ref[at][:, 0:1], limits, factor
            )

        def arrived(step, state):
            group = me ^ step
            for i, (own, full) in enumerate(((k_ref, keys), (v_ref, values))):
                remote(
                    own.at[core], full.at[place(group)], send.at[i, step], recv.at[i, step], {"dp": group}
                ).wait_recv()
            return block(group, state)

        state = block(
            me,
            (
                jnp.full((1, count), NEG_FILL, f32),
                jnp.zeros((1, count), f32),
                jnp.zeros((size, count), f32),
            ),
        )
        peak, total, acc = lax.fori_loop(1, N_DP, arrived, state)
        out = (acc / total).T
        wide_ref[...] = out
        log_ref[...] = jnp.broadcast_to(peak + jnp.log2(total), (8, count))
        own_out[...] = out.astype(bf16).reshape(2, tok, size)
        across = remote(
            own_out.at[1 - core], heads.at[core], out_sems[0].at[0], out_sems[1].at[0], {"dp": me ^ 1}
        )
        across.start()
        heads[core] = own_out[core]
        stores = [
            pltpu.make_async_copy(keys, keys_ref, store_sems.at[0]),
            pltpu.make_async_copy(values, values_ref, store_sems.at[1]),
            pltpu.make_async_copy(pair, pair_ref, store_sems.at[2]),
        ]
        for store in stores:
            store.start()
        across.wait_recv()
        heads_ref[:, 0:size] = heads[0]
        heads_ref[:, size : 2 * size] = heads[1]

        def project(j, carry):
            cols = pl.ds(pl.multiple_of(j * 512, 512), 512)
            value = mm(heads_ref[...], w_ref[:, cols])
            part[:, :, cols] = value.reshape(N_T, rows, 512).astype(bf16)
            return carry

        lax.fori_loop(0, width // 512, project, 0)
        scatter, gather = direct_parts(part, full_ref, join)
        scatter.start()
        resid = x_ref[lax.axis_index("tensor")].astype(f32)
        attn_out = scatter.total()
        middle = resid + attn_out
        gather.start(middle * second_moment(middle) * gain_ref[...])
        middle_ref[...] = middle
        stats_ref[0:1] = column_sum(resid * resid)
        stats_ref[1:2] = column_sum(attn_out * attn_out)
        stats_ref[2:3] = column_sum(middle * middle)
        for step in ORDER:
            for copy in copies(step, core):
                copy.wait_send()
        across.wait_send()
        scatter.wait_send()
        for store in stores:
            store.wait()
        gather.wait()
        both.wait()

    return pl.pallas_call(
        kernel,
        out_shape=(
            struct((stream, size), bf16),
            struct((stream, size), bf16),
            struct(q.shape, bf16),
            struct((count, size), f32),
            struct((8, count), f32),
            struct((tok, 2 * size), bf16),
            struct(layer_input.shape, bf16),
            struct((rows, width), f32),
            struct((8, width), f32),
            struct((sum(n_rows), width), bf16),
            struct((sum(n_rows), width), bf16),
        ),
        in_specs=[HBM] * 3 + [VMEM] * 5 + [HBM] * 2,
        out_specs=(HBM,) * 3 + (VMEM,) * 3 + (HBM,) + (VMEM,) * 2 + (HBM,) * 2,
        scratch_shapes=[
            pltpu.VMEM((stream, size), bf16),
            pltpu.VMEM((stream, size), bf16),
            pltpu.VMEM(q.shape, bf16),
            pltpu.VMEM(q.shape, bf16),
            pltpu.VMEM(q.shape, bf16),
            pltpu.VMEM(layer_input.shape, bf16),
        ]
        + sems((2, N_DP), (2, N_DP), 2)
        + SWAP_SEMS
        + sems(1, 1, 3, 4, 4)
        + direct_scratch(rows, width),
        compiler_params=comm_params(number, LIMIT),
        name="attend_forward",
        cost_estimate=cost(85),
    )(k, v, q, codes, bounds, out_weight, layer_input, gain, *weights)


def sigmoid(x):
    return 1.0 / (1.0 + jnp.exp(-x))


TILE = 176
HALF = 256


def shared_expert(x_ref, up_ref, w_ref, vec_ref, part_ref, d_ref, grads_ref, row_ref, low_ref):
    hidden = w_ref.shape[0] // 3
    vec = vec_ref[...]
    gate = sigmoid(jnp.sum(x_ref[...].astype(f32) * vec, axis=1, keepdims=True))
    low_ref[...] = (gate * up_ref[...].astype(f32)).astype(bf16)
    part_ref[...] = jnp.zeros_like(part_ref)
    d_ref[...] = jnp.zeros_like(d_ref)

    def tile(i, carry):
        rows = [pl.ds(pl.multiple_of(i * TILE + k * hidden, 16), TILE) for k in range(3)]
        x, d_out = x_ref[...], low_ref[...]
        gate_part = mm(w_ref[rows[0]], x, NT)
        up_part = mm(w_ref[rows[1]], x, NT)
        sig = sigmoid(gate_part)
        act = gate_part * sig
        unit = (act * up_part).astype(bf16)
        d_unit = mm(w_ref[rows[2]], d_out, NT)
        d_gate = (d_unit * up_part * sig * (1.0 + gate_part * (1.0 - sig))).astype(bf16)
        d_up = (d_unit * act).astype(bf16)

        def block(j, carry):
            cols = pl.ds(pl.multiple_of(j * 256, 256), 256)
            xs, ds = x_ref[:, cols], low_ref[:, cols]
            part_ref[:, cols] += mm(unit, w_ref[rows[2], cols], TN)
            d_ref[:, cols] += mm(d_gate, w_ref[rows[0], cols], TN) + mm(d_up, w_ref[rows[1], cols], TN)
            for k, grad in enumerate((mm(d_gate, xs), mm(d_up, xs), mm(unit, ds))):
                grad = grad.astype(bf16)
                grads_ref[j, 0, rows[k]] = grad[:, :128]
                grads_ref[j, 1, rows[k]] = grad[:, 128:]
            return carry

        return lax.fori_loop(0, x.shape[1] // 256, block, carry)

    lax.fori_loop(0, hidden // TILE, tile, 0)
    total = part_ref[...]
    d_logit = jnp.sum(up_ref[...].astype(f32) * total, axis=1, keepdims=True) * gate * (1.0 - gate)
    part_ref[...] = gate * total
    d_ref[...] += d_logit * vec
    row_ref[...] = column_sum(d_logit * x_ref[...].astype(f32))


def routed_expert(x_ref, up_ref, w_ref, router_ref, own, acc, dgu_ref, unit_ref, router_grad_ref, before_far):
    groups, slots, width = x_ref.shape
    rows = groups * slots
    units = w_ref.shape[1] // 3

    def flat(ref):
        return ref[...].reshape(rows, width)

    logits = mm(router_ref[...], flat(x_ref), NT)
    terms = jnp.exp(logits - jnp.max(logits, axis=0, keepdims=True))
    probs = terms / jnp.sum(terms, axis=0, keepdims=True)
    gate = jnp.sum(probs * own, axis=0, keepdims=True)
    acc[...] = jnp.zeros_like(acc)

    def piece(step, d_gate_row):
        i = jnp.where(step < 2, step, 5 - step)

        @pl.when(step == 3)
        def _():
            before_far()

        gate_part = mm(w_ref[i, 0:units], flat(x_ref), NT)
        up_part = mm(w_ref[i, units : 2 * units], flat(x_ref), NT)
        raw = mm(w_ref[i, 2 * units : 3 * units], flat(up_ref), NT)
        sig = sigmoid(gate_part)
        act = gate_part * sig
        unit = (act * up_part).astype(bf16).astype(f32)
        d_unit = gate * raw
        gated = (unit * gate).astype(bf16)
        d_gate = (d_unit * up_part * sig * (1.0 + gate_part * (1.0 - sig))).astype(bf16)
        d_up = (d_unit * act).astype(bf16)
        unit_ref[i] = gated
        dgu_ref[i, 0:units] = d_gate
        dgu_ref[i, units : 2 * units] = d_up

        def block(j, carry):
            cols = pl.ds(pl.multiple_of(j * 512, 512), 512)
            acc[0:rows, cols] += mm(gated, w_ref[i, 2 * units : 3 * units, cols], TN)
            acc[rows : 2 * rows, cols] += mm(d_gate, w_ref[i, 0:units, cols], TN) + mm(
                d_up, w_ref[i, units : 2 * units, cols], TN
            )
            return carry

        lax.fori_loop(0, width // 512, block, 0)
        return d_gate_row + jnp.sum(unit * raw, axis=0, keepdims=True)

    d_gate_row = lax.fori_loop(0, GROUPS, piece, jnp.zeros((1, rows), f32))
    d_logits = (d_gate_row * gate * (own - probs)).astype(bf16)
    router_grad_ref[...] = mm(d_logits, flat(x_ref))
    acc[rows : 2 * rows] += mm(d_logits, router_ref[...], TN)


def experts(rows, ups, below, above, in_rows, out_rows, tokens, upstream, w_in, w_out, vec, router, own, number):
    _, slots, width = rows.shape
    tok = tokens.shape[0]
    hidden, units = w_out.shape[0], out_rows.shape[0]
    n_rows = GROUPS * slots
    half, rest = pl.ds(0, HALF), pl.ds(HALF, 3 * units - HALF)

    def kernel(*refs):
        (rows_ref, ups_ref, below_ref, above_ref, in_ref, out_ref, w_in_ref, w_out_ref), refs = refs[:8], refs[8:]
        (x_ref, up_ref, vec_ref, router_ref, own_ref), refs = refs[:5], refs[5:]
        (back_d, back_out, part_ref, d_ref, by_z_ref, row_ref, router_grad_ref, mine_ref, *sent_refs), refs = (
            refs[:11],
            refs[11:],
        )
        (weights, low, grads, xs, us, w, acc, dgu, unit, far, send_d, send_out), refs = refs[:12], refs[12:]
        row_sems, refs = [refs[3 * i : 3 * i + 3] for i in range(4)], refs[12:]
        rsend, rrecv, csend, crecv, loaded, stored = refs
        d = lax.axis_index("dp")
        core = lax.rem(d, 2)
        out_x = Rows(rows_ref, xs, *row_sems[0])
        out_u = Rows(ups_ref, us, *row_sems[1])
        in_d = Rows(send_d, back_d, *row_sems[2], back=True)
        in_out = Rows(send_out, back_out, *row_sems[3], back=True)
        greet([along_y(1), along_y(3), {"dp": d ^ 1}], out_x, in_d)
        out_x.start()
        out_u.start()
        relay = Sends(
            [
                (below_ref.at[half], w.at[2, half], along_y(1)),
                (above_ref.at[rest], w.at[2, rest], along_y(3)),
            ],
            rsend,
            rrecv,
        )
        relay.start()
        loads = [
            pltpu.make_async_copy(src, dst, loaded.at[i])
            for i, (src, dst) in enumerate(
                (
                    (w_in_ref, weights.at[pl.ds(0, 2 * hidden)]),
                    (w_out_ref, weights.at[pl.ds(2 * hidden, hidden)]),
                    (in_ref, w.at[0, pl.ds(0, 2 * units)]),
                    (out_ref, w.at[0, pl.ds(2 * units, units)]),
                    (above_ref, w.at[1]),
                    (below_ref, w.at[3]),
                )
            )
        ]
        for load in loads:
            load.start()
        for load in loads[:2]:
            load.wait()
        shared_expert(x_ref, up_ref, weights, vec_ref, part_ref, d_ref, grads, row_ref, low)
        cores = Sends(
            [(grads.at[chip, 1 - core], far.at[chip], {"dp": d ^ 1}) for chip in range(8)], csend, crecv
        )
        cores.start()
        for load in loads[2:]:
            load.wait()
        out_x.wait()
        out_u.wait()

        def before_far():
            for copy in relay.copies:
                copy.wait_recv()

        routed_expert(
            xs,
            us,
            w,
            router_ref,
            own_ref[:, 0:1],
            acc,
            dgu,
            unit,
            router_grad_ref,
            before_far,
        )
        send_d[...] = acc[n_rows : 2 * n_rows].astype(bf16).reshape(GROUPS, slots, width)
        in_d.start()
        send_out[...] = acc[0:n_rows].astype(bf16).reshape(GROUPS, slots, width)
        in_out.start()

        def block(j, carry):
            cols = pl.ds(pl.multiple_of(j * 256, 256), 256)
            x, up = xs[:, :, cols].reshape(n_rows, 256), us[:, :, cols].reshape(n_rows, 256)
            acc[0 : 2 * units, cols] = mm(dgu[0], x)
            acc[2 * units : 3 * units, cols] = mm(unit[0], up)
            for i in range(1, GROUPS):
                at = 3 * units * (i - 1)
                weights[at : at + 2 * units, cols] = mm(dgu[i], x).astype(bf16)
                weights[at + 2 * units : at + 3 * units, cols] = mm(unit[i], up).astype(bf16)
            return carry

        lax.fori_loop(0, width // 256, block, 0)
        stores = [pltpu.make_async_copy(acc.at[pl.ds(0, 3 * units)], mine_ref, stored.at[0])] + [
            pltpu.make_async_copy(weights.at[pl.ds(3 * units * i, 3 * units)], ref, stored.at[i + 1])
            for i, ref in enumerate(sent_refs)
        ]
        for store in stores:
            store.start()
        for chip in range(8):
            cores.copies[chip].wait_recv()
            far[chip] = (far[chip].astype(f32) + grads[chip, core].astype(f32)).astype(bf16)
            stores.append(pltpu.make_async_copy(far.at[chip], by_z_ref.at[chip], stored.at[4 + chip]))
            stores[-1].start()
        for copy in relay.copies + cores.copies:
            copy.wait_send()
        in_d.wait()
        in_out.wait()
        for store in stores:
            store.wait()

    row = struct(rows.shape, bf16)
    return pl.pallas_call(
        kernel,
        out_shape=(
            row,
            row,
            struct((tok, width), f32),
            struct((tok, width), f32),
            struct((8, 3 * hidden, 128), bf16),
            struct((1, width), f32),
            struct((router.shape[0], width), f32),
            struct((3 * units, width), f32),
        )
        + (struct((3 * units, width), bf16),) * 3,
        in_specs=[HBM] * 8 + [VMEM] * 5,
        out_specs=(HBM, HBM, VMEM, VMEM, HBM, VMEM, VMEM) + (HBM,) * 4,
        scratch_shapes=[
            pltpu.VMEM((3 * hidden, width), bf16),
            pltpu.VMEM((tok, width), bf16),
            pltpu.VMEM((8, 2, 3 * hidden, 128), bf16),
            pltpu.VMEM(rows.shape, bf16),
            pltpu.VMEM(rows.shape, bf16),
            pltpu.VMEM((GROUPS, 3 * units, width), bf16),
            pltpu.VMEM((2 * n_rows, width), f32),
            pltpu.VMEM((GROUPS, 2 * units, n_rows), bf16),
            pltpu.VMEM((GROUPS, units, n_rows), bf16),
            pltpu.VMEM((8, 3 * hidden, 128), bf16),
            pltpu.VMEM(rows.shape, bf16),
            pltpu.VMEM(rows.shape, bf16),
        ]
        + ROW_SEMS * 4
        + sems(2, 2, 8, 8, 6, 12),
        compiler_params=comm_params(number, 61 * 1024 * 1024),
        name="experts",
        cost_estimate=cost(115),
    )(rows, ups, below, above, in_rows, out_rows, w_in, w_out, tokens, upstream, vec, router, own)


def join_ffn(part, moe_part, cotangent, middle, gain, weights, number):
    _, rows, width = part.shape

    def kernel(part_ref, moe_ref, up_ref, middle_ref, gain_ref, w_ref, full_ref, out_ref, d_ref, sums_ref, got_ref, *scratch):
        d, z, _, _ = coordinates()
        greet(tensor_peers() + [{"dp": d ^ (4 * k)} for k in (1, 2, 3)])
        scatter, gather = direct_parts(part_ref, full_ref, scratch[:N_DIRECT])
        scatter.start()
        got, send, recv, local = scratch[2 * N_DIRECT :]
        side = Sends(
            [(w_ref.at[z ^ k], got.at[k], {"dp": d ^ (4 * k)}) for k in (1, 3, 2)], send, recv
        )
        side.start()
        load = pltpu.make_async_copy(w_ref.at[z], got.at[0], local.at[0])
        load.start()
        scatter_moe, gather_moe = direct_parts(moe_ref, out_ref, scratch[N_DIRECT : 2 * N_DIRECT])
        scatter_moe.start()
        middle = middle_ref[...]
        inv = second_moment(middle)
        d_normed = scatter.total()
        scaled = d_normed * gain_ref[...]
        d_middle = (
            up_ref[lax.axis_index("tensor")].astype(f32)
            + inv * scaled
            - middle * (inv * inv * inv) * jnp.mean(scaled * middle, axis=1, keepdims=True)
        )
        gather.start(d_middle)
        d_ref[...] = d_middle
        sums_ref[0:1] = column_sum(d_normed * middle * inv)
        moe_out = scatter_moe.total()
        output = middle_ref[...] + moe_out
        gather_moe.start(output)
        sums_ref[1:2] = column_sum(moe_out * moe_out)
        sums_ref[2:3] = column_sum(output * output)
        scatter.wait_send()
        scatter_moe.wait_send()
        gather.wait()
        gather_moe.wait()
        load.wait()
        side.wait()
        for half in range(2):
            total = got[0, half].astype(f32)
            for k in (1, 2, 3):
                total = total + got[k, half].astype(f32)
            got_ref[half] = total.astype(bf16)

    return pl.pallas_call(
        kernel,
        out_shape=(
            struct(part.shape, bf16),
            struct(part.shape, bf16),
            struct((rows, width), f32),
            struct((8, width), f32),
            struct(weights.shape[1:], weights.dtype),
        ),
        in_specs=[VMEM] * 5 + [HBM],
        out_specs=(HBM, HBM, VMEM, VMEM, VMEM),
        scratch_shapes=direct_scratch(rows, width) * 2
        + [pltpu.VMEM(weights.shape, weights.dtype)]
        + sems(3, 3, 1),
        compiler_params=comm_params(number, LIMIT),
        name="join_ffn",
        cost_estimate=cost(60),
    )(part, moe_part, cotangent, middle, gain, weights)


def attend_backward(d_attn, out_weight, heads, q, keys, values, codes, bounds, wide, logs, by_x, sent, number):
    n_sent = sent[0].shape[0]
    half, rest = pl.ds(0, HALF), pl.ds(HALF, n_sent - HALF)
    tok, width = d_attn.shape
    size = q.shape[2]
    stream, count = N_DP * tok, 2 * tok
    scale = size ** (-0.5)
    factor = scale * math.log2(math.e)

    def kernel(
        d_ref, w_ref, heads_ref, q_ref, k_ref, v_ref, code_ref, bound_ref, wide_ref, log_ref, x_ref, *refs
    ):
        (one_up, two_up, one_down), refs = refs[:3], refs[3:]
        (sums_ref, pair_ref, out_ref, shared_ref, below_ref, above_ref), scratch = refs[:6], refs[6:]
        d_heads, d_pair, made, got, d_query, out_part, out_got, x_got, up, down, far = scratch[:11]
        send, recv, osend, orecv, small_send, small_recv, fsend, frecv, wsend, wrecv, loaded = scratch[11:]
        me = lax.axis_index("dp")
        core, x_index = lax.rem(me, 2), lax.rem(me // 2, 2)
        greet(dp_peers() + [along_y(1), along_y(3)])
        first = Sends(
            [
                (two_up.at[half], far.at[half], along_y(1)),
                (two_up.at[rest], far.at[rest], along_y(3)),
            ],
            fsend,
            frecv,
        )
        first.start()
        loads = [
            pltpu.make_async_copy(one_up, up, loaded.at[0]),
            pltpu.make_async_copy(one_down, down, loaded.at[1]),
        ]
        for load in loads:
            load.start()
        second = Sends(
            [(up, below_ref, along_y(1)), (down, above_ref, along_y(3))], wsend, wrecv
        )
        along_x = remote(
            x_ref.at[1 - x_index], x_got, small_send.at[0], small_recv.at[0], {"dp": me ^ 2}
        )
        along_x.start()
        value = mm(d_ref[...], w_ref[...], NT).astype(bf16)
        d_heads[0] = value[:, 0:size]
        d_heads[1] = value[:, size : 2 * size]
        swap = remote(
            d_heads.at[1 - core], d_pair.at[core], small_send.at[1], small_recv.at[1], {"dp": me ^ 1}
        )
        swap.start()
        d_pair[core] = d_heads[core]
        for d in range(N_DP):
            out_part[d] = mm(d_ref[:, d * 128 : (d + 1) * 128], heads_ref[...], TN).astype(bf16)
        outs = [
            remote(out_part.at[me ^ k], out_got.at[k], osend.at[k], orecv.at[k], {"dp": me ^ k})
            for k in range(1, N_DP)
        ]
        swap.wait_recv()
        q, d_out = q_ref[...].reshape(count, size), d_pair[...].reshape(count, size)
        lowest, highest = bound_ref[0:1], bound_ref[1:2]
        log = log_ref[0:1]
        delta = jnp.sum((wide_ref[...] * d_out.astype(f32)).T, axis=0, keepdims=True)

        def send_to(step):
            return remote(
                made.at[me ^ step], got.at[step], send.at[step], recv.at[step], {"dp": me ^ step}
            )

        def block(group, acc):
            at = pl.ds(pl.multiple_of(group * tok, tok), tok)
            k = k_ref[at]
            scores = mm(k, q, NT) * factor
            code = code_ref[at][:, 0:1]
            seen = (code >= lowest) & (code <= highest)
            probs = jnp.where(seen, jnp.exp2(scores - log), 0.0)
            d_probs = mm(v_ref[at], d_out, NT)
            d_scores = (probs * (d_probs - delta)).astype(bf16)
            made[group, 0:tok] = (mm(d_scores, q) * scale).astype(bf16)
            made[group, tok : 2 * tok] = mm(probs.astype(bf16), d_out).astype(bf16)
            return acc + mm(k, d_scores, TN)

        def other(step, acc):
            acc = block(me ^ step, acc)
            send_to(step).start()
            return acc

        acc = lax.fori_loop(1, N_DP, other, jnp.zeros((size, count), f32))
        for copy in outs:
            copy.start()
        acc = block(me, acc)
        for load in loads:
            load.wait()
        for copy in first.copies:
            copy.wait_recv()

        def add(rows, target):
            def step(j, carry):
                cols = pl.ds(pl.multiple_of(j * 512, 512), 512)
                target[rows, cols] = (target[rows, cols].astype(f32) + far[rows, cols].astype(f32)).astype(bf16)
                return carry

            lax.fori_loop(0, width // 512, step, 0)

        add(half, up)
        add(rest, down)
        second.start()
        d_query[...] = (acc.T * scale).astype(bf16).reshape(2, tok, size)
        back = remote(
            d_query.at[1 - core], pair_ref.at[core], small_send.at[2], small_recv.at[2], {"dp": me ^ 1}
        )
        back.start()
        pair_ref[core] = d_query[core]
        got[0] = made[me]
        along_x.wait_recv()
        shared_ref[...] = x_got[...].astype(f32)
        for k in range(1, N_DP):
            send_to(k).wait_recv()
        for head in range(2):
            total = jnp.zeros((2 * tok, size), f32)
            for k in range(N_DP // 2):
                total = total + got[2 * k + (core + head) % 2].astype(f32)
            sums_ref[head] = total
        total = out_part[me].astype(f32)
        for k, copy in enumerate(outs):
            copy.wait_recv()
            total = total + out_got[k + 1].astype(f32)
        out_ref[...] = total
        back.wait_recv()
        for copy in [along_x, swap, back] + outs + first.copies:
            copy.wait_send()
        second.wait()
        for k in range(1, N_DP):
            send_to(k).wait_send()

    return pl.pallas_call(
        kernel,
        out_shape=(
            struct((2, 2 * tok, size), f32),
            struct(q.shape, bf16),
            struct((width // N_DP, 2 * size), f32),
            struct(by_x.shape[1:], f32),
            struct((n_sent, width), bf16),
            struct((n_sent, width), bf16),
        ),
        in_specs=[VMEM] * 10 + [HBM] * 4,
        out_specs=(VMEM,) * 4 + (HBM,) * 2,
        scratch_shapes=[
            pltpu.VMEM(q.shape, bf16),
            pltpu.VMEM(q.shape, bf16),
            pltpu.VMEM((N_DP, 2 * tok, size), bf16),
            pltpu.VMEM((N_DP, 2 * tok, size), bf16),
            pltpu.VMEM(q.shape, bf16),
            pltpu.VMEM((N_DP, 128, 2 * size), bf16),
            pltpu.VMEM((N_DP, 128, 2 * size), bf16),
            pltpu.VMEM(by_x.shape[1:], bf16),
        ]
        + [pltpu.VMEM((n_sent, width), bf16)] * 3
        + sems(N_DP, N_DP, N_DP, N_DP, 3, 3, 2, 2, 2, 2, 2),
        compiler_params=comm_params(number, LIMIT),
        name="attend_backward",
        cost_estimate=cost(65),
    )(d_attn, out_weight, heads, q, keys, values, codes, bounds, wide, logs, by_x, *sent)


def join_tail(part, layer_input, d_middle, gain, normed, d_proj, pack, own_grads, received, number):
    _, rows, width = part.shape
    small = pack.shape[1]
    wide = d_proj.shape[1]
    n_in, n_out = 8 + len(received), 6
    n_expert = own_grads.shape[0]
    units = n_expert // 3

    def kernel(*refs):
        part_ref, x_ref, d_ref, gain_ref, n_ref, proj_ref, pack_ref, own_grads_ref = refs[:8]
        received_refs = refs[8:n_in]
        full_ref, qkv_ref, one_ref, both_ref, in_ref, out_ref = refs[n_in : n_in + n_out]
        scratch = refs[n_in + n_out :]
        join, scratch = scratch[:N_JOIN], scratch[N_JOIN:]
        own, few, mine, more, send, recv, tsend, trecv = scratch[:8]
        qbuf, qgot, qsum, qin, csend, crecv, ksend, krecv = scratch[8:16]
        acc, others, lsem, osem = scratch[16:]
        me, t = lax.axis_index("dp"), lax.axis_index("tensor")
        core, chip = me % 2, me // 2
        greet(tensor_peers() + dp_peers())
        scatter, gather = join_parts(part_ref, full_ref, join)
        scatter.start()
        loads = [pltpu.make_async_copy(own_grads_ref, acc, lsem.at[0])] + [
            pltpu.make_async_copy(r, others.at[i], lsem.at[i + 1]) for i, r in enumerate(received_refs)
        ]
        for load in loads:
            load.start()
        across = []
        for c in range(8):
            for side in range(2):
                cols = slice((2 * c + side) * 128, (2 * c + side + 1) * 128)
                qbuf[c, side] = mm(n_ref[:, cols], proj_ref[...], TN).astype(bf16)
            across.append(
                remote(qbuf.at[c, 1 - core], qgot.at[c], csend.at[c], crecv.at[c], {"dp": me ^ 1})
            )
            across[-1].start()
        for c in range(8):
            across[c].wait_recv()
            qsum[c] = (qbuf[c, core].astype(f32) + qgot[c].astype(f32)).astype(bf16)
        chips = [
            remote(
                qsum.at[chip ^ k], qin.at[k], ksend.at[k], krecv.at[k], {"dp": me ^ (2 * k)}
            )
            for k in range(1, 8)
        ]
        for copy in chips:
            copy.start()
        resid = x_ref[t].astype(f32)
        inv = second_moment(resid)
        scatter.middle()
        d_normed = scatter.total()
        scaled = d_normed * gain_ref[...]
        gather.start(
            d_ref[...]
            + inv * scaled
            - resid * (inv * inv * inv) * jnp.mean(scaled * resid, axis=1, keepdims=True)
        )
        gain_grad = column_sum(d_normed * resid * inv)
        own[...] = pack_ref[...]
        for i in range(N_DP):
            own[i, small - 1 : small] = gain_grad[:, i * 128 : (i + 1) * 128]
        firsts = [
            remote(own.at[me ^ k], few.at[k], send.at[k], recv.at[k], {"dp": me ^ k})
            for k in range(1, N_DP)
        ]
        for copy in firsts:
            copy.start()
        gather.relay()
        value = own[me]
        for k in range(1, N_DP):
            firsts[k - 1].wait_recv()
            value = value + few[k]
        one_ref[...] = value
        mine[...] = value
        seconds = [
            remote(mine, more.at[k], tsend.at[k], trecv.at[k], {"tensor": t ^ k}) for k in range(1, N_T)
        ]
        for copy in seconds:
            copy.start()
        for load in loads:
            load.wait()

        def add(j, carry):
            cols = pl.ds(pl.multiple_of(j * 256, 256), 256)
            total = acc[:, cols]
            for i in range(len(received)):
                total = total + others[i, :, cols].astype(f32)
            acc[:, cols] = total
            return carry

        lax.fori_loop(0, width // 256, add, 0)
        stores = [
            pltpu.make_async_copy(acc.at[pl.ds(0, 2 * units)], in_ref, osem.at[0]),
            pltpu.make_async_copy(acc.at[pl.ds(2 * units, units)], out_ref, osem.at[1]),
        ]
        for store in stores:
            store.start()
        total = qsum[chip].astype(f32)
        for k in range(1, 8):
            chips[k - 1].wait_recv()
            total = total + qin[k].astype(f32)
        qkv_ref[...] = total
        for k in range(1, N_T):
            seconds[k - 1].wait_recv()
            value = value + more[k]
        both_ref[...] = value
        for copy in firsts + seconds + across + chips:
            copy.wait_send()
        scatter.wait_send()
        gather.wait()
        for store in stores:
            store.wait()

    return pl.pallas_call(
        kernel,
        out_shape=(
            struct(part.shape, bf16),
            struct((width // N_DP, wide), f32),
            struct((small, 128), f32),
            struct((small, 128), f32),
            struct((2 * units, width), f32),
            struct((units, width), f32),
        ),
        in_specs=[VMEM] * 7 + [HBM] * (n_in - 7),
        out_specs=(HBM, VMEM, VMEM, VMEM, HBM, HBM),
        scratch_shapes=join_scratch(rows, width)
        + [
            pltpu.VMEM((N_DP, small, 128), f32),
            pltpu.VMEM((N_DP, small, 128), f32),
            pltpu.VMEM((small, 128), f32),
            pltpu.VMEM((N_T, small, 128), f32),
        ]
        + sems(N_DP, N_DP, N_T, N_T)
        + [
            pltpu.VMEM((8, 2, 128, wide), bf16),
            pltpu.VMEM((8, 128, wide), bf16),
            pltpu.VMEM((8, 128, wide), bf16),
            pltpu.VMEM((8, 128, wide), bf16),
        ]
        + sems(8, 8, 8, 8)
        + [
            pltpu.VMEM((n_expert, width), f32),
            pltpu.VMEM((len(received), n_expert, width), bf16),
        ]
        + sems(n_in - 7, 2),
        compiler_params=comm_params(number, LIMIT),
        name="join_tail",
        cost_estimate=cost(55),
    )(part, layer_input, d_middle, gain, normed, d_proj, pack, own_grads, *received)


def doc_layout(lengths, token_index):
    doc_ends = jnp.cumsum(lengths)
    starts = doc_ends - lengths
    seq_ids = jnp.sum((token_index[:, None] >= doc_ends[None, :]).astype(jnp.int32), axis=1)
    member = seq_ids[:, None] == jnp.arange(lengths.shape[0], dtype=jnp.int32)[None, :]
    begins = jnp.sum(jnp.where(member, starts[None, :], 0), axis=1)
    offsets = token_index - begins
    return (seq_ids, offsets, offsets // DBLOCK)


def rope_tables(offsets, head_dim):
    half_dim = head_dim // 2
    frequencies = jnp.exp(
        jnp.arange(half_dim, dtype=f32) * (-2.0 * math.log(THETA) / head_dim)
    )
    angles = offsets.astype(f32)[:, None] * frequencies[None, :]
    return (jnp.cos(angles)[:, None, :], jnp.sin(angles)[:, None, :])


def rotate(vectors, cosine, sine):
    half_dim = vectors.shape[-1] // 2
    front, back = vectors[..., :half_dim], vectors[..., half_dim:]
    return jnp.concatenate([front * cosine - back * sine, back * cosine + front * sine], axis=-1)


def dot(pattern, a, b):
    return jnp.einsum(pattern, a, b, preferred_element_type=f32)


def on_device(
    layer_input,
    doc_lengths,
    expert_ids,
    attn_gain,
    qkv_weight,
    qkv_bias,
    out_weight,
    ffn_gain,
    router_weight,
    shared_gate,
    shared_in,
    shared_out,
    expert_in,
    expert_out,
    cotangent,
):
    tok, width = layer_input.shape
    dp, tn = lax.axis_index("dp"), lax.axis_index("tensor")
    experts_n = router_weight.shape[1]
    head_dim = qkv_weight.shape[3]
    stream = tok * N_DP
    part_rows = tok // N_T
    score_scale = head_dim ** (-0.5)
    eff = expert_out.shape[1]

    in_rows = expert_in[0].transpose(1, 2, 0).reshape(2 * eff, width)

    hot = jnp.sum(
        (expert_ids[:, :, None] == jnp.arange(experts_n, dtype=jnp.int32)[None, None, :]).astype(f32),
        axis=1,
    )
    before = (jnp.arange(tok)[:, None] > jnp.arange(tok)[None, :]).astype(bf16)
    rank = dot("ts,se->te", before, hot.astype(bf16))
    place = jnp.where(hot > 0, rank, -1.0).astype(jnp.int32).T
    _, offset = route_plane()
    served = lax.dynamic_slice_in_dim(place, GROUPS * ((dp // 4) ^ offset), GROUPS, 0)
    places = (
        (served[:, None, :] == jnp.arange(SLOTS, dtype=jnp.int32)[None, :, None])
        .astype(bf16)
        .reshape(GROUPS * SLOTS, tok)
    )
    returned = lax.dynamic_index_in_dim(place.reshape(GROUPS, 4, tok), offset, 1, keepdims=False)
    places_back = (
        (returned[:, None, :] == jnp.arange(SLOTS, dtype=jnp.int32)[None, :, None])
        .astype(bf16)
        .reshape(GROUPS * SLOTS, tok)
    )
    by_group = (GROUPS, SLOTS, width)
    up_send = dot("rt,td->rd", places, cotangent).astype(bf16)

    local_index = dp * tok + jnp.arange(tok, dtype=jnp.int32)
    pair_index = (dp // 2) * (2 * tok) + jnp.arange(2 * tok, dtype=jnp.int32)
    every_index = jnp.arange(stream, dtype=jnp.int32)
    _, pos_local, _ = doc_layout(doc_lengths, local_index)
    seq_pair, _, blk_pair = doc_layout(doc_lengths, pair_index)
    seq_all, _, blk_all = doc_layout(doc_lengths, every_index)
    codes = jnp.broadcast_to((seq_all * CODE + blk_all)[:, None], (stream, 128))
    bounds = jnp.stack([seq_pair * CODE, seq_pair * CODE + blk_pair] + [seq_pair] * 6)
    cosine, sine = rope_tables(pos_local, head_dim)
    residual = layer_input.astype(f32)
    inv_first = lax.rsqrt(jnp.mean(residual * residual, axis=1, keepdims=True) + EPSILON)
    normed_one = (residual * inv_first * attn_gain).astype(bf16)
    projected = dot("td,dshe->tshe", normed_one, qkv_weight) + qkv_bias.astype(f32)[None]
    q_own = rotate(projected[:, 0], cosine, sine).astype(bf16).transpose(1, 0, 2)
    k_own = rotate(projected[:, 1], cosine, sine).astype(bf16).transpose(1, 0, 2)
    v_own = projected[:, 2].astype(bf16).transpose(1, 0, 2)
    by_slice = (N_T, part_rows, width)
    out_flat = out_weight.reshape(2 * head_dim, width)
    keys, values, queries, wide, logs, heads_out, normed_two, middle, stats_one, *neighbours = attend_forward(
        k_own,
        v_own,
        q_own,
        codes,
        bounds,
        out_flat,
        layer_input.reshape(by_slice),
        ffn_gain.reshape(1, width),
        [in_rows, expert_out[0]],
        1,
    )
    normed_two = normed_two.reshape(tok, width)

    row_send = dot("rt,td->rd", places, normed_two).astype(bf16)
    own_expert = jnp.broadcast_to(
        (jnp.arange(experts_n, dtype=jnp.int32) == dp).astype(f32)[:, None], (experts_n, 128)
    )
    back_grads, back_out, mixed, shared_d_normed, got, gate_vec_part, router_part, own_grads, *sent = experts(
        row_send.reshape(by_group),
        up_send.reshape(by_group),
        *neighbours,
        in_rows,
        expert_out[0],
        normed_two,
        cotangent,
        shared_in.transpose(1, 2, 0).reshape(-1, width),
        shared_out,
        shared_gate.astype(f32).reshape(1, width),
        router_weight.T,
        own_expert,
        5,
    )

    by_z = got.reshape((4, 2) + got.shape[1:])

    def combine(rows):
        return dot("rt,rd->td", places_back, rows.reshape(-1, width))

    d_normed_part = (shared_d_normed + combine(back_grads)).astype(bf16)
    moe_part = (mixed + combine(back_out)).astype(bf16)
    d_attn, output, d_middle, stats_two, by_x = join_ffn(
        d_normed_part.reshape(by_slice),
        moe_part.reshape(by_slice),
        cotangent.reshape(by_slice),
        middle,
        ffn_gain.reshape(1, width),
        by_z,
        7,
    )
    d_attn = d_attn.reshape(tok, width)

    d_keys, d_queries, outproj_grad, shared_far, *received = attend_backward(
        d_attn, out_flat, heads_out, queries, keys, values, codes, bounds, wide, logs, by_x, sent, 9
    )
    shared_grads = lax.dynamic_index_in_dim(by_x, (dp // 2) % 2, 0, keepdims=False).astype(f32) + shared_far
    n_shared = shared_in.shape[2]

    cosine, sine = cosine[:, 0], sine[:, 0]
    d_proj = jnp.concatenate(
        [rotate(d_queries[h].astype(f32), cosine, -sine) for h in range(2)]
        + [rotate(d_keys[h, :tok], cosine, -sine) for h in range(2)]
        + [d_keys[h, tok:] for h in range(2)],
        axis=1,
    ).astype(bf16)
    d_normed_one = dot(
        "tshe,dshe->td", d_proj.reshape(tok, 3, 2, head_dim), qkv_weight
    ).astype(bf16)
    bias_part = jnp.sum(d_proj.astype(f32), axis=0)

    def slices(row):
        return row.reshape(-1, N_DP, 128).transpose(1, 0, 2)

    five = jnp.sum(jnp.concatenate([stats_one[:3], stats_two[1:3]]), axis=1)
    pack = jnp.concatenate(
        [
            slices(router_part),
            slices(gate_vec_part[0]),
            slices(stats_two[0]),
            jnp.broadcast_to(jnp.pad(five, (0, 123))[None, None], (N_DP, 1, 128)),
            jnp.pad(
                bias_part.reshape(6, N_DP, 8).transpose(1, 0, 2).reshape(N_DP, 1, 48),
                ((0, 0), (0, 4), (0, 80)),
            ),
        ],
        axis=1,
    )
    input_grad, qkv_grad, over_dp, over_both, expert_in_grad, expert_out_grad = join_tail(
        d_normed_one.reshape(by_slice),
        layer_input.reshape(by_slice),
        d_middle,
        attn_gain.reshape(1, width),
        normed_one,
        d_proj,
        pack,
        own_grads,
        received,
        10,
    )
    bias_grad = over_dp[19, :48].reshape(3, 2, 8)
    rms_stats = jnp.sqrt(over_both[18, :5] / (stream * width))

    return (
        output.reshape(tok, width),
        input_grad.reshape(tok, width).astype(f32),
        qkv_grad.reshape(width // N_DP, 3, 2, head_dim),
        bias_grad,
        outproj_grad.T.reshape(2, head_dim, width // N_DP),
        over_both[23],
        over_both[17],
        over_both[:16].T,
        over_both[16],
        shared_grads[: 2 * n_shared].reshape(2, n_shared, -1).transpose(2, 0, 1),
        shared_grads[2 * n_shared :],
        expert_in_grad.reshape(2, eff, width).transpose(2, 0, 1)[None],
        expert_out_grad[None],
        rms_stats,
    )


def solution(mesh):
    in_specs = (
        P("dp", None),
        P(),
        P("dp", None),
        P(),
        P(None, None, "tensor", None),
        P(None, "tensor", None),
        P("tensor", None, None),
        P(),
        P(),
        P(),
        P(None, None, "tensor"),
        P("tensor", None),
        P("dp", None, None, "tensor"),
        P("dp", "tensor", None),
        P("dp", None),
    )
    out_specs = (
        P("dp", None),
        P("dp", None),
        P("dp", None, "tensor", None),
        P(None, "tensor", "dp"),
        P("tensor", None, "dp"),
        P("dp"),
        P("dp"),
        P("dp", None),
        P("dp"),
        P("dp", None, "tensor"),
        P("tensor", "dp"),
        P("dp", None, None, "tensor"),
        P("dp", "tensor", None),
        P(),
    )
    return jax.shard_map(
        on_device, mesh=mesh, in_specs=in_specs, out_specs=out_specs, check_vma=False
    )
```

time: 574 us -> 489 us (0.85); the launches traced: 564 us -> 486 us
  Pallas kernels: 457 us -> 431 us
  local copies, waits for them, and re-layouts: 42.2 us -> 21.7 us
  other arithmetic: 29.8 us -> 14.9 us
  starting transfers between devices: 13 us -> 0 us
    pallas_call x11 -> x4, Pallas kernels: 381 us -> 354 us  [the longest x1 128 us: experts(): pl.pallas_call(kernel, out_shape=(row, row, struct((tok, width), f32), st...]
    ppermute x6 -> x0, starting transfers between devices: 13 us -> none  [permute(): return lax.ppermute(x, 'tensor', [(i, i ^ bits) for i in range(N_T)])]
    unnamed x103 -> x71, local copies, waits for them, and re-layouts: 17.7 us -> 8.62 us
    reshape x1 -> x0, local copies, waits for them, and re-layouts: 8.07 us -> none  [on_device(): qkv_weight.reshape(width, -1)]
    convert_element_type x2, other arithmetic: 6.84 us -> 0.37 us  [the longest x1 0.37 us: on_device(): normed_one = (residual * inv_first * attn_gain).astype(bf16)]
    dot_general x11 -> x7, matrix products: 20.4 us -> 16.9 us  [dot(): return jnp.einsum(pattern, a, b, preferred_element_type=f32)]
  transfers between devices with their start and end apart: 6 -> 0, of which waited for: 0 -> 0; matrix products, arithmetic and copies ran while one was open for 6% -> 0% of each run, Pallas kernels for 43% -> 0%
where the time goes in v4:
time: 489 us; the launch traced here: 486 us
  Pallas kernels  431 us (88%)
  local copies, waits for them, and re-layouts  21.7 us (4%)
  matrix products  16.9 us (3%)
  other arithmetic  14.9 us (3%)
    pallas_call x1, Pallas kernels, experts(): pl.pallas_call(kernel, out_shape=(row, row, struct((tok, width), f32), st...  128 us
    pallas_call x1, Pallas kernels, attend_forward(): pl.pallas_call(kernel, out_shape=(struct((stream, size), bf16), struct((s...  90.9 us
    pallas_call x1, Pallas kernels, attend_backward(): pl.pallas_call(kernel, out_shape=(struct((2, 2 * tok, size), f32), struct...  80.7 us
    pallas_call x1, Pallas kernels, join_ffn(): pl.pallas_call(kernel, out_shape=(struct(part.shape, bf16), struct(part.s...  77.1 us
    pallas_call x1, Pallas kernels, join_tail(): pl.pallas_call(kernel, out_shape=(struct(part.shape, bf16), struct((width...  54.5 us
    dot_general x7, matrix products, dot(): return jnp.einsum(pattern, a, b, preferred_element_type=f32)  16.9 us

profile of v4, /device:TPU:1, one launch (start us, length us, event | category | flops | bytes accessed | tf_op | source)
XLA Modules:
  0.0 486.0 jit_solution(12875184094968685920)
XLA Ops:
  0.8 0.9 reduce-window.8
  1.7 0.7 bitcast_subtract_fusion
  2.4 1.7 fusion.14
  4.0 0.1 convert_reduce_fusion.4
  4.1 0.1 select_reduce_fusion.2
  4.3 0.1 eq.133
  4.3 0.7 convert_element_type.111
  5.0 0.1 convert_reduce_fusion.3
  5.1 0.1 select_reduce_fusion.1
  5.2 0.7 broadcast_in_dim.60.refs_12_
  5.9 1.3 reshape.395
  7.2 0.1 convert_reduce_fusion.2
  7.4 0.1 select_reduce_fusion
  7.5 0.7 convert_reduce_fusion.1
  8.2 0.1 fusion.23
  8.5 0.2 bitcast_compare_fusion
  8.7 0.1 iota_compare_fusion
  8.8 0.6 multiply_cosine_fusion
  9.4 0.4 fusion.16.refs_4_
  9.8 0.5 copy-done.32
  10.4 1.2 fusion.18
  11.7 0.3 subtract_convert_fusion
  12.0 0.2 maximum_bitcast_fusion
  12.2 0.8 copy-done.17
  13.0 2.4 convolution_convert_fusion
  15.4 3.4 broadcast_in_dim.57.code_ref
  18.8 90.9 %attend_forward.1 = (bf16[5120,128]{1,0:T(8,128)(2,1)S(1)}, bf16[5120,128]{1,0:T(8,128)(2,1)S(1)}, bf16[2,320,128]{2,1,0:T(8,128)(2,1)S(1)}, f32[640,128]{1,0:T(...) custom-call(bf16[2,320,128]{2,1,0:T(8,128)(2,1)S(1)} %get-tuple-elem, ...), custom_call_target="tpu_custom_call" | custom-call | bytes 255000000 | tf_op jit(solution)/shard_map/attend_forward/pallas_call | solution.py:573
  109.8 0.7 slice.119
  110.5 4.1 convolution_convert_fusion.1
  114.6 127.8 %experts.1 = (bf16[4,112,2048]{2,1,0:T(8,128)(2,1)}, bf16[4,112,2048]{2,1,0:T(8,128)(2,1)}, f32[320,2048]{1,0:T(8,128)}, f32[320,2048]{1,0:T(8,128)}, bf16[8,211...) custom-call(bf16[4,112,2048]{2,1,0:T(8,128)(2,1)} %bitcast.155, ...), custom_call_target="tpu_custom_call" | custom-call | bytes 345000000 | tf_op jit(solution)/shard_map/experts/pallas_call | solution.py:823
  242.4 3.5 fusion.10
  245.9 0.1 copy-done.22
  246.0 2.2 fusion.9
  248.2 77.1 %join_ffn.1 = (bf16[8,40,2048]{2,1,0:T(8,128)(2,1)S(1)}, bf16[8,40,2048]{2,1,0:T(8,128)(2,1)S(1)}, f32[40,2048]{1,0:T(8,128)S(1)}, f32[8,2048]{1,0:T(8,128)S(1)}, bf16[2,2112,128]{2,1,0:T(8,128)(2,1)S(1)}) custom-call(bf16[8,40,2048]{2,1,0:T(8,128)(2,1)S(1)} %bitcast.135, bf16[8,40,2048]{2,1,0:T(8,128)(2,1)} %bitcast.151, bf16[8,40,2048]{2,1,0:T(8,128)(2,1)} %bitcast.150, ...), custom_call_target="tpu_custom_call" | custom-call | bytes 180000000 | tf_op jit(solution)/shard_map/join_ffn/pallas_call | solution.py:906
  325.3 0.7 copy-done.7
  326.1 80.7 %attend_backward.1 = (f32[2,640,128]{2,1,0:T(8,128)S(1)}, bf16[2,320,128]{2,1,0:T(8,128)(2,1)S(1)}, f32[128,256]{1,0:T(8,128)S(1)}, f32[2112,128]{1,0:T(8,128)S(...) custom-call(bf16[320,2048]{1,0:T(8,128)(2,1)S(1)} %bitcast.140, bf16[256,2048]{1,0:T(8,128)(2,1)S(1)} %bitcast.137, ...), custom_call_target="tpu_custom_call" | custom-call | bytes 195000000 | tf_op jit(solution)/shard_map/attend_backward/pallas_call | solution.py:1058
  406.8 1.1 convert_add_fusion
  407.9 0.1 maximum_reduce_fusion
  408.0 0.8 copy.51
  408.8 0.7 bitcast_bitcast_fusion
  409.5 0.7 slice_bitcast_fusion.2
  410.2 1.5 fusion.42
  411.7 1.1 concatenate.19.refs_5_
  412.9 0.1 convert_reduce_fusion
  413.0 0.1 reshape.389
  413.1 0.1 copy.46
  413.1 0.1 copy.47
  413.2 0.1 concatenate.21.refs_6_
  413.3 0.8 slice.145
  414.1 0.9 slice.144
  415.0 0.9 convert_element_type.128
  415.9 3.4 fusion.11
  419.3 54.5 %join_tail.1 = (bf16[8,40,2048]{2,1,0:T(8,128)(2,1)S(1)}, f32[128,768]{1,0:T(8,128)S(1)}, f32[24,128]{1,0:T(8,128)S(1)}, f32[24,128]{1,0:T(8,128)S(1)}, f32[352,2048]{1,0:T(8,128)}, /*index=5*/f32[176,2048]{1,0:T(8,128)}) custom-call(bf16[8,40,2048]{2,1,0:T(8,128)(2,1)S(1)} %bitcast.141, bf16[8,40,2048]{2,1,0:T(8,128)(2,1)S(1)} %bitcast.134, ...), custom_call_target="tpu_custom_call" | custom-call | bytes 165000000 | tf_op jit(solution)/shard_map/join_tail/pallas_call | solution.py:1201
  473.8 1.0 copy-done.6
  474.9 0.5 sqrt_bitcast_fusion
  475.4 0.5 slice_bitcast_fusion.8
  475.9 0.6 slice_bitcast_fusion.6
  476.5 0.7 reshape_squeeze.3
  477.2 0.9 reshape.391
  478.1 3.3 bitcast_convert_fusion
  481.4 1.1 copy.74
  482.5 1.6 copy.75
  484.0 0.8 copy-done.23
  484.9 1.1 copy.76
  (85 shorter events, 0.5 us)
Async XLA Ops:
  0.6 8.8 %copy-start = (bf16[320,2048]{1,0:T(8,128)(2,1)S(1)}, bf16[320,2048]{1,0:T(8,128)(2,1)}, u32[]{:S(2)}) copy-start(bf16[320,2048]{1,0:T(8,128)(2,1)} %param.15) | copy-start | bytes 3932164
  0.7 8.8 %copy-start.16 = (f32[2048]{0:T(1024)S(1)}, f32[2048]{0:T(1024)}, u32[]{:S(2)}) copy-start(f32[2048]{0:T(1024)} %param.18) | copy-start | bytes 24580
  2.3 7.5 %copy-start.30 = (f32[64]{0:T(128)}, f32[64]{0:T(128)S(1)}, u32[]{:S(2)}) copy-start(f32[64]{0:T(128)S(1)} %multiply_exponential_fusion) | copy-start | bytes 772
  4.2 5.6 %copy-start.27 = (f32[320]{0:T(512)}, f32[320]{0:T(512)S(1)}, u32[]{:S(2)}) copy-start(f32[320]{0:T(512)S(1)} %subtract_convert_fusion.2) | copy-start | bytes 3844
  8.5 1.9 copy-start.32
  10.4 1.2 copy-start.18
  11.7 1.3 copy-start.17
  15.4 3.4 copy-start.2
  15.4 3.4 copy-start.3
  15.4 3.4 copy-start.15
  109.7 4.8 copy-start.4
  109.7 4.8 copy-start.5
  109.7 4.8 copy-start.9
  109.7 4.8 copy-start.11
  109.8 4.8 copy-start.13
  242.4 3.5 copy-start.21
  242.4 3.6 copy-start.22
  248.2 77.9 %copy-start.10 = (f32[640,128]{1,0:T(8,128)S(1)}, f32[640,128]{1,0:T(8,128)}, u32[]{:S(2)}) copy-start(f32[640,128]{1,0:T(8,128)} %copy-done.9) | copy-start | bytes 983044
  248.2 77.9 %copy-start.12 = (bf16[2,320,128]{2,1,0:T(8,128)(2,1)S(1)}, bf16[2,320,128]{2,1,0:T(8,128)(2,1)}, u32[]{:S(2)}) copy-start(bf16[2,320,128]{2,1,0:T(8,128)(2,1)} %copy-done.11) | copy-start | bytes 491524
  248.2 77.9 %copy-start.14 = (bf16[320,256]{1,0:T(8,128)(2,1)S(1)}, bf16[320,256]{1,0:T(8,128)(2,1)}, u32[]{:S(2)}) copy-start(bf16[320,256]{1,0:T(8,128)(2,1)} %copy-done.13) | copy-start | bytes 491524
  325.3 0.7 copy-start.7
  406.7 1.1 copy-start.26
  406.7 2.1 copy-start.25
  406.7 3.4 copy-start.28
  406.8 3.4 copy-start.31
  410.2 3.0 copy-start.24
  410.2 3.0 copy-start.29
  410.2 3.1 copy-start.19
  415.9 3.4 copy-start.1
  415.9 3.4 copy-start.8
  473.8 1.1 copy-start.6
  478.1 4.3 copy-start.20
  482.5 2.4 copy-start.23

commit v5 on v4

--- a/solution.py
+++ b/solution.py
@@ -22,6 +22,7 @@
 
 HBM = pl.BlockSpec(memory_space=pl.ANY)
 VMEM = pl.BlockSpec(memory_space=pltpu.VMEM)
+SMEM = pl.BlockSpec(memory_space=pltpu.SMEM)
 
 
 def greet(peers, *more):
@@ -68,6 +69,7 @@
 
 
 GROUPS = 4
+HALF = 256
 ORDER = (4, 12, 2, 5, 13, 3, 8, 6, 14, 9, 7, 15, 10, 11, 1)
 STEPS = (1, 3, 2, 4, 5, 7, 6)
 CHUNKS = ((0, 48), (48, 64))
@@ -160,17 +162,19 @@
     def inside(self):
         return pltpu.make_async_copy(self.x.at[self.mine], self.out.at[self.slot], self.local.at[0])
 
-    def start(self):
-        for c in range(len(CHUNKS)):
-            for j in range(GROUPS):
-
-                @pl.when(jnp.logical_not(self.is_own(j)))
-                def _():
-                    self.copy(j, c).start()
-
-        @pl.when(self.own)
+    def start_one(self, j):
+        @pl.when(jnp.logical_not(self.is_own(j)))
+        def _():
+            for c in range(len(CHUNKS)):
+                self.copy(j, c).start()
+
+        @pl.when(self.is_own(j))
         def _():
             self.inside().start()
+
+    def start(self):
+        for j in range(GROUPS):
+            self.start_one(j)
 
     def wait(self):
         @pl.when(self.own)
@@ -339,63 +343,34 @@
         self.across.wait_send()
 
 
-class Gather:
+class YGather:
     def __init__(self, mine, full_ref, send, recv, local):
         t = lax.axis_index("tensor")
-        self.mine = mine
-        self.across = remote(
-            mine, full_ref.at[t], send.at[0, 0], recv.at[0, 0], {"tensor": t ^ 4}
-        )
         self.first = [
             remote(mine, full_ref.at[t], send.at[0, k], recv.at[0, k], {"tensor": t ^ k})
             for k in (1, 3, 2)
         ]
         self.second = [
-            remote(
-                full_ref.at[t ^ 4],
-                full_ref.at[t ^ 4],
-                send.at[1, k],
-                recv.at[1, k],
-                {"tensor": t ^ k},
-            )
+            remote(full_ref.at[t ^ k], full_ref.at[t ^ k], send.at[1, k], recv.at[1, k], {"tensor": t ^ 4})
             for k in (1, 3, 2)
         ]
+        self.across = remote(mine, full_ref.at[t], send.at[1, 0], recv.at[1, 0], {"tensor": t ^ 4})
         self.own = pltpu.make_async_copy(mine, full_ref.at[t], local.at[0])
 
-    def start(self, value):
-        self.mine[...] = value.astype(bf16)
-        for copy in [self.across] + self.first + [self.own]:
+    def start(self):
+        for copy in self.first + [self.across, self.own]:
             copy.start()
 
     def relay(self):
-        self.across.wait_recv()
-        for copy in self.second:
-            copy.start()
+        for first, second in zip(self.first, self.second):
+            first.wait_recv()
+            second.start()
 
     def wait(self):
-        self.across.wait_send()
-        for copy in self.first + self.second + [self.own]:
+        for copy in self.first:
+            copy.wait_send()
+        for copy in self.second + [self.across, self.own]:
             copy.wait()
-
-
-JOIN_SEMS = sems((2, 4), (2, 4), (2, 4), (2, 4), 1)
-
-
-def join_scratch(rows, width):
-    return [
-        pltpu.VMEM((2, 4, rows, width), bf16),
-        pltpu.VMEM((rows, width), bf16),
-        pltpu.VMEM((rows, width), bf16),
-        pltpu.VMEM((rows, width), bf16),
-    ] + JOIN_SEMS
-
-
-N_JOIN = 9
-
-
-def join_parts(part_ref, full_ref, scratch):
-    got, mid, last, mine, send, recv, asend, arecv, local = scratch
-    return Scatter(part_ref, got, mid, last, send, recv), Gather(mine, full_ref, asend, arecv, local)
 
 
 class Sends:
@@ -420,10 +395,30 @@
     return lax.rsqrt(jnp.mean(value * value, axis=1, keepdims=True) + EPSILON)
 
 
-def attend(q, rows, state, k, v, code, bounds, factor):
+def codes_of(index, lengths_ref):
+    end, seq, begin = 0, 0, 0
+    for j in range(lengths_ref.shape[0]):
+        end = end + lengths_ref[j]
+        past = index >= end
+        seq = seq + past.astype(jnp.int32)
+        begin = jnp.where(past, end, begin)
+    return seq * CODE, seq * CODE + lax.shift_right_arithmetic(index - begin, DBLOCK.bit_length() - 1)
+
+
+def codes_of_keys(group, count, lengths_ref):
+    index = group * count + lax.broadcasted_iota(jnp.int32, (count, 1), 0)
+    return codes_of(index, lengths_ref)[1]
+
+
+def codes_of_queries(chip, count, lengths_ref):
+    index = chip * count + lax.broadcasted_iota(jnp.int32, (1, count), 1)
+    return codes_of(index, lengths_ref)
+
+
+def attend(q, state, k, v, code, bounds, factor):
     peak, total, acc = state
     scores = mm(k, q, NT) * factor
-    seen = (code >= bounds[0:1]) & (code <= bounds[1:2])
+    seen = (code >= bounds[0]) & (code <= bounds[1])
     scores = jnp.where(seen, scores, NEG_FILL)
     new_peak = jnp.maximum(peak, jnp.max(scores, axis=0, keepdims=True))
     terms = jnp.exp2(scores - new_peak)
@@ -448,24 +443,25 @@
     return Sends(messages, send, recv)
 
 
-def attend_forward(k, v, q, codes, bounds, out_weight, layer_input, gain, weights, number):
+def attend_forward(k, v, q, lengths, out_weight, layer_input, gain, weights, number):
     _, tok, size = q.shape
     n_rows = [w.shape[0] for w in weights]
+    half, rest = pl.ds(0, HALF), pl.ds(HALF, sum(n_rows) - HALF)
     stream, count = N_DP * tok, 2 * tok
     _, rows, width = layer_input.shape
     factor = size ** (-0.5) * math.log2(math.e)
 
-    def kernel(k_ref, v_ref, q_ref, code_ref, bound_ref, w_ref, x_ref, gain_ref, *refs):
-        weight_refs, outs, scratch = refs[:2], refs[2:13], refs[13:]
+    def kernel(k_ref, v_ref, q_ref, lengths_ref, w_ref, x_ref, gain_ref, *refs):
+        weight_refs, outs, scratch = refs[:2], refs[2:14], refs[14:]
         keys_ref, values_ref, pair_ref, wide_ref, log_ref, heads_ref, full_ref, middle_ref, stats_ref = outs[:9]
         keys, values, pair, own_out, heads, part = scratch[:6]
         send, recv, local = scratch[6:9]
         swap_sems, out_sems, store_sems, weight_sems = scratch[9:12], scratch[12:14], scratch[14], scratch[15:17]
-        join = scratch[17:]
+        relay_sems, join = scratch[17:19], scratch[19:]
         me = lax.axis_index("dp")
         core = lax.rem(me, 2)
         greet(tensor_peers() + dp_peers())
-        both = weights_along_y(weight_refs, n_rows, outs[9:], *weight_sems)
+        both = weights_along_y(weight_refs, n_rows, outs[9:11], *weight_sems)
         both.start()
         swap = Swap(q_ref, pair, *swap_sems)
         swap.start()
@@ -498,13 +494,12 @@
         for copy in locals_:
             copy.wait()
         queries = pair[...].reshape(count, size)
-        limits = bound_ref[...]
+        limits = codes_of_queries(me // 2, count, lengths_ref)
 
         def block(group, state):
             at = place(group)
-            return attend(
-                queries, at, state, keys[at], values[at], code_ref[at][:, 0:1], limits, factor
-            )
+            code = codes_of_keys(group, tok, lengths_ref)
+            return attend(queries, state, keys[at], values[at], code, limits, factor)
 
         def arrived(step, state):
             group = me ^ step
@@ -552,6 +547,17 @@
         lax.fori_loop(0, width // 512, project, 0)
         scatter, gather = direct_parts(part, full_ref, join)
         scatter.start()
+        for copy in both.copies:
+            copy.wait_recv()
+        below_ref, above_ref, far_ref = outs[9:]
+        relay = Sends(
+            [
+                (below_ref.at[half], far_ref.at[half], along_y(1)),
+                (above_ref.at[rest], far_ref.at[rest], along_y(3)),
+            ],
+            *relay_sems,
+        )
+        relay.start()
         resid = x_ref[lax.axis_index("tensor")].astype(f32)
         attn_out = scatter.total()
         middle = resid + attn_out
@@ -568,7 +574,9 @@
         for store in stores:
             store.wait()
         gather.wait()
-        both.wait()
+        for copy in both.copies:
+            copy.wait_send()
+        relay.wait()
 
     return pl.pallas_call(
         kernel,
@@ -582,11 +590,10 @@
             struct(layer_input.shape, bf16),
             struct((rows, width), f32),
             struct((8, width), f32),
-            struct((sum(n_rows), width), bf16),
-            struct((sum(n_rows), width), bf16),
-        ),
-        in_specs=[HBM] * 3 + [VMEM] * 5 + [HBM] * 2,
-        out_specs=(HBM,) * 3 + (VMEM,) * 3 + (HBM,) + (VMEM,) * 2 + (HBM,) * 2,
+        )
+        + (struct((sum(n_rows), width), bf16),) * 3,
+        in_specs=[HBM] * 3 + [SMEM] + [VMEM] * 3 + [HBM] * 2,
+        out_specs=(HBM,) * 3 + (VMEM,) * 3 + (HBM,) + (VMEM,) * 2 + (HBM,) * 3,
         scratch_shapes=[
             pltpu.VMEM((stream, size), bf16),
             pltpu.VMEM((stream, size), bf16),
@@ -597,12 +604,12 @@
         ]
         + sems((2, N_DP), (2, N_DP), 2)
         + SWAP_SEMS
-        + sems(1, 1, 3, 4, 4)
+        + sems(1, 1, 3, 4, 4, 2, 2)
         + direct_scratch(rows, width),
         compiler_params=comm_params(number, LIMIT),
         name="attend_forward",
         cost_estimate=cost(85),
-    )(k, v, q, codes, bounds, out_weight, layer_input, gain, *weights)
+    )(k, v, q, lengths, out_weight, layer_input, gain, *weights)
 
 
 def sigmoid(x):
@@ -610,7 +617,8 @@
 
 
 TILE = 176
-HALF = 256
+NOW = 256
+SOON = 96
 
 
 def shared_expert(x_ref, up_ref, w_ref, vec_ref, part_ref, d_ref, grads_ref, row_ref, low_ref):
@@ -654,93 +662,106 @@
     row_ref[...] = column_sum(d_logit * x_ref[...].astype(f32))
 
 
-def routed_expert(x_ref, up_ref, w_ref, router_ref, own, acc, dgu_ref, unit_ref, router_grad_ref, before_far):
-    groups, slots, width = x_ref.shape
-    rows = groups * slots
-    units = w_ref.shape[1] // 3
-
-    def flat(ref):
-        return ref[...].reshape(rows, width)
-
-    logits = mm(router_ref[...], flat(x_ref), NT)
-    terms = jnp.exp(logits - jnp.max(logits, axis=0, keepdims=True))
-    probs = terms / jnp.sum(terms, axis=0, keepdims=True)
-    gate = jnp.sum(probs * own, axis=0, keepdims=True)
-    acc[...] = jnp.zeros_like(acc)
-
-    def piece(step, d_gate_row):
-        i = jnp.where(step < 2, step, 5 - step)
-
-        @pl.when(step == 3)
-        def _():
-            before_far()
-
-        gate_part = mm(w_ref[i, 0:units], flat(x_ref), NT)
-        up_part = mm(w_ref[i, units : 2 * units], flat(x_ref), NT)
-        raw = mm(w_ref[i, 2 * units : 3 * units], flat(up_ref), NT)
-        sig = sigmoid(gate_part)
-        act = gate_part * sig
-        unit = (act * up_part).astype(bf16).astype(f32)
-        d_unit = gate * raw
-        gated = (unit * gate).astype(bf16)
-        d_gate = (d_unit * up_part * sig * (1.0 + gate_part * (1.0 - sig))).astype(bf16)
-        d_up = (d_unit * act).astype(bf16)
-        unit_ref[i] = gated
-        dgu_ref[i, 0:units] = d_gate
-        dgu_ref[i, units : 2 * units] = d_up
-
+class Routed:
+    def __init__(self, x_ref, up_ref, w_ref, router_ref, own, acc, dgu_ref, unit_ref, slope_ref, router_grad_ref):
+        groups, slots, self.width = x_ref.shape
+        self.rows, self.units = groups * slots, w_ref.shape[1] // 3
+        self.x_ref, self.up_ref, self.w_ref, self.router_ref, self.own = x_ref, up_ref, w_ref, router_ref, own
+        self.acc, self.dgu_ref, self.unit_ref, self.slope_ref = acc, dgu_ref, unit_ref, slope_ref
+        self.router_grad_ref = router_grad_ref
+
+    def flat(self, ref):
+        return ref[...].reshape(self.rows, self.width)
+
+    def start(self):
+        logits = mm(self.router_ref[...], self.flat(self.x_ref), NT)
+        terms = jnp.exp(logits - jnp.max(logits, axis=0, keepdims=True))
+        self.probs = terms / jnp.sum(terms, axis=0, keepdims=True)
+        self.gate = jnp.sum(self.probs * self.own, axis=0, keepdims=True)
+        self.acc[...] = jnp.zeros_like(self.acc)
+
+    def blocks(self, body):
         def block(j, carry):
-            cols = pl.ds(pl.multiple_of(j * 512, 512), 512)
-            acc[0:rows, cols] += mm(gated, w_ref[i, 2 * units : 3 * units, cols], TN)
-            acc[rows : 2 * rows, cols] += mm(d_gate, w_ref[i, 0:units, cols], TN) + mm(
-                d_up, w_ref[i, units : 2 * units, cols], TN
-            )
+            body(pl.ds(pl.multiple_of(j * 512, 512), 512))
             return carry
 
-        lax.fori_loop(0, width // 512, block, 0)
-        return d_gate_row + jnp.sum(unit * raw, axis=0, keepdims=True)
-
-    d_gate_row = lax.fori_loop(0, GROUPS, piece, jnp.zeros((1, rows), f32))
-    d_logits = (d_gate_row * gate * (own - probs)).astype(bf16)
-    router_grad_ref[...] = mm(d_logits, flat(x_ref))
-    acc[rows : 2 * rows] += mm(d_logits, router_ref[...], TN)
-
-
-def experts(rows, ups, below, above, in_rows, out_rows, tokens, upstream, w_in, w_out, vec, router, own, number):
-    _, slots, width = rows.shape
-    tok = tokens.shape[0]
+        lax.fori_loop(0, self.width // 512, block, 0)
+
+    def forward(self):
+        units, rows, w_ref = self.units, self.rows, self.w_ref
+
+        def piece(i, carry):
+            gate_part = mm(w_ref[i, 0:units], self.flat(self.x_ref), NT)
+            up_part = mm(w_ref[i, units : 2 * units], self.flat(self.x_ref), NT)
+            sig = sigmoid(gate_part)
+            act = gate_part * sig
+            gated = (act * up_part * self.gate).astype(bf16)
+            slope = self.gate * up_part * sig * (1.0 + gate_part * (1.0 - sig))
+            self.slope_ref[i, 0] = slope.astype(bf16)
+            self.slope_ref[i, 1] = (self.gate * act).astype(bf16)
+            self.unit_ref[i] = gated
+
+            def add(cols):
+                self.acc[0:rows, cols] += mm(gated, w_ref[i, 2 * units : 3 * units, cols], TN)
+
+            self.blocks(add)
+            return carry
+
+        lax.fori_loop(0, GROUPS, piece, 0)
+
+    def backward(self):
+        units, rows, w_ref = self.units, self.rows, self.w_ref
+
+        def piece(i, gated_d_gate):
+            raw = mm(w_ref[i, 2 * units : 3 * units], self.flat(self.up_ref), NT)
+            d_gate = (raw * self.slope_ref[i, 0].astype(f32)).astype(bf16)
+            d_up = (raw * self.slope_ref[i, 1].astype(f32)).astype(bf16)
+            self.dgu_ref[i, 0:units] = d_gate
+            self.dgu_ref[i, units : 2 * units] = d_up
+
+            def add(cols):
+                self.acc[rows : 2 * rows, cols] += mm(d_gate, w_ref[i, 0:units, cols], TN) + mm(
+                    d_up, w_ref[i, units : 2 * units, cols], TN
+                )
+
+            self.blocks(add)
+            return gated_d_gate + jnp.sum(self.unit_ref[i].astype(f32) * raw, axis=0, keepdims=True)
+
+        gated_d_gate = lax.fori_loop(0, GROUPS, piece, jnp.zeros((1, rows), f32))
+        d_logits = (gated_d_gate * (self.own - self.probs)).astype(bf16)
+        self.router_grad_ref[...] = mm(d_logits, self.flat(self.x_ref))
+        self.acc[rows : 2 * rows] += mm(d_logits, self.router_ref[...], TN)
+
+
+def experts(places, below, above, far_rows, in_rows, out_rows, tokens, upstream, w_in, w_out, vec, router, own, number):
+    slots = places.shape[1]
+    tok, width = tokens.shape
     hidden, units = w_out.shape[0], out_rows.shape[0]
     n_rows = GROUPS * slots
-    half, rest = pl.ds(0, HALF), pl.ds(HALF, 3 * units - HALF)
 
     def kernel(*refs):
-        (rows_ref, ups_ref, below_ref, above_ref, in_ref, out_ref, w_in_ref, w_out_ref), refs = refs[:8], refs[8:]
-        (x_ref, up_ref, vec_ref, router_ref, own_ref), refs = refs[:5], refs[5:]
+        (below_ref, above_ref, far_ref, in_ref, out_ref, w_in_ref, w_out_ref), refs = refs[:7], refs[7:]
+        (places_ref, x_ref, up_ref, vec_ref, router_ref, own_ref), refs = refs[:6], refs[6:]
         (back_d, back_out, part_ref, d_ref, by_z_ref, row_ref, router_grad_ref, mine_ref, *sent_refs), refs = (
             refs[:11],
             refs[11:],
         )
-        (weights, low, grads, xs, us, w, acc, dgu, unit, far, send_d, send_out), refs = refs[:12], refs[12:]
+        (weights, low, grads, xs, us, w, acc, dgu, unit, slope, far, send_d, send_out), refs = refs[:13], refs[13:]
         row_sems, refs = [refs[3 * i : 3 * i + 3] for i in range(4)], refs[12:]
-        rsend, rrecv, csend, crecv, loaded, stored = refs
+        csend, crecv, loaded, stored = refs
         d = lax.axis_index("dp")
         core = lax.rem(d, 2)
-        out_x = Rows(rows_ref, xs, *row_sems[0])
-        out_u = Rows(ups_ref, us, *row_sems[1])
+        out_x = Rows(send_d, xs, *row_sems[0])
+        out_u = Rows(send_out, us, *row_sems[1])
         in_d = Rows(send_d, back_d, *row_sems[2], back=True)
         in_out = Rows(send_out, back_out, *row_sems[3], back=True)
-        greet([along_y(1), along_y(3), {"dp": d ^ 1}], out_x, in_d)
-        out_x.start()
-        out_u.start()
-        relay = Sends(
-            [
-                (below_ref.at[half], w.at[2, half], along_y(1)),
-                (above_ref.at[rest], w.at[2, rest], along_y(3)),
-            ],
-            rsend,
-            rrecv,
-        )
-        relay.start()
+        greet([{"dp": d ^ 1}], out_x, in_d)
+        for j in range(GROUPS):
+            send_d[j] = mm(places_ref[j], x_ref[...]).astype(bf16)
+            out_x.start_one(j)
+        for j in range(GROUPS):
+            send_out[j] = mm(places_ref[j], up_ref[...]).astype(bf16)
+            out_u.start_one(j)
         loads = [
             pltpu.make_async_copy(src, dst, loaded.at[i])
             for i, (src, dst) in enumerate(
@@ -750,6 +771,7 @@
                     (in_ref, w.at[0, pl.ds(0, 2 * units)]),
                     (out_ref, w.at[0, pl.ds(2 * units, units)]),
                     (above_ref, w.at[1]),
+                    (far_ref, w.at[2]),
                     (below_ref, w.at[3]),
                 )
             )
@@ -766,28 +788,16 @@
         for load in loads[2:]:
             load.wait()
         out_x.wait()
+        routed = Routed(xs, us, w, router_ref, own_ref[:, 0:1], acc, dgu, unit, slope, router_grad_ref)
+        routed.start()
+
+        routed.forward()
         out_u.wait()
-
-        def before_far():
-            for copy in relay.copies:
-                copy.wait_recv()
-
-        routed_expert(
-            xs,
-            us,
-            w,
-            router_ref,
-            own_ref[:, 0:1],
-            acc,
-            dgu,
-            unit,
-            router_grad_ref,
-            before_far,
-        )
+        send_out[...] = acc[0:n_rows].astype(bf16).reshape(GROUPS, slots, width)
+        in_out.start()
+        routed.backward()
         send_d[...] = acc[n_rows : 2 * n_rows].astype(bf16).reshape(GROUPS, slots, width)
         in_d.start()
-        send_out[...] = acc[0:n_rows].astype(bf16).reshape(GROUPS, slots, width)
-        in_out.start()
 
         def block(j, carry):
             cols = pl.ds(pl.multiple_of(j * 256, 256), 256)
@@ -812,14 +822,14 @@
             far[chip] = (far[chip].astype(f32) + grads[chip, core].astype(f32)).astype(bf16)
             stores.append(pltpu.make_async_copy(far.at[chip], by_z_ref.at[chip], stored.at[4 + chip]))
             stores[-1].start()
-        for copy in relay.copies + cores.copies:
+        for copy in cores.copies:
             copy.wait_send()
+        in_out.wait()
         in_d.wait()
-        in_out.wait()
         for store in stores:
             store.wait()
 
-    row = struct(rows.shape, bf16)
+    row = struct((GROUPS, slots, width), bf16)
     return pl.pallas_call(
         kernel,
         out_shape=(
@@ -833,115 +843,86 @@
             struct((3 * units, width), f32),
         )
         + (struct((3 * units, width), bf16),) * 3,
-        in_specs=[HBM] * 8 + [VMEM] * 5,
+        in_specs=[HBM] * 7 + [VMEM] * 6,
         out_specs=(HBM, HBM, VMEM, VMEM, HBM, VMEM, VMEM) + (HBM,) * 4,
         scratch_shapes=[
             pltpu.VMEM((3 * hidden, width), bf16),
             pltpu.VMEM((tok, width), bf16),
             pltpu.VMEM((8, 2, 3 * hidden, 128), bf16),
-            pltpu.VMEM(rows.shape, bf16),
-            pltpu.VMEM(rows.shape, bf16),
+            pltpu.VMEM(row.shape, bf16),
+            pltpu.VMEM(row.shape, bf16),
             pltpu.VMEM((GROUPS, 3 * units, width), bf16),
             pltpu.VMEM((2 * n_rows, width), f32),
             pltpu.VMEM((GROUPS, 2 * units, n_rows), bf16),
             pltpu.VMEM((GROUPS, units, n_rows), bf16),
+            pltpu.VMEM((GROUPS, 2, units, n_rows), bf16),
             pltpu.VMEM((8, 3 * hidden, 128), bf16),
-            pltpu.VMEM(rows.shape, bf16),
-            pltpu.VMEM(rows.shape, bf16),
+            pltpu.VMEM(row.shape, bf16),
+            pltpu.VMEM(row.shape, bf16),
         ]
         + ROW_SEMS * 4
-        + sems(2, 2, 8, 8, 6, 12),
+        + sems(8, 8, 7, 12),
         compiler_params=comm_params(number, 61 * 1024 * 1024),
         name="experts",
         cost_estimate=cost(115),
-    )(rows, ups, below, above, in_rows, out_rows, w_in, w_out, tokens, upstream, vec, router, own)
-
-
-def join_ffn(part, moe_part, cotangent, middle, gain, weights, number):
+    )(below, above, far_rows, in_rows, out_rows, w_in, w_out, places, tokens, upstream, vec, router, own)
+
+
+def backward(
+    part, moe_part, cotangent, middle, gain, out_weight, heads, q, keys, values, wide, logs, lengths, weights, sent, number
+):
     _, rows, width = part.shape
-
-    def kernel(part_ref, moe_ref, up_ref, middle_ref, gain_ref, w_ref, full_ref, out_ref, d_ref, sums_ref, got_ref, *scratch):
-        d, z, _, _ = coordinates()
-        greet(tensor_peers() + [{"dp": d ^ (4 * k)} for k in (1, 2, 3)])
-        scatter, gather = direct_parts(part_ref, full_ref, scratch[:N_DIRECT])
+    tok, size = q.shape[1:]
+    stream, count = N_DP * tok, 2 * tok
+    scale = size ** (-0.5)
+    factor = scale * math.log2(math.e)
+    n_sent = sent[0].shape[0]
+    half, rest = pl.ds(0, HALF), pl.ds(HALF, n_sent - HALF)
+    now, later = pl.ds(0, NOW), pl.ds(NOW, n_sent - NOW)
+
+    def kernel(*refs):
+        (part_ref, moe_ref, up_in_ref, middle_ref, gain_ref, w_ref, heads_ref, q_ref, k_ref, v_ref), refs = (
+            refs[:10],
+            refs[10:],
+        )
+        (wide_ref, log_ref, lengths_ref, by_z_ref, one_up, two_up, one_down), refs = refs[:7], refs[7:]
+        (d_middle_ref, stats_ref, sums_ref, pair_ref, out_ref, by_x), refs = refs[:6], refs[6:]
+        (full_ref, below_ref, above_ref, up_ref, down_ref), refs = refs[:5], refs[5:]
+        (full, d_attn, out_slice, d_heads, d_pair, made, got, d_query, out_part, out_got), refs = refs[:10], refs[10:]
+        (z_got, up, down, far), refs = refs[:4], refs[4:]
+        direct, refs = refs[:N_DIRECT], refs[N_DIRECT:]
+        moe_scratch, refs = refs[:5], refs[5:]
+        send, recv, osend, orecv, small_send, small_recv, fsend, frecv, wsend, wrecv, loaded = refs[:11]
+        zsend, zrecv, gather_sems = refs[11], refs[12], refs[13:]
+        me, z, _, _ = coordinates()
+        t = lax.axis_index("tensor")
+        core = lax.rem(me, 2)
+        greet(dp_peers() + tensor_peers())
+        scatter, gather = direct_parts(part_ref, full, direct)
         scatter.start()
-        got, send, recv, local = scratch[2 * N_DIRECT :]
-        side = Sends(
-            [(w_ref.at[z ^ k], got.at[k], {"dp": d ^ (4 * k)}) for k in (1, 3, 2)], send, recv
-        )
-        side.start()
-        load = pltpu.make_async_copy(w_ref.at[z], got.at[0], local.at[0])
-        load.start()
-        scatter_moe, gather_moe = direct_parts(moe_ref, out_ref, scratch[N_DIRECT : 2 * N_DIRECT])
+        scatter_moe = Scatter(moe_ref, *moe_scratch)
         scatter_moe.start()
+        over_z = Sends(
+            [(by_z_ref.at[z ^ k], z_got.at[k], {"dp": me ^ (4 * k)}) for k in (1, 3, 2)], zsend, zrecv
+        )
+        over_z.start()
+        loads = [
+            pltpu.make_async_copy(one_up, up, loaded.at[0]),
+            pltpu.make_async_copy(one_down, down, loaded.at[1]),
+            pltpu.make_async_copy(by_z_ref.at[z], z_got.at[0], loaded.at[2]),
+        ]
+        for load in loads:
+            load.start()
         middle = middle_ref[...]
         inv = second_moment(middle)
         d_normed = scatter.total()
         scaled = d_normed * gain_ref[...]
         d_middle = (
-            up_ref[lax.axis_index("tensor")].astype(f32)
+            up_in_ref[t].astype(f32)
             + inv * scaled
             - middle * (inv * inv * inv) * jnp.mean(scaled * middle, axis=1, keepdims=True)
         )
         gather.start(d_middle)
-        d_ref[...] = d_middle
-        sums_ref[0:1] = column_sum(d_normed * middle * inv)
-        moe_out = scatter_moe.total()
-        output = middle_ref[...] + moe_out
-        gather_moe.start(output)
-        sums_ref[1:2] = column_sum(moe_out * moe_out)
-        sums_ref[2:3] = column_sum(output * output)
-        scatter.wait_send()
-        scatter_moe.wait_send()
-        gather.wait()
-        gather_moe.wait()
-        load.wait()
-        side.wait()
-        for half in range(2):
-            total = got[0, half].astype(f32)
-            for k in (1, 2, 3):
-                total = total + got[k, half].astype(f32)
-            got_ref[half] = total.astype(bf16)
-
-    return pl.pallas_call(
-        kernel,
-        out_shape=(
-            struct(part.shape, bf16),
-            struct(part.shape, bf16),
-            struct((rows, width), f32),
-            struct((8, width), f32),
-            struct(weights.shape[1:], weights.dtype),
-        ),
-        in_specs=[VMEM] * 5 + [HBM],
-        out_specs=(HBM, HBM, VMEM, VMEM, VMEM),
-        scratch_shapes=direct_scratch(rows, width) * 2
-        + [pltpu.VMEM(weights.shape, weights.dtype)]
-        + sems(3, 3, 1),
-        compiler_params=comm_params(number, LIMIT),
-        name="join_ffn",
-        cost_estimate=cost(60),
-    )(part, moe_part, cotangent, middle, gain, weights)
-
-
-def attend_backward(d_attn, out_weight, heads, q, keys, values, codes, bounds, wide, logs, by_x, sent, number):
-    n_sent = sent[0].shape[0]
-    half, rest = pl.ds(0, HALF), pl.ds(HALF, n_sent - HALF)
-    tok, width = d_attn.shape
-    size = q.shape[2]
-    stream, count = N_DP * tok, 2 * tok
-    scale = size ** (-0.5)
-    factor = scale * math.log2(math.e)
-
-    def kernel(
-        d_ref, w_ref, heads_ref, q_ref, k_ref, v_ref, code_ref, bound_ref, wide_ref, log_ref, x_ref, *refs
-    ):
-        (one_up, two_up, one_down), refs = refs[:3], refs[3:]
-        (sums_ref, pair_ref, out_ref, shared_ref, below_ref, above_ref), scratch = refs[:6], refs[6:]
-        d_heads, d_pair, made, got, d_query, out_part, out_got, x_got, up, down, far = scratch[:11]
-        send, recv, osend, orecv, small_send, small_recv, fsend, frecv, wsend, wrecv, loaded = scratch[11:]
-        me = lax.axis_index("dp")
-        core, x_index = lax.rem(me, 2), lax.rem(me // 2, 2)
-        greet(dp_peers() + [along_y(1), along_y(3)])
         first = Sends(
             [
                 (two_up.at[half], far.at[half], along_y(1)),
@@ -951,20 +932,12 @@
             frecv,
         )
         first.start()
-        loads = [
-            pltpu.make_async_copy(one_up, up, loaded.at[0]),
-            pltpu.make_async_copy(one_down, down, loaded.at[1]),
-        ]
-        for load in loads:
-            load.start()
-        second = Sends(
-            [(up, below_ref, along_y(1)), (down, above_ref, along_y(3))], wsend, wrecv
-        )
-        along_x = remote(
-            x_ref.at[1 - x_index], x_got, small_send.at[0], small_recv.at[0], {"dp": me ^ 2}
-        )
-        along_x.start()
-        value = mm(d_ref[...], w_ref[...], NT).astype(bf16)
+        d_middle_ref[...] = d_middle
+        stats_ref[0:1] = column_sum(d_normed * middle * inv)
+        scatter_moe.middle()
+        gather.wait()
+        d_attn[...] = full[...].astype(f32).reshape(tok, width).astype(bf16)
+        value = mm(d_attn[...], w_ref[...], NT).astype(bf16)
         d_heads[0] = value[:, 0:size]
         d_heads[1] = value[:, size : 2 * size]
         swap = remote(
@@ -973,14 +946,24 @@
         swap.start()
         d_pair[core] = d_heads[core]
         for d in range(N_DP):
-            out_part[d] = mm(d_ref[:, d * 128 : (d + 1) * 128], heads_ref[...], TN).astype(bf16)
+            out_part[d] = mm(d_attn[:, d * 128 : (d + 1) * 128], heads_ref[...], TN).astype(bf16)
         outs = [
             remote(out_part.at[me ^ k], out_got.at[k], osend.at[k], orecv.at[k], {"dp": me ^ k})
             for k in range(1, N_DP)
         ]
+        for copy in outs:
+            copy.start()
+        moe_out = scatter_moe.total()
+        output = middle_ref[...] + moe_out
+        out_slice[...] = output.astype(bf16)
+        gather_out = YGather(out_slice, full_ref, *gather_sems)
+        gather_out.start()
+        stats_ref[1:2] = column_sum(moe_out * moe_out)
+        stats_ref[2:3] = column_sum(output * output)
+
         swap.wait_recv()
         q, d_out = q_ref[...].reshape(count, size), d_pair[...].reshape(count, size)
-        lowest, highest = bound_ref[0:1], bound_ref[1:2]
+        lowest, highest = codes_of_queries(me // 2, count, lengths_ref)
         log = log_ref[0:1]
         delta = jnp.sum((wide_ref[...] * d_out.astype(f32)).T, axis=0, keepdims=True)
 
@@ -993,7 +976,7 @@
             at = pl.ds(pl.multiple_of(group * tok, tok), tok)
             k = k_ref[at]
             scores = mm(k, q, NT) * factor
-            code = code_ref[at][:, 0:1]
+            code = codes_of_keys(group, tok, lengths_ref)
             seen = (code >= lowest) & (code <= highest)
             probs = jnp.where(seen, jnp.exp2(scores - log), 0.0)
             d_probs = mm(v_ref[at], d_out, NT)
@@ -1008,10 +991,23 @@
             return acc
 
         acc = lax.fori_loop(1, N_DP, other, jnp.zeros((size, count), f32))
-        for copy in outs:
-            copy.start()
         acc = block(me, acc)
-        for load in loads:
+        d_query[...] = (acc.T * scale).astype(bf16).reshape(2, tok, size)
+        back = remote(
+            d_query.at[1 - core], pair_ref.at[core], small_send.at[2], small_recv.at[2], {"dp": me ^ 1}
+        )
+        back.start()
+        pair_ref[core] = d_query[core]
+
+        loads[2].wait()
+        over_z.wait()
+        for side in range(2):
+            total = z_got[0, side].astype(f32)
+            for k in (1, 2, 3):
+                total = total + z_got[k, side].astype(f32)
+            by_x[side] = total.astype(bf16)
+
+        for load in loads[:2]:
             load.wait()
         for copy in first.copies:
             copy.wait_recv()
@@ -1026,16 +1022,18 @@
 
         add(half, up)
         add(rest, down)
+        second = Sends(
+            [(up.at[now], below_ref, along_y(1)), (down.at[now], above_ref, along_y(3))], wsend, wrecv
+        )
         second.start()
-        d_query[...] = (acc.T * scale).astype(bf16).reshape(2, tok, size)
-        back = remote(
-            d_query.at[1 - core], pair_ref.at[core], small_send.at[2], small_recv.at[2], {"dp": me ^ 1}
-        )
-        back.start()
-        pair_ref[core] = d_query[core]
+        stores = [
+            pltpu.make_async_copy(up.at[later], up_ref, loaded.at[3]),
+            pltpu.make_async_copy(down.at[later], down_ref, loaded.at[4]),
+        ]
+        for store in stores:
+            store.start()
+        gather_out.relay()
         got[0] = made[me]
-        along_x.wait_recv()
-        shared_ref[...] = x_got[...].astype(f32)
         for k in range(1, N_DP):
             send_to(k).wait_recv()
         for head in range(2):
@@ -1049,8 +1047,13 @@
             total = total + out_got[k + 1].astype(f32)
         out_ref[...] = total
         back.wait_recv()
-        for copy in [along_x, swap, back] + outs + first.copies:
+        for copy in [swap, back] + outs + first.copies:
             copy.wait_send()
+        scatter.wait_send()
+        scatter_moe.wait_send()
+        for store in stores:
+            store.wait()
+        gather_out.wait()
         second.wait()
         for k in range(1, N_DP):
             send_to(k).wait_send()
@@ -1058,16 +1061,24 @@
     return pl.pallas_call(
         kernel,
         out_shape=(
+            struct((rows, width), f32),
+            struct((8, width), f32),
             struct((2, 2 * tok, size), f32),
             struct(q.shape, bf16),
             struct((width // N_DP, 2 * size), f32),
-            struct(by_x.shape[1:], f32),
-            struct((n_sent, width), bf16),
-            struct((n_sent, width), bf16),
+            struct(weights.shape[1:], bf16),
+            struct(part.shape, bf16),
+            struct((NOW, width), bf16),
+            struct((NOW, width), bf16),
+            struct((n_sent - NOW, width), bf16),
+            struct((n_sent - NOW, width), bf16),
         ),
-        in_specs=[VMEM] * 10 + [HBM] * 4,
-        out_specs=(VMEM,) * 4 + (HBM,) * 2,
+        in_specs=[VMEM] * 12 + [SMEM] + [HBM] * 4,
+        out_specs=(VMEM,) * 6 + (HBM,) * 5,
         scratch_shapes=[
+            pltpu.VMEM(part.shape, bf16),
+            pltpu.VMEM((tok, width), bf16),
+            pltpu.VMEM((rows, width), bf16),
             pltpu.VMEM(q.shape, bf16),
             pltpu.VMEM(q.shape, bf16),
             pltpu.VMEM((N_DP, 2 * tok, size), bf16),
@@ -1075,43 +1086,73 @@
             pltpu.VMEM(q.shape, bf16),
             pltpu.VMEM((N_DP, 128, 2 * size), bf16),
             pltpu.VMEM((N_DP, 128, 2 * size), bf16),
-            pltpu.VMEM(by_x.shape[1:], bf16),
+            pltpu.VMEM(weights.shape, bf16),
         ]
         + [pltpu.VMEM((n_sent, width), bf16)] * 3
-        + sems(N_DP, N_DP, N_DP, N_DP, 3, 3, 2, 2, 2, 2, 2),
+        + direct_scratch(rows, width)
+        + [pltpu.VMEM((2, 4, rows, width), bf16)]
+        + [pltpu.VMEM((rows, width), bf16)] * 2
+        + sems((2, 4), (2, 4))
+        + sems(N_DP, N_DP, N_DP, N_DP, 3, 3, 2, 2, 2, 2, 5, 3, 3, (2, 4), (2, 4), 1),
         compiler_params=comm_params(number, LIMIT),
-        name="attend_backward",
-        cost_estimate=cost(65),
-    )(d_attn, out_weight, heads, q, keys, values, codes, bounds, wide, logs, by_x, *sent)
-
-
-def join_tail(part, layer_input, d_middle, gain, normed, d_proj, pack, own_grads, received, number):
+        name="backward",
+        cost_estimate=cost(110),
+    )(
+        part, moe_part, cotangent, middle, gain, out_weight, heads, q, keys, values, wide, logs, lengths, weights, *sent
+    )
+
+
+def join_tail(part, layer_input, d_middle, gain, normed, d_proj, smalls, own_grads, received, waiting, by_x, number):
     _, rows, width = part.shape
-    small = pack.shape[1]
+    small = 32
     wide = d_proj.shape[1]
-    n_in, n_out = 8 + len(received), 6
+    n_in, n_out = 14 + len(received), 8
+    n_hidden = by_x.shape[1] // 3
     n_expert = own_grads.shape[0]
+    n_late = n_expert - NOW - SOON
+    first = pl.ds(0, NOW)
+    parts = ((0, SOON), (SOON, n_late))
     units = n_expert // 3
 
     def kernel(*refs):
-        part_ref, x_ref, d_ref, gain_ref, n_ref, proj_ref, pack_ref, own_grads_ref = refs[:8]
-        received_refs = refs[8:n_in]
-        full_ref, qkv_ref, one_ref, both_ref, in_ref, out_ref = refs[n_in : n_in + n_out]
+        part_ref, x_ref, d_ref, gain_ref, n_ref, proj_ref = refs[:6]
+        router_ref, vec_ref, one_stats, two_stats, own_grads_ref = refs[6:11]
+        received_refs, (up_ref, down_ref, by_x_ref) = refs[11 : n_in - 3], refs[n_in - 3 : n_in]
+        full_ref, qkv_ref, one_ref, both_ref, shared_in_ref, shared_out_ref, in_ref, out_ref = refs[n_in : n_in + n_out]
         scratch = refs[n_in + n_out :]
-        join, scratch = scratch[:N_JOIN], scratch[N_JOIN:]
-        own, few, mine, more, send, recv, tsend, trecv = scratch[:8]
+        join, scratch = scratch[:N_DIRECT], scratch[N_DIRECT:]
+        own, few, summed, more, send, recv, tsend, trecv = scratch[:8]
         qbuf, qgot, qsum, qin, csend, crecv, ksend, krecv = scratch[8:16]
-        acc, others, lsem, osem = scratch[16:]
+        acc, others, lsem, osem, esend, erecv, x_near, x_far, xsend, xrecv = scratch[16:]
         me, t = lax.axis_index("dp"), lax.axis_index("tensor")
         core, chip = me % 2, me // 2
         greet(tensor_peers() + dp_peers())
-        scatter, gather = join_parts(part_ref, full_ref, join)
+        got, mine, jsend, jrecv, asend, arecv, alocal = join
+        scatter = DirectScatter(part_ref, got, jsend, jrecv)
+        gather = YGather(mine, full_ref, asend, arecv, alocal)
         scatter.start()
+        rest = Sends(
+            [
+                (ref.at[pl.ds(at, n)], others.at[i, pl.ds(NOW + at, n)], along_y(shift))
+                for at, n in parts
+                for i, (ref, shift) in enumerate(((up_ref, 1), (down_ref, 3)))
+            ],
+            esend,
+            erecv,
+        )
+        for copy in rest.copies[:2]:
+            copy.start()
         loads = [pltpu.make_async_copy(own_grads_ref, acc, lsem.at[0])] + [
-            pltpu.make_async_copy(r, others.at[i], lsem.at[i + 1]) for i, r in enumerate(received_refs)
+            pltpu.make_async_copy(r, others.at[i, first], lsem.at[i + 1])
+            for i, r in enumerate(received_refs)
         ]
         for load in loads:
             load.start()
+        x_index = chip % 2
+        along_x = remote(by_x_ref.at[1 - x_index], x_far, xsend.at[0], xrecv.at[0], {"dp": me ^ 2})
+        along_x.start()
+        near = pltpu.make_async_copy(by_x_ref.at[x_index], x_near, xsend.at[1])
+        near.start()
         across = []
         for c in range(8):
             for side in range(2):
@@ -1132,40 +1173,56 @@
         ]
         for copy in chips:
             copy.start()
+        bias = column_sum(proj_ref[...].astype(f32))
+        stats = [one_stats[k : k + 1] for k in range(3)] + [two_stats[k : k + 1] for k in (1, 2)]
+        rows_all = [sum(row[:, i * 128 : (i + 1) * 128] for i in range(N_DP)) for row in stats] + [
+            bias[:, i * 128 : (i + 1) * 128] for i in range(wide // 128)
+        ]
+        for i in range(N_DP):
+            cols = slice(i * 128, (i + 1) * 128)
+            own[i, 0:16] = router_ref[:, cols]
+            own[i, 16:17] = vec_ref[:, cols]
+            own[i, 17:18] = two_stats[0:1, cols]
+            for k, row in enumerate(rows_all):
+                own[i, 19 + k : 20 + k] = row
+            own[i, 19 + len(rows_all) : small] = jnp.zeros((small - 19 - len(rows_all), 128), f32)
         resid = x_ref[t].astype(f32)
         inv = second_moment(resid)
-        scatter.middle()
         d_normed = scatter.total()
         scaled = d_normed * gain_ref[...]
-        gather.start(
+        mine[...] = (
             d_ref[...]
             + inv * scaled
             - resid * (inv * inv * inv) * jnp.mean(scaled * resid, axis=1, keepdims=True)
-        )
+        ).astype(bf16)
+        gather.start()
         gain_grad = column_sum(d_normed * resid * inv)
-        own[...] = pack_ref[...]
         for i in range(N_DP):
-            own[i, small - 1 : small] = gain_grad[:, i * 128 : (i + 1) * 128]
+            own[i, 18:19] = gain_grad[:, i * 128 : (i + 1) * 128]
         firsts = [
             remote(own.at[me ^ k], few.at[k], send.at[k], recv.at[k], {"dp": me ^ k})
             for k in range(1, N_DP)
         ]
         for copy in firsts:
             copy.start()
-        gather.relay()
+        for copy in rest.copies[2:]:
+            copy.start()
         value = own[me]
         for k in range(1, N_DP):
             firsts[k - 1].wait_recv()
             value = value + few[k]
         one_ref[...] = value
-        mine[...] = value
+        summed[...] = value
         seconds = [
-            remote(mine, more.at[k], tsend.at[k], trecv.at[k], {"tensor": t ^ k}) for k in range(1, N_T)
+            remote(summed, more.at[k], tsend.at[k], trecv.at[k], {"tensor": t ^ k}) for k in range(1, N_T)
         ]
         for copy in seconds:
             copy.start()
+        gather.relay()
         for load in loads:
             load.wait()
+        for copy in rest.copies:
+            copy.wait_recv()
 
         def add(j, carry):
             cols = pl.ds(pl.multiple_of(j * 256, 256), 256)
@@ -1182,6 +1239,11 @@
         ]
         for store in stores:
             store.start()
+        near.wait()
+        along_x.wait_recv()
+        total = x_near[...].astype(f32) + x_far[...].astype(f32)
+        shared_in_ref[...] = total[0 : 2 * n_hidden]
+        shared_out_ref[...] = total[2 * n_hidden :]
         total = qsum[chip].astype(f32)
         for k in range(1, 8):
             chips[k - 1].wait_recv()
@@ -1191,7 +1253,7 @@
             seconds[k - 1].wait_recv()
             value = value + more[k]
         both_ref[...] = value
-        for copy in firsts + seconds + across + chips:
+        for copy in firsts + seconds + across + chips + rest.copies + [along_x]:
             copy.wait_send()
         scatter.wait_send()
         gather.wait()
@@ -1205,12 +1267,18 @@
             struct((width // N_DP, wide), f32),
             struct((small, 128), f32),
             struct((small, 128), f32),
+            struct((2 * n_hidden, 128), f32),
+            struct((n_hidden, 128), f32),
             struct((2 * units, width), f32),
             struct((units, width), f32),
         ),
-        in_specs=[VMEM] * 7 + [HBM] * (n_in - 7),
-        out_specs=(HBM, VMEM, VMEM, VMEM, HBM, HBM),
-        scratch_shapes=join_scratch(rows, width)
+        in_specs=[VMEM] * 10 + [HBM] * (n_in - 10),
+        out_specs=(HBM,) + (VMEM,) * 5 + (HBM,) * 2,
+        scratch_shapes=[
+            pltpu.VMEM(part.shape, bf16),
+            pltpu.VMEM((rows, width), bf16),
+        ]
+        + sems(N_T, N_T, (2, 4), (2, 4), 1)
         + [
             pltpu.VMEM((N_DP, small, 128), f32),
             pltpu.VMEM((N_DP, small, 128), f32),
@@ -1229,11 +1297,13 @@
             pltpu.VMEM((n_expert, width), f32),
             pltpu.VMEM((len(received), n_expert, width), bf16),
         ]
-        + sems(n_in - 7, 2),
+        + sems(1 + len(received), 2, 4, 4)
+        + [pltpu.VMEM(by_x.shape[1:], bf16)] * 2
+        + sems(2, 1),
         compiler_params=comm_params(number, LIMIT),
         name="join_tail",
         cost_estimate=cost(55),
-    )(part, layer_input, d_middle, gain, normed, d_proj, pack, own_grads, *received)
+    )(part, layer_input, d_middle, gain, normed, d_proj, *smalls, own_grads, *received, *waiting, by_x)
 
 
 def doc_layout(lengths, token_index):
@@ -1302,28 +1372,16 @@
     place = jnp.where(hot > 0, rank, -1.0).astype(jnp.int32).T
     _, offset = route_plane()
     served = lax.dynamic_slice_in_dim(place, GROUPS * ((dp // 4) ^ offset), GROUPS, 0)
-    places = (
-        (served[:, None, :] == jnp.arange(SLOTS, dtype=jnp.int32)[None, :, None])
-        .astype(bf16)
-        .reshape(GROUPS * SLOTS, tok)
-    )
+    places = (served[:, None, :] == jnp.arange(SLOTS, dtype=jnp.int32)[None, :, None]).astype(bf16)
     returned = lax.dynamic_index_in_dim(place.reshape(GROUPS, 4, tok), offset, 1, keepdims=False)
     places_back = (
         (returned[:, None, :] == jnp.arange(SLOTS, dtype=jnp.int32)[None, :, None])
         .astype(bf16)
         .reshape(GROUPS * SLOTS, tok)
     )
-    by_group = (GROUPS, SLOTS, width)
-    up_send = dot("rt,td->rd", places, cotangent).astype(bf16)
 
     local_index = dp * tok + jnp.arange(tok, dtype=jnp.int32)
-    pair_index = (dp // 2) * (2 * tok) + jnp.arange(2 * tok, dtype=jnp.int32)
-    every_index = jnp.arange(stream, dtype=jnp.int32)
     _, pos_local, _ = doc_layout(doc_lengths, local_index)
-    seq_pair, _, blk_pair = doc_layout(doc_lengths, pair_index)
-    seq_all, _, blk_all = doc_layout(doc_lengths, every_index)
-    codes = jnp.broadcast_to((seq_all * CODE + blk_all)[:, None], (stream, 128))
-    bounds = jnp.stack([seq_pair * CODE, seq_pair * CODE + blk_pair] + [seq_pair] * 6)
     cosine, sine = rope_tables(pos_local, head_dim)
     residual = layer_input.astype(f32)
     inv_first = lax.rsqrt(jnp.mean(residual * residual, axis=1, keepdims=True) + EPSILON)
@@ -1338,8 +1396,7 @@
         k_own,
         v_own,
         q_own,
-        codes,
-        bounds,
+        doc_lengths,
         out_flat,
         layer_input.reshape(by_slice),
         ffn_gain.reshape(1, width),
@@ -1348,13 +1405,11 @@
     )
     normed_two = normed_two.reshape(tok, width)
 
-    row_send = dot("rt,td->rd", places, normed_two).astype(bf16)
     own_expert = jnp.broadcast_to(
         (jnp.arange(experts_n, dtype=jnp.int32) == dp).astype(f32)[:, None], (experts_n, 128)
     )
     back_grads, back_out, mixed, shared_d_normed, got, gate_vec_part, router_part, own_grads, *sent = experts(
-        row_send.reshape(by_group),
-        up_send.reshape(by_group),
+        places,
         *neighbours,
         in_rows,
         expert_out[0],
@@ -1375,22 +1430,24 @@
 
     d_normed_part = (shared_d_normed + combine(back_grads)).astype(bf16)
     moe_part = (mixed + combine(back_out)).astype(bf16)
-    d_attn, output, d_middle, stats_two, by_x = join_ffn(
+    d_middle, stats_two, d_keys, d_queries, outproj_grad, by_x, output, *moved = backward(
         d_normed_part.reshape(by_slice),
         moe_part.reshape(by_slice),
         cotangent.reshape(by_slice),
         middle,
         ffn_gain.reshape(1, width),
+        out_flat,
+        heads_out,
+        queries,
+        keys,
+        values,
+        wide,
+        logs,
+        doc_lengths,
         by_z,
+        sent,
         7,
     )
-    d_attn = d_attn.reshape(tok, width)
-
-    d_keys, d_queries, outproj_grad, shared_far, *received = attend_backward(
-        d_attn, out_flat, heads_out, queries, keys, values, codes, bounds, wide, logs, by_x, sent, 9
-    )
-    shared_grads = lax.dynamic_index_in_dim(by_x, (dp // 2) % 2, 0, keepdims=False).astype(f32) + shared_far
-    n_shared = shared_in.shape[2]
 
     cosine, sine = cosine[:, 0], sine[:, 0]
     d_proj = jnp.concatenate(
@@ -1402,39 +1459,22 @@
     d_normed_one = dot(
         "tshe,dshe->td", d_proj.reshape(tok, 3, 2, head_dim), qkv_weight
     ).astype(bf16)
-    bias_part = jnp.sum(d_proj.astype(f32), axis=0)
-
-    def slices(row):
-        return row.reshape(-1, N_DP, 128).transpose(1, 0, 2)
-
-    five = jnp.sum(jnp.concatenate([stats_one[:3], stats_two[1:3]]), axis=1)
-    pack = jnp.concatenate(
-        [
-            slices(router_part),
-            slices(gate_vec_part[0]),
-            slices(stats_two[0]),
-            jnp.broadcast_to(jnp.pad(five, (0, 123))[None, None], (N_DP, 1, 128)),
-            jnp.pad(
-                bias_part.reshape(6, N_DP, 8).transpose(1, 0, 2).reshape(N_DP, 1, 48),
-                ((0, 0), (0, 4), (0, 80)),
-            ),
-        ],
-        axis=1,
-    )
-    input_grad, qkv_grad, over_dp, over_both, expert_in_grad, expert_out_grad = join_tail(
+    input_grad, qkv_grad, over_dp, over_both, shared_in_grad, shared_out_grad, expert_in_grad, expert_out_grad = join_tail(
         d_normed_one.reshape(by_slice),
         layer_input.reshape(by_slice),
         d_middle,
         attn_gain.reshape(1, width),
         normed_one,
         d_proj,
-        pack,
+        [router_part, gate_vec_part, stats_one, stats_two],
         own_grads,
-        received,
+        moved[:2],
+        moved[2:],
+        by_x,
         10,
     )
-    bias_grad = over_dp[19, :48].reshape(3, 2, 8)
-    rms_stats = jnp.sqrt(over_both[18, :5] / (stream * width))
+    bias_grad = lax.dynamic_slice_in_dim(over_dp[24:30], 8 * dp, 8, 1).reshape(3, 2, 8)
+    rms_stats = jnp.sqrt(jnp.sum(over_both[19:24], axis=1) / (stream * width))
 
     return (
         output.reshape(tok, width),
@@ -1442,12 +1482,12 @@
         qkv_grad.reshape(width // N_DP, 3, 2, head_dim),
         bias_grad,
         outproj_grad.T.reshape(2, head_dim, width // N_DP),
-        over_both[23],
+        over_both[18],
         over_both[17],
         over_both[:16].T,
         over_both[16],
-        shared_grads[: 2 * n_shared].reshape(2, n_shared, -1).transpose(2, 0, 1),
-        shared_grads[2 * n_shared :],
+        shared_in_grad.reshape(2, shared_in.shape[2], -1).transpose(2, 0, 1),
+        shared_out_grad,
         expert_in_grad.reshape(2, eff, width).transpose(2, 0, 1)[None],
         expert_out_grad[None],
         rms_stats,

time: 489 us -> 460 us (0.941)
  Pallas kernels: 431 us -> 413 us
    pallas_call x2 -> x1, Pallas kernels: 158 us -> 118 us  [backward(): pl.pallas_call(kernel, out_shape=(struct((rows, width), f32), struct((8,...]
    pallas_call x1, Pallas kernels: 54.5 us -> 78.6 us  [join_tail(): pl.pallas_call(kernel, out_shape=(struct(part.shape, bf16), struct((width...]
    pallas_call x1, Pallas kernels: 128 us -> 107 us  [experts(): pl.pallas_call(kernel, out_shape=(row, row, struct((tok, width), f32), st...]
    pallas_call x1, Pallas kernels: 90.9 us -> 110 us  [attend_forward(): pl.pallas_call(kernel, out_shape=(struct((stream, size), bf16), struct((s...]
    unnamed x71 -> x81, local copies, waits for them, and re-layouts: 8.62 us -> 15.1 us
    dot_general x7 -> x5, matrix products: 16.9 us -> 12.3 us  [dot(): return jnp.einsum(pattern, a, b, preferred_element_type=f32)]
where the time goes in v5:
time: 460 us; the launch traced here: 459 us
  Pallas kernels  413 us (90%)
  local copies, waits for them, and re-layouts  19.1 us (4%)
  other arithmetic  13.2 us (3%)
  matrix products  12.3 us (3%)
    pallas_call x1, Pallas kernels, backward(): pl.pallas_call(kernel, out_shape=(struct((rows, width), f32), struct((8,...  118 us
    pallas_call x1, Pallas kernels, attend_forward(): pl.pallas_call(kernel, out_shape=(struct((stream, size), bf16), struct((s...  110 us
    pallas_call x1, Pallas kernels, experts(): pl.pallas_call(kernel, out_shape=(row, row, struct((tok, width), f32), st...  107 us
    pallas_call x1, Pallas kernels, join_tail(): pl.pallas_call(kernel, out_shape=(struct(part.shape, bf16), struct((width...  78.6 us
    unnamed x81, local copies, waits for them, and re-layouts  15.1 us
    dot_general x5, matrix products, dot(): return jnp.einsum(pattern, a, b, preferred_element_type=f32)  12.3 us

profile of v5, /device:TPU:1, one launch (start us, length us, event | category | flops | bytes accessed | tf_op | source)
XLA Modules:
  0.0 459.4 jit_solution(5067654140413886373)
XLA Ops:
  0.6 0.0 copy-start.29
  0.7 0.0 copy-start.22
  0.7 0.9 reduce-window.8
  1.7 0.7 bitcast_subtract_fusion
  2.3 1.7 fusion.14
  4.0 0.1 convert_reduce_fusion.1
  4.1 0.1 select_reduce_fusion
  4.2 0.7 convert_element_type.85
  4.9 0.7 broadcast_in_dim.27.refs_12_
  5.6 1.3 reshape.230
  6.8 0.7 convert_reduce_fusion
  7.6 0.1 fusion.23
  7.8 0.0 copy-start.36
  7.8 0.6 multiply_cosine_fusion
  8.5 0.8 fusion.24.refs_7_
  9.3 0.4 fusion.16.refs_4_
  9.7 0.1 copy-done.36
  9.8 1.2 fusion.18
  11.0 0.0 copy-start
  11.1 0.0 copy-start.1
  11.1 0.0 copy-start.20
  11.1 0.0 copy-start.27
  11.1 0.3 subtract_convert_fusion
  11.5 0.2 maximum_bitcast_fusion
  11.7 0.6 copy-done
  12.3 0.2 copy-done.1
  12.5 109.7 %attend_forward.1 = (bf16[5120,128]{1,0:T(8,128)(2,1)S(1)}, bf16[5120,128]{1,0:T(8,128)(2,1)S(1)}, bf16[2,320,128]{2,1,0:T(8,128)(2,1)S(1)}, f32[640,128]{1,0:T(...) custom-call(bf16[2,320,128]{2,1,0:T(8,128)(2,1)S(1)} %get-tuple-elem, ...), custom_call_target="tpu_custom_call" | custom-call | bytes 255000000 | tf_op jit(solution)/shard_map/attend_forward/pallas_call | solution.py:581
  122.2 1.0 copy-done.2
  123.2 1.1 copy-done.3
  124.3 0.7 copy-done.9
  125.0 0.7 copy-done.11
  125.7 0.7 copy-done.13
  126.4 0.6 copy-done.16
  127.0 0.6 copy-done.24
  127.6 107.2 %experts.1 = (bf16[4,112,2048]{2,1,0:T(8,128)(2,1)}, bf16[4,112,2048]{2,1,0:T(8,128)(2,1)}, f32[320,2048]{1,0:T(8,128)}, f32[320,2048]{1,0:T(8,128)}, bf16[8,211...) custom-call(bf16[528,2048]{1,0:T(8,128)(2,1)} %get-tuple-element.56., ...), custom_call_target="tpu_custom_call" | custom-call | bytes 345000000 | tf_op jit(solution)/shard_map/experts/pallas_call | solution.py:833
  234.8 4.6 fusion.10
  239.4 0.0 copy-start.14
  239.4 0.0 copy-start.21
  239.4 2.1 fusion.9
  241.6 118.1 %backward.1 = (f32[40,2048]{1,0:T(8,128)S(1)}, f32[8,2048]{1,0:T(8,128)S(1)}, f32[2,640,128]{2,1,0:T(8,128)S(1)}, bf16[2,320,128]{2,1,0:T(8,128)(2,1)S(1)}, f32[...) custom-call(bf16[8,40,2048]{2,1,0:T(8,128)(2,1)} %bitcast.122, ...), custom_call_target="tpu_custom_call" | custom-call | bytes 330000000 | tf_op jit(solution)/shard_map/backward/pallas_call | solution.py:1061
  359.7 1.0 copy-done.5
  360.6 0.7 copy-done.7
  361.4 0.8 copy.40
  362.2 0.8 fusion.43
  363.1 0.4 concatenate.13.refs_5_
  363.4 0.1 convert_element_type.102
  363.6 0.0 copy-start.6
  363.6 0.0 copy-start.23
  363.7 4.3 fusion.11
  368.0 78.6 %join_tail.1 = (bf16[8,40,2048]{2,1,0:T(8,128)(2,1)}, f32[128,768]{1,0:T(8,128)S(1)}, f32[32,128]{1,0:T(8,128)S(1)}, f32[32,128]{1,0:T(8,128)S(1)}, f32[1408,128...) custom-call(bf16[8,40,2048]{2,1,0:T(8,128)(2,1)} %bitcast.129, ...), custom_call_target="tpu_custom_call" | custom-call | bytes 165000000 | tf_op jit(solution)/shard_map/join_tail/pallas_call | solution.py:1263
  446.6 0.1 slice_reduce_fusion
  446.7 0.5 multiply_sqrt_fusion
  447.2 0.5 slice_bitcast_fusion.7
  447.8 0.6 slice_bitcast_fusion.6
  448.4 0.1 constant_dynamic-slice_fusion.1
  448.4 0.6 reshape.226
  449.0 0.9 reshape.225
  450.0 3.2 bitcast_convert_fusion
  453.2 1.1 copy.61
  454.3 0.9 copy.62
  455.1 0.7 copy.63
  455.9 1.6 copy.64
  457.4 0.8 copy-done.34
  458.3 1.1 copy.65
  (65 shorter events, 0.3 us)
Async XLA Ops:
  0.6 8.6 %copy-start.29 = (bf16[320,2048]{1,0:T(8,128)(2,1)S(1)}, bf16[320,2048]{1,0:T(8,128)(2,1)}, u32[]{:S(2)}) copy-start(bf16[320,2048]{1,0:T(8,128)(2,1)} %param.15) | copy-start | bytes 3932164
  0.7 8.6 %copy-start.22 = (f32[2048]{0:T(1024)S(1)}, f32[2048]{0:T(1024)}, u32[]{:S(2)}) copy-start(f32[2048]{0:T(1024)} %param.18) | copy-start | bytes 24580
  7.8 2.0 copy-start.36
  9.8 1.2 copy-start.30
  11.0 1.2 copy-start
  11.1 1.4 copy-start.1
  11.1 1.4 copy-start.20
  11.1 1.4 copy-start.27
  122.2 1.1 copy-start.2
  123.2 1.1 copy-start.3
  124.3 0.7 copy-start.9
  125.0 0.7 copy-start.11
  125.7 0.7 copy-start.13
  126.4 0.6 copy-start.16
  127.0 0.6 copy-start.24
  234.8 4.6 copy-start.32
  234.8 4.6 copy-start.33
  239.4 2.2 copy-start.10
  239.4 2.2 copy-start.12
  239.4 2.2 copy-start.14
  239.4 2.2 copy-start.21
  239.4 2.2 copy-start.25
  239.4 2.2 copy-start.28
  359.7 1.0 copy-start.5
  360.6 0.7 copy-start.7
  361.4 1.7 copy-start.18
  363.6 4.4 copy-start.4
  363.6 4.4 copy-start.6
  363.6 4.4 copy-start.8
  363.6 4.4 copy-start.15
  363.6 4.4 copy-start.17
  363.6 4.4 copy-start.19
  363.6 4.4 copy-start.23
  363.6 4.4 copy-start.26
  450.0 3.2 copy-start.35
  453.2 2.7 copy-start.31
  455.9 2.4 copy-start.34

commit v6 on v5

--- a/solution.py
+++ b/solution.py
@@ -70,6 +70,7 @@
 
 GROUPS = 4
 HALF = 256
+SOON = 96
 ORDER = (4, 12, 2, 5, 13, 3, 8, 6, 14, 9, 7, 15, 10, 11, 1)
 STEPS = (1, 3, 2, 4, 5, 7, 6)
 CHUNKS = ((0, 48), (48, 64))
@@ -343,6 +344,45 @@
         self.across.wait_send()
 
 
+class Gather:
+    def __init__(self, mine, full_ref, send, recv, local):
+        t = lax.axis_index("tensor")
+        self.mine = mine
+        self.across = remote(
+            mine, full_ref.at[t], send.at[0, 0], recv.at[0, 0], {"tensor": t ^ 4}
+        )
+        self.first = [
+            remote(mine, full_ref.at[t], send.at[0, k], recv.at[0, k], {"tensor": t ^ k})
+            for k in (1, 3, 2)
+        ]
+        self.second = [
+            remote(
+                full_ref.at[t ^ 4],
+                full_ref.at[t ^ 4],
+                send.at[1, k],
+                recv.at[1, k],
+                {"tensor": t ^ k},
+            )
+            for k in (1, 3, 2)
+        ]
+        self.own = pltpu.make_async_copy(mine, full_ref.at[t], local.at[0])
+
+    def start(self, value):
+        self.mine[...] = value.astype(bf16)
+        for copy in [self.across] + self.first + [self.own]:
+            copy.start()
+
+    def relay(self):
+        self.across.wait_recv()
+        for copy in self.second:
+            copy.start()
+
+    def wait(self):
+        self.across.wait_send()
+        for copy in self.first + self.second + [self.own]:
+            copy.wait()
+
+
 class YGather:
     def __init__(self, mine, full_ref, send, recv, local):
         t = lax.axis_index("tensor")
@@ -446,7 +486,6 @@
 def attend_forward(k, v, q, lengths, out_weight, layer_input, gain, weights, number):
     _, tok, size = q.shape
     n_rows = [w.shape[0] for w in weights]
-    half, rest = pl.ds(0, HALF), pl.ds(HALF, sum(n_rows) - HALF)
     stream, count = N_DP * tok, 2 * tok
     _, rows, width = layer_input.shape
     factor = size ** (-0.5) * math.log2(math.e)
@@ -545,27 +584,39 @@
             return carry
 
         lax.fori_loop(0, width // 512, project, 0)
-        scatter, gather = direct_parts(part, full_ref, join)
+        scatter = DirectScatter(part, join[0], *join[2:4])
+        mine = join[1]
+        gather = YGather(mine, full_ref, *join[4:])
         scatter.start()
         for copy in both.copies:
             copy.wait_recv()
         below_ref, above_ref, far_ref = outs[9:]
         relay = Sends(
             [
-                (below_ref.at[half], far_ref.at[half], along_y(1)),
-                (above_ref.at[rest], far_ref.at[rest], along_y(3)),
+                (ref.at[pl.ds(at, n)], far_ref.at[pl.ds(at, n)], along_y(shift))
+                for ref, shift, at, n in (
+                    (below_ref, 1, 0, SOON),
+                    (above_ref, 3, HALF, SOON),
+                    (below_ref, 1, SOON, HALF - SOON),
+                    (above_ref, 3, HALF + SOON, sum(n_rows) - HALF - SOON),
+                )
             ],
             *relay_sems,
         )
-        relay.start()
+        for copy in relay.copies[:2]:
+            copy.start()
         resid = x_ref[lax.axis_index("tensor")].astype(f32)
         attn_out = scatter.total()
         middle = resid + attn_out
-        gather.start(middle * second_moment(middle) * gain_ref[...])
+        mine[...] = (middle * second_moment(middle) * gain_ref[...]).astype(bf16)
+        gather.start()
+        for copy in relay.copies[2:]:
+            copy.start()
         middle_ref[...] = middle
         stats_ref[0:1] = column_sum(resid * resid)
         stats_ref[1:2] = column_sum(attn_out * attn_out)
         stats_ref[2:3] = column_sum(middle * middle)
+        gather.relay()
         for step in ORDER:
             for copy in copies(step, core):
                 copy.wait_send()
@@ -604,8 +655,12 @@
         ]
         + sems((2, N_DP), (2, N_DP), 2)
         + SWAP_SEMS
-        + sems(1, 1, 3, 4, 4, 2, 2)
-        + direct_scratch(rows, width),
+        + sems(1, 1, 3, 4, 4, 4, 4)
+        + [
+            pltpu.VMEM(layer_input.shape, bf16),
+            pltpu.VMEM((rows, width), bf16),
+        ]
+        + sems(N_T, N_T, (2, 4), (2, 4), 1),
         compiler_params=comm_params(number, LIMIT),
         name="attend_forward",
         cost_estimate=cost(85),
@@ -617,8 +672,7 @@
 
 
 TILE = 176
-NOW = 256
-SOON = 96
+NOW = 96
 
 
 def shared_expert(x_ref, up_ref, w_ref, vec_ref, part_ref, d_ref, grads_ref, row_ref, low_ref):
@@ -876,7 +930,7 @@
     stream, count = N_DP * tok, 2 * tok
     scale = size ** (-0.5)
     factor = scale * math.log2(math.e)
-    n_sent = sent[0].shape[0]
+    n_sent, n_hidden = sent[0].shape[0], weights.shape[2] // 3
     half, rest = pl.ds(0, HALF), pl.ds(HALF, n_sent - HALF)
     now, later = pl.ds(0, NOW), pl.ds(NOW, n_sent - NOW)
 
@@ -886,17 +940,17 @@
             refs[10:],
         )
         (wide_ref, log_ref, lengths_ref, by_z_ref, one_up, two_up, one_down), refs = refs[:7], refs[7:]
-        (d_middle_ref, stats_ref, sums_ref, pair_ref, out_ref, by_x), refs = refs[:6], refs[6:]
+        (d_middle_ref, stats_ref, sums_ref, pair_ref, out_ref, shared_in_ref, shared_out_ref), refs = refs[:7], refs[7:]
         (full_ref, below_ref, above_ref, up_ref, down_ref), refs = refs[:5], refs[5:]
         (full, d_attn, out_slice, d_heads, d_pair, made, got, d_query, out_part, out_got), refs = refs[:10], refs[10:]
-        (z_got, up, down, far), refs = refs[:4], refs[4:]
+        (z_got, by_x, x_got, up, down, far), refs = refs[:6], refs[6:]
         direct, refs = refs[:N_DIRECT], refs[N_DIRECT:]
         moe_scratch, refs = refs[:5], refs[5:]
         send, recv, osend, orecv, small_send, small_recv, fsend, frecv, wsend, wrecv, loaded = refs[:11]
         zsend, zrecv, gather_sems = refs[11], refs[12], refs[13:]
         me, z, _, _ = coordinates()
         t = lax.axis_index("tensor")
-        core = lax.rem(me, 2)
+        core, x_index = lax.rem(me, 2), lax.rem(me // 2, 2)
         greet(dp_peers() + tensor_peers())
         scatter, gather = direct_parts(part_ref, full, direct)
         scatter.start()
@@ -955,9 +1009,8 @@
             copy.start()
         moe_out = scatter_moe.total()
         output = middle_ref[...] + moe_out
-        out_slice[...] = output.astype(bf16)
-        gather_out = YGather(out_slice, full_ref, *gather_sems)
-        gather_out.start()
+        gather_out = Gather(out_slice, full_ref, *gather_sems)
+        gather_out.start(output)
         stats_ref[1:2] = column_sum(moe_out * moe_out)
         stats_ref[2:3] = column_sum(output * output)
 
@@ -991,6 +1044,7 @@
             return acc
 
         acc = lax.fori_loop(1, N_DP, other, jnp.zeros((size, count), f32))
+        gather_out.relay()
         acc = block(me, acc)
         d_query[...] = (acc.T * scale).astype(bf16).reshape(2, tok, size)
         back = remote(
@@ -1006,6 +1060,10 @@
             for k in (1, 2, 3):
                 total = total + z_got[k, side].astype(f32)
             by_x[side] = total.astype(bf16)
+        along_x = remote(
+            by_x.at[1 - x_index], x_got, small_send.at[0], small_recv.at[0], {"dp": me ^ 2}
+        )
+        along_x.start()
 
         for load in loads[:2]:
             load.wait()
@@ -1032,7 +1090,6 @@
         ]
         for store in stores:
             store.start()
-        gather_out.relay()
         got[0] = made[me]
         for k in range(1, N_DP):
             send_to(k).wait_recv()
@@ -1046,8 +1103,12 @@
             copy.wait_recv()
             total = total + out_got[k + 1].astype(f32)
         out_ref[...] = total
+        along_x.wait_recv()
+        total = by_x[x_index].astype(f32) + x_got[...].astype(f32)
+        shared_in_ref[...] = total[0 : 2 * n_hidden]
+        shared_out_ref[...] = total[2 * n_hidden :]
         back.wait_recv()
-        for copy in [swap, back] + outs + first.copies:
+        for copy in [along_x, swap, back] + outs + first.copies:
             copy.wait_send()
         scatter.wait_send()
         scatter_moe.wait_send()
@@ -1066,7 +1127,8 @@
             struct((2, 2 * tok, size), f32),
             struct(q.shape, bf16),
             struct((width // N_DP, 2 * size), f32),
-            struct(weights.shape[1:], bf16),
+            struct((2 * n_hidden, 128), f32),
+            struct((n_hidden, 128), f32),
             struct(part.shape, bf16),
             struct((NOW, width), bf16),
             struct((NOW, width), bf16),
@@ -1074,7 +1136,7 @@
             struct((n_sent - NOW, width), bf16),
         ),
         in_specs=[VMEM] * 12 + [SMEM] + [HBM] * 4,
-        out_specs=(VMEM,) * 6 + (HBM,) * 5,
+        out_specs=(VMEM,) * 7 + (HBM,) * 5,
         scratch_shapes=[
             pltpu.VMEM(part.shape, bf16),
             pltpu.VMEM((tok, width), bf16),
@@ -1087,6 +1149,8 @@
             pltpu.VMEM((N_DP, 128, 2 * size), bf16),
             pltpu.VMEM((N_DP, 128, 2 * size), bf16),
             pltpu.VMEM(weights.shape, bf16),
+            pltpu.VMEM(weights.shape[1:], bf16),
+            pltpu.VMEM(weights.shape[2:], bf16),
         ]
         + [pltpu.VMEM((n_sent, width), bf16)] * 3
         + direct_scratch(rows, width)
@@ -1102,12 +1166,11 @@
     )
 
 
-def join_tail(part, layer_input, d_middle, gain, normed, d_proj, smalls, own_grads, received, waiting, by_x, number):
+def join_tail(part, layer_input, d_middle, gain, normed, d_proj, smalls, own_grads, received, waiting, number):
     _, rows, width = part.shape
     small = 32
     wide = d_proj.shape[1]
-    n_in, n_out = 14 + len(received), 8
-    n_hidden = by_x.shape[1] // 3
+    n_in, n_out = 13 + len(received), 6
     n_expert = own_grads.shape[0]
     n_late = n_expert - NOW - SOON
     first = pl.ds(0, NOW)
@@ -1117,19 +1180,19 @@
     def kernel(*refs):
         part_ref, x_ref, d_ref, gain_ref, n_ref, proj_ref = refs[:6]
         router_ref, vec_ref, one_stats, two_stats, own_grads_ref = refs[6:11]
-        received_refs, (up_ref, down_ref, by_x_ref) = refs[11 : n_in - 3], refs[n_in - 3 : n_in]
-        full_ref, qkv_ref, one_ref, both_ref, shared_in_ref, shared_out_ref, in_ref, out_ref = refs[n_in : n_in + n_out]
+        received_refs, (up_ref, down_ref) = refs[11 : n_in - 2], refs[n_in - 2 : n_in]
+        grad_ref, qkv_ref, one_ref, both_ref, in_ref, out_ref = refs[n_in : n_in + n_out]
         scratch = refs[n_in + n_out :]
         join, scratch = scratch[:N_DIRECT], scratch[N_DIRECT:]
         own, few, summed, more, send, recv, tsend, trecv = scratch[:8]
         qbuf, qgot, qsum, qin, csend, crecv, ksend, krecv = scratch[8:16]
-        acc, others, lsem, osem, esend, erecv, x_near, x_far, xsend, xrecv = scratch[16:]
+        acc, others, lsem, osem, esend, erecv, full = scratch[16:]
         me, t = lax.axis_index("dp"), lax.axis_index("tensor")
         core, chip = me % 2, me // 2
         greet(tensor_peers() + dp_peers())
         got, mine, jsend, jrecv, asend, arecv, alocal = join
         scatter = DirectScatter(part_ref, got, jsend, jrecv)
-        gather = YGather(mine, full_ref, asend, arecv, alocal)
+        gather = YGather(mine, full, asend, arecv, alocal)
         scatter.start()
         rest = Sends(
             [
@@ -1148,11 +1211,6 @@
         ]
         for load in loads:
             load.start()
-        x_index = chip % 2
-        along_x = remote(by_x_ref.at[1 - x_index], x_far, xsend.at[0], xrecv.at[0], {"dp": me ^ 2})
-        along_x.start()
-        near = pltpu.make_async_copy(by_x_ref.at[x_index], x_near, xsend.at[1])
-        near.start()
         across = []
         for c in range(8):
             for side in range(2):
@@ -1239,11 +1297,6 @@
         ]
         for store in stores:
             store.start()
-        near.wait()
-        along_x.wait_recv()
-        total = x_near[...].astype(f32) + x_far[...].astype(f32)
-        shared_in_ref[...] = total[0 : 2 * n_hidden]
-        shared_out_ref[...] = total[2 * n_hidden :]
         total = qsum[chip].astype(f32)
         for k in range(1, 8):
             chips[k - 1].wait_recv()
@@ -1253,27 +1306,26 @@
             seconds[k - 1].wait_recv()
             value = value + more[k]
         both_ref[...] = value
-        for copy in firsts + seconds + across + chips + rest.copies + [along_x]:
+        for copy in firsts + seconds + across + chips + rest.copies:
             copy.wait_send()
         scatter.wait_send()
         gather.wait()
+        grad_ref[...] = full[...].astype(f32)
         for store in stores:
             store.wait()
 
     return pl.pallas_call(
         kernel,
         out_shape=(
-            struct(part.shape, bf16),
+            struct(part.shape, f32),
             struct((width // N_DP, wide), f32),
             struct((small, 128), f32),
             struct((small, 128), f32),
-            struct((2 * n_hidden, 128), f32),
-            struct((n_hidden, 128), f32),
             struct((2 * units, width), f32),
             struct((units, width), f32),
         ),
         in_specs=[VMEM] * 10 + [HBM] * (n_in - 10),
-        out_specs=(HBM,) + (VMEM,) * 5 + (HBM,) * 2,
+        out_specs=(VMEM,) * 4 + (HBM,) * 2,
         scratch_shapes=[
             pltpu.VMEM(part.shape, bf16),
             pltpu.VMEM((rows, width), bf16),
@@ -1298,12 +1350,11 @@
             pltpu.VMEM((len(received), n_expert, width), bf16),
         ]
         + sems(1 + len(received), 2, 4, 4)
-        + [pltpu.VMEM(by_x.shape[1:], bf16)] * 2
-        + sems(2, 1),
+        + [pltpu.VMEM(part.shape, bf16)],
         compiler_params=comm_params(number, LIMIT),
         name="join_tail",
         cost_estimate=cost(55),
-    )(part, layer_input, d_middle, gain, normed, d_proj, *smalls, own_grads, *received, *waiting, by_x)
+    )(part, layer_input, d_middle, gain, normed, d_proj, *smalls, own_grads, *received, *waiting)
 
 
 def doc_layout(lengths, token_index):
@@ -1430,7 +1481,7 @@
 
     d_normed_part = (shared_d_normed + combine(back_grads)).astype(bf16)
     moe_part = (mixed + combine(back_out)).astype(bf16)
-    d_middle, stats_two, d_keys, d_queries, outproj_grad, by_x, output, *moved = backward(
+    d_middle, stats_two, d_keys, d_queries, outproj_grad, shared_in_grad, shared_out_grad, output, *moved = backward(
         d_normed_part.reshape(by_slice),
         moe_part.reshape(by_slice),
         cotangent.reshape(by_slice),
@@ -1459,7 +1510,7 @@
     d_normed_one = dot(
         "tshe,dshe->td", d_proj.reshape(tok, 3, 2, head_dim), qkv_weight
     ).astype(bf16)
-    input_grad, qkv_grad, over_dp, over_both, shared_in_grad, shared_out_grad, expert_in_grad, expert_out_grad = join_tail(
+    input_grad, qkv_grad, over_dp, over_both, expert_in_grad, expert_out_grad = join_tail(
         d_normed_one.reshape(by_slice),
         layer_input.reshape(by_slice),
         d_middle,
@@ -1470,7 +1521,6 @@
         own_grads,
         moved[:2],
         moved[2:],
-        by_x,
         10,
     )
     bias_grad = lax.dynamic_slice_in_dim(over_dp[24:30], 8 * dp, 8, 1).reshape(3, 2, 8)
@@ -1478,7 +1528,7 @@
 
     return (
         output.reshape(tok, width),
-        input_grad.reshape(tok, width).astype(f32),
+        input_grad.reshape(tok, width),
         qkv_grad.reshape(width // N_DP, 3, 2, head_dim),
         bias_grad,
         outproj_grad.T.reshape(2, head_dim, width // N_DP),

time: 460 us -> 453 us (0.985)
  Pallas kernels: 413 us -> 405 us
  local copies, waits for them, and re-layouts: 19.1 us -> 24.8 us
    pallas_call x1, Pallas kernels: 110 us -> 102 us  [attend_forward(): pl.pallas_call(kernel, out_shape=(struct((stream, size), bf16), struct((s...]
    unnamed x81 -> x80, local copies, waits for them, and re-layouts: 15.1 us -> 18.7 us
where the time goes in v6:
time: 453 us; the launch traced here: 452 us
  Pallas kernels  405 us (89%)
  local copies, waits for them, and re-layouts  24.8 us (5%)
  matrix products  11.2 us (2%)
  other arithmetic  9.94 us (2%)
    pallas_call x1, Pallas kernels, backward(): pl.pallas_call(kernel, out_shape=(struct((rows, width), f32), struct((8,...  121 us
    pallas_call x1, Pallas kernels, experts(): pl.pallas_call(kernel, out_shape=(row, row, struct((tok, width), f32), st...  107 us
    pallas_call x1, Pallas kernels, attend_forward(): pl.pallas_call(kernel, out_shape=(struct((stream, size), bf16), struct((s...  102 us
    pallas_call x1, Pallas kernels, join_tail(): pl.pallas_call(kernel, out_shape=(struct(part.shape, f32), struct((width...  75.3 us
    unnamed x80, local copies, waits for them, and re-layouts  18.7 us
    dot_general x5, matrix products, dot(): return jnp.einsum(pattern, a, b, preferred_element_type=f32)  11.2 us

profile of v6, /device:TPU:1, one launch (start us, length us, event | category | flops | bytes accessed | tf_op | source)
XLA Modules:
  0.0 452.4 jit_solution(13847835030046192002)
XLA Ops:
  0.6 0.0 copy-start
  0.7 0.0 copy-start.22
  0.7 0.9 reduce-window.8
  1.7 0.7 bitcast_subtract_fusion
  2.3 1.7 fusion.14
  4.0 0.1 convert_reduce_fusion.1
  4.1 0.1 select_reduce_fusion
  4.2 0.7 convert_element_type.79
  4.9 0.7 broadcast_in_dim.27.refs_12_
  5.6 1.3 reshape.231
  6.8 0.7 convert_reduce_fusion
  7.6 0.1 fusion.23
  7.8 0.0 copy-start.35
  7.8 0.6 multiply_cosine_fusion
  8.5 0.8 fusion.24.refs_7_
  9.3 0.4 fusion.16.refs_4_
  9.7 0.1 copy-done.35
  9.8 1.2 fusion.18
  11.1 0.0 copy-start.20
  11.1 0.0 copy-start.27
  11.1 0.3 subtract_convert_fusion
  11.4 0.2 maximum_bitcast_fusion
  11.6 0.6 copy-done.2
  12.3 0.2 copy-done.3
  12.5 102.5 %attend_forward.1 = (bf16[5120,128]{1,0:T(8,128)(2,1)S(1)}, bf16[5120,128]{1,0:T(8,128)(2,1)S(1)}, bf16[2,320,128]{2,1,0:T(8,128)(2,1)S(1)}, f32[640,128]{1,0:T(...) custom-call(bf16[2,320,128]{2,1,0:T(8,128)(2,1)S(1)} %get-tuple-elem, ...), custom_call_target="tpu_custom_call" | custom-call | bytes 255000000 | tf_op jit(solution)/shard_map/attend_forward/pallas_call | solution.py:632
  114.9 1.0 copy-done.4
  116.0 1.1 copy-done.5
  117.1 0.7 copy-done.9
  117.8 0.7 copy-done.11
  118.5 0.7 copy-done.13
  119.2 0.6 copy-done.16
  119.8 0.6 copy-done.24
  120.4 106.8 %experts.1 = (bf16[4,112,2048]{2,1,0:T(8,128)(2,1)}, bf16[4,112,2048]{2,1,0:T(8,128)(2,1)}, f32[320,2048]{1,0:T(8,128)}, f32[320,2048]{1,0:T(8,128)}, bf16[8,211...) custom-call(bf16[528,2048]{1,0:T(8,128)(2,1)} %get-tuple-element.55., ...), custom_call_target="tpu_custom_call" | custom-call | bytes 345000000 | tf_op jit(solution)/shard_map/experts/pallas_call | solution.py:887
  227.2 4.6 %fusion.10 = bf16[320,2048]{1,0:T(8,128)(2,1)} fusion(f32[320,2048]{1,0:T(8,128)} %get-tuple-element.59, bf16[4,112,2048]{2,1,0:T(8,128)(2,1)} %get-tuple-element.60, s32[4,320]{1,0:T(4,128)S(1)} %bitcast.131), kind=kOutput, calls=%fused_computation.12 | convolution fusion | flops 588656640 | bytes 5772288 | tf_op jit(solution)/shard_map/rt,rd->td/dot_general | solution.py:1386
  231.8 0.0 copy-start.25
  231.9 0.0 copy-start.28
  231.9 2.1 fusion.9
  234.0 120.7 %backward.1 = (f32[40,2048]{1,0:T(8,128)S(1)}, f32[8,2048]{1,0:T(8,128)S(1)}, f32[2,640,128]{2,1,0:T(8,128)S(1)}, bf16[2,320,128]{2,1,0:T(8,128)(2,1)S(1)}, f32[...) custom-call(bf16[8,40,2048]{2,1,0:T(8,128)(2,1)} %bitcast.121, ...), custom_call_target="tpu_custom_call" | custom-call | bytes 330000000 | tf_op jit(solution)/shard_map/backward/pallas_call | solution.py:1122
  354.7 0.8 copy-done.6
  355.6 0.7 copy-done.7
  356.3 0.6 copy-done.18
  356.9 0.8 copy.40
  357.7 1.0 slice_bitcast_fusion.2
  358.7 1.0 slice_bitcast_fusion.4
  359.8 0.8 fusion.43
  360.6 0.4 concatenate.13.refs_5_
  361.0 0.1 convert_element_type.96
  361.1 0.0 copy-start.1
  361.2 3.2 fusion.11
  364.5 75.3 %join_tail.1 = (f32[8,40,2048]{2,1,0:T(8,128)}, f32[128,768]{1,0:T(8,128)S(1)}, f32[32,128]{1,0:T(8,128)S(1)}, f32[32,128]{1,0:T(8,128)S(1)}, f32[352,2048]{1,0:T(8,128)}, /*index=5*/f32[176,2048]{1,0:T(8,128)}) custom-call(bf16[8,40,2048]{2,1,0:T(8,128)(2,1)S(1)} %bitcast.110, bf16[8,40,2048]{2,1,0:T(8,128)(2,1)S(1)} %bitcast.105, ...), custom_call_target="tpu_custom_call" | custom-call | bytes 165000000 | tf_op jit(solution)/shard_map/join_tail/pallas_call | solution.py:1317
  439.8 0.1 slice_reduce_fusion
  439.9 0.5 multiply_sqrt_fusion
  440.4 0.5 slice_bitcast_fusion.7
  441.0 0.6 slice_bitcast_fusion.6
  441.6 0.1 constant_dynamic-slice_fusion.1
  441.6 0.6 reshape.227
  442.2 0.9 reshape.226
  443.2 2.7 copy.62
  445.8 1.5 copy.63
  447.3 0.9 copy.64
  448.2 0.7 copy.65
  448.9 1.6 copy.66
  450.5 0.8 copy-done.34
  451.3 1.1 copy.67
  (63 shorter events, 0.3 us)
Async XLA Ops:
  0.6 8.6 %copy-start = (bf16[320,2048]{1,0:T(8,128)(2,1)S(1)}, bf16[320,2048]{1,0:T(8,128)(2,1)}, u32[]{:S(2)}) copy-start(bf16[320,2048]{1,0:T(8,128)(2,1)} %param.15) | copy-start | bytes 3932164
  0.7 8.6 %copy-start.22 = (f32[2048]{0:T(1024)S(1)}, f32[2048]{0:T(1024)}, u32[]{:S(2)}) copy-start(f32[2048]{0:T(1024)} %param.18) | copy-start | bytes 24580
  7.8 2.0 copy-start.35
  9.8 1.2 copy-start.29
  11.0 1.2 copy-start.2
  11.0 1.4 copy-start.3
  11.1 1.4 copy-start.20
  11.1 1.4 copy-start.27
  114.9 1.1 copy-start.4
  116.0 1.1 copy-start.5
  117.1 0.7 copy-start.9
  117.8 0.7 copy-start.11
  118.5 0.7 copy-start.13
  119.2 0.6 copy-start.16
  119.8 0.6 copy-start.24
  227.2 4.6 %copy-start.32 = (f32[320,2048]{1,0:T(8,128)S(1)}, f32[320,2048]{1,0:T(8,128)}, u32[]{:S(2)}) copy-start(f32[320,2048]{1,0:T(8,128)} %get-tuple-element.61) | copy-start | bytes 7864324
  227.2 4.6 %copy-start.33 = (bf16[4,112,2048]{2,1,0:T(8,128)(2,1)S(1)}, bf16[4,112,2048]{2,1,0:T(8,128)(2,1)}, u32[]{:S(2)}) copy-start(bf16[4,112,2048]{2,1,0:T(8,128)(2,1)} %get-tuple-element.62) | copy-start | bytes 5505028
  231.8 2.2 copy-start.10
  231.8 2.2 copy-start.12
  231.8 2.2 copy-start.14
  231.8 2.2 copy-start.21
  231.8 2.2 copy-start.25
  231.9 2.2 copy-start.28
  354.7 0.8 copy-start.6
  355.6 0.7 copy-start.7
  356.3 0.6 copy-start.18
  361.1 3.3 copy-start.1
  361.1 3.3 copy-start.8
  361.1 3.3 copy-start.15
  361.1 3.3 copy-start.17
  361.1 3.3 copy-start.19
  361.2 3.3 copy-start.23
  361.2 3.3 copy-start.26
  443.2 2.7 copy-start.31
  445.8 3.1 copy-start.30
  448.9 2.4 copy-start.34

commit v7 on v6

--- a/solution.py
+++ b/solution.py
@@ -672,7 +672,7 @@
 
 
 TILE = 176
-NOW = 96
+NOW = 208
 
 
 def shared_expert(x_ref, up_ref, w_ref, vec_ref, part_ref, d_ref, grads_ref, row_ref, low_ref):

time: 453 us -> 446 us (0.985)
  Pallas kernels: 405 us -> 396 us
    pallas_call x1, Pallas kernels: 75.3 us -> 65.7 us  [join_tail(): pl.pallas_call(kernel, out_shape=(struct(part.shape, f32), struct((width...]
    unnamed x80 -> x92, local copies, waits for them, and re-layouts: 18.7 us -> 19.7 us
where the time goes in v7:
time: 446 us; the launch traced here: 445 us
  Pallas kernels  396 us (89%)
  local copies, waits for them, and re-layouts  26.5 us (6%)
  matrix products  11.4 us (3%)
  other arithmetic  10.7 us (2%)
    pallas_call x1, Pallas kernels, backward(): pl.pallas_call(kernel, out_shape=(struct((rows, width), f32), struct((8,...  120 us
    pallas_call x1, Pallas kernels, experts(): pl.pallas_call(kernel, out_shape=(row, row, struct((tok, width), f32), st...  107 us
    pallas_call x1, Pallas kernels, attend_forward(): pl.pallas_call(kernel, out_shape=(struct((stream, size), bf16), struct((s...  102 us
    pallas_call x1, Pallas kernels, join_tail(): pl.pallas_call(kernel, out_shape=(struct(part.shape, f32), struct((width...  65.7 us
    unnamed x92, local copies, waits for them, and re-layouts  19.7 us
    dot_general x5, matrix products, dot(): return jnp.einsum(pattern, a, b, preferred_element_type=f32)  11.4 us

profile of v7, /device:TPU:1, one launch (start us, length us, event | category | flops | bytes accessed | tf_op | source)
XLA Modules:
  0.0 445.5 jit_solution(16302044807393614010)
XLA Ops:
  0.6 0.0 copy-start
  0.7 0.0 copy-start.26
  0.7 0.9 reduce-window.8
  1.7 0.7 bitcast_subtract_fusion
  2.3 1.7 fusion.14
  4.0 0.1 convert_reduce_fusion.1
  4.1 0.1 select_reduce_fusion
  4.2 0.7 convert_element_type.79
  4.9 0.7 broadcast_in_dim.27.refs_12_
  5.6 1.3 reshape.231
  6.9 0.7 convert_reduce_fusion
  7.6 0.1 fusion.23
  7.8 0.0 copy-start.41
  7.8 0.6 multiply_cosine_fusion
  8.5 0.8 fusion.24.refs_7_
  9.3 0.4 fusion.16.refs_4_
  9.7 0.1 copy-done.41
  9.8 1.2 fusion.18
  11.1 0.0 copy-start.24
  11.1 0.0 copy-start.31
  11.2 0.3 subtract_convert_fusion
  11.5 0.2 maximum_bitcast_fusion
  11.7 0.6 copy-done.2
  12.3 0.2 copy-done.3
  12.5 102.5 %attend_forward.1 = (bf16[5120,128]{1,0:T(8,128)(2,1)S(1)}, bf16[5120,128]{1,0:T(8,128)(2,1)S(1)}, bf16[2,320,128]{2,1,0:T(8,128)(2,1)S(1)}, f32[640,128]{1,0:T(...) custom-call(bf16[2,320,128]{2,1,0:T(8,128)(2,1)S(1)} %get-tuple-elem, ...), custom_call_target="tpu_custom_call" | custom-call | bytes 255000000 | tf_op jit(solution)/shard_map/attend_forward/pallas_call | solution.py:632
  115.0 1.0 copy-done.4
  116.0 1.1 copy-done.5
  117.1 0.7 copy-done.11
  117.8 0.7 copy-done.13
  118.5 0.7 copy-done.15
  119.2 0.7 copy-done.17
  119.9 0.6 copy-done.20
  120.5 0.6 copy-done.28
  121.1 107.1 %experts.1 = (bf16[4,112,2048]{2,1,0:T(8,128)(2,1)}, bf16[4,112,2048]{2,1,0:T(8,128)(2,1)}, f32[320,2048]{1,0:T(8,128)}, f32[320,2048]{1,0:T(8,128)}, bf16[8,211...) custom-call(bf16[528,2048]{1,0:T(8,128)(2,1)} %get-tuple-element.55., ...), custom_call_target="tpu_custom_call" | custom-call | bytes 345000000 | tf_op jit(solution)/shard_map/experts/pallas_call | solution.py:887
  228.2 4.6 %fusion.10 = bf16[320,2048]{1,0:T(8,128)(2,1)} fusion(f32[320,2048]{1,0:T(8,128)} %get-tuple-element.59, bf16[4,112,2048]{2,1,0:T(8,128)(2,1)} %get-tuple-element.60, s32[4,320]{1,0:T(4,128)S(1)} %bitcast.131), kind=kOutput, calls=%fused_computation.12 | convolution fusion | flops 588656640 | bytes 5772288 | tf_op jit(solution)/shard_map/rt,rd->td/dot_general | solution.py:1386
  232.9 2.1 fusion.9
  235.0 120.4 %backward.1 = (f32[40,2048]{1,0:T(8,128)S(1)}, f32[8,2048]{1,0:T(8,128)S(1)}, f32[2,640,128]{2,1,0:T(8,128)S(1)}, bf16[2,320,128]{2,1,0:T(8,128)(2,1)S(1)}, f32[...) custom-call(bf16[8,40,2048]{2,1,0:T(8,128)(2,1)} %bitcast.121, ...), custom_call_target="tpu_custom_call" | custom-call | bytes 330000000 | tf_op jit(solution)/shard_map/backward/pallas_call | solution.py:1122
  355.5 0.8 copy-done.6
  356.3 0.8 copy-done.8
  357.2 0.7 copy-done.9
  357.9 0.8 copy.40
  358.7 1.0 slice_bitcast_fusion.2
  359.7 1.0 slice_bitcast_fusion.4
  360.7 1.5 fusion.43
  362.3 0.4 concatenate.13.refs_5_
  362.7 0.9 convert_element_type.96
  363.6 3.4 fusion.11
  367.1 65.7 %join_tail.1 = (f32[8,40,2048]{2,1,0:T(8,128)}, f32[128,768]{1,0:T(8,128)S(1)}, f32[32,128]{1,0:T(8,128)S(1)}, f32[32,128]{1,0:T(8,128)S(1)}, f32[352,2048]{1,0:T(8,128)}, /*index=5*/f32[176,2048]{1,0:T(8,128)}) custom-call(bf16[8,40,2048]{2,1,0:T(8,128)(2,1)S(1)} %bitcast.110, bf16[8,40,2048]{2,1,0:T(8,128)(2,1)S(1)} %bitcast.105, ...), custom_call_target="tpu_custom_call" | custom-call | bytes 165000000 | tf_op jit(solution)/shard_map/join_tail/pallas_call | solution.py:1317
  432.7 0.1 slice_reduce_fusion
  432.8 0.5 multiply_sqrt_fusion
  433.4 0.5 slice_bitcast_fusion.7
  433.9 0.6 slice_bitcast_fusion.6
  434.5 0.1 constant_dynamic-slice_fusion.1
  434.6 0.6 reshape.227
  435.1 0.9 reshape.226
  436.1 2.5 copy.62
  438.6 1.5 copy.63
  440.1 0.1 copy-done.7
  440.2 0.9 copy.64
  441.0 0.7 copy.65
  441.8 0.2 copy-done.34
  442.0 1.6 copy.66
  443.5 0.8 copy-done.38
  444.4 1.1 copy.67
  (75 shorter events, 0.3 us)
Async XLA Ops:
  0.6 8.7 %copy-start = (bf16[320,2048]{1,0:T(8,128)(2,1)S(1)}, bf16[320,2048]{1,0:T(8,128)(2,1)}, u32[]{:S(2)}) copy-start(bf16[320,2048]{1,0:T(8,128)(2,1)} %param.15) | copy-start | bytes 3932164
  0.7 8.7 %copy-start.26 = (f32[2048]{0:T(1024)S(1)}, f32[2048]{0:T(1024)}, u32[]{:S(2)}) copy-start(f32[2048]{0:T(1024)} %param.18) | copy-start | bytes 24580
  1.7 8.0 %copy-start.40 = (f32[64]{0:T(128)}, f32[64]{0:T(128)S(1)}, u32[]{:S(2)}) copy-start(f32[64]{0:T(128)S(1)} %multiply_exponential_fusion) | copy-start | bytes 772
  4.2 6.8 %copy-start.39 = (f32[320]{0:T(512)}, f32[320]{0:T(512)S(1)}, u32[]{:S(2)}) copy-start(f32[320]{0:T(512)S(1)} %subtract_convert_fusion.2) | copy-start | bytes 3844
  7.8 2.0 copy-start.41
  9.8 1.2 copy-start.33
  11.1 1.2 copy-start.2
  11.1 1.4 copy-start.3
  11.1 1.4 copy-start.24
  11.1 1.4 copy-start.31
  115.0 1.1 copy-start.4
  116.0 1.1 copy-start.5
  117.1 0.7 copy-start.11
  117.8 0.7 copy-start.13
  118.5 0.7 copy-start.15
  119.2 0.7 copy-start.17
  119.9 0.6 copy-start.20
  120.5 0.6 copy-start.28
  228.2 4.6 %copy-start.36 = (f32[320,2048]{1,0:T(8,128)S(1)}, f32[320,2048]{1,0:T(8,128)}, u32[]{:S(2)}) copy-start(f32[320,2048]{1,0:T(8,128)} %get-tuple-element.61) | copy-start | bytes 7864324
  228.2 4.6 %copy-start.37 = (bf16[4,112,2048]{2,1,0:T(8,128)(2,1)S(1)}, bf16[4,112,2048]{2,1,0:T(8,128)(2,1)}, u32[]{:S(2)}) copy-start(bf16[4,112,2048]{2,1,0:T(8,128)(2,1)} %get-tuple-element.62) | copy-start | bytes 5505028
  232.8 2.2 copy-start.12
  232.8 2.2 copy-start.14
  232.8 2.2 copy-start.16
  232.8 2.2 copy-start.18
  232.8 2.2 copy-start.25
  232.8 2.2 copy-start.29
  232.9 2.2 copy-start.32
  355.5 0.9 copy-start.6
  356.3 0.8 copy-start.8
  357.2 0.7 copy-start.9
  357.9 4.4 copy-start.22
  363.6 3.4 copy-start.1
  363.6 3.4 copy-start.19
  363.6 3.4 copy-start.21
  363.6 3.4 copy-start.23
  363.6 3.4 copy-start.27
  363.6 3.4 copy-start.30
  434.5 4.1 copy-start.35
  438.6 1.6 copy-start.7
  438.6 2.4 copy-start.10
  438.6 3.4 copy-start.34
  442.0 2.4 copy-start.38
